TPU v7x, 32 devices: a whole 2x2x4 slice. The times are simulated.
32 devices in a mesh: shard: 8 (over z, x), rep: 4 (over y, core).
Axes of the slice: x: 2, y: 2, z: 4, core: 2. Of those that a mesh axis runs over, the one named last changes fastest.
Arguments:
- tokens: bfloat16 [4, 4096, 1024], P('rep', 'shard'), may hold values from -15 to 15
- cotangent: bfloat16 [4, 4096, 1024], P('rep', 'shard'), may hold values from -6 to 6
- in_weight: bfloat16 [1024, 3072], P('shard'), may hold values from -0.1875 to 0.1875
- out_weight: bfloat16 [1024, 1024], P('shard'), may hold values from -0.1875 to 0.1875
- gate_weight: bfloat16 [1024, 4608], P('shard'), may hold values from -0.1875 to 0.1875
- up_weight: bfloat16 [1024, 4608], P('shard'), may hold values from -0.1875 to 0.1875
- down_weight: bfloat16 [4608, 1024], P('shard'), may hold values from -0.09375 to 0.09375
- mix_gain: bfloat16 [1024], P('shard'), may hold values from 0.5 to 1.5
- ffn_gain: bfloat16 [1024], P('shard'), may hold values from 0.5 to 1.5
- conv_taps: bfloat16 [3, 1024], P(None, 'shard'), may hold values from -3 to 3
Outputs:
- output: bfloat16 [4, 4096, 1024], P('rep', 'shard')
- grad_tokens: bfloat16 [4, 4096, 1024], P('rep', 'shard')
- grad_in: float32 [1024, 3072], P('shard')
- grad_out: float32 [1024, 1024], P('shard')
- grad_gate: float32 [1024, 4608], P('shard')
- grad_up: float32 [1024, 4608], P('shard')
- grad_down: float32 [4608, 1024], P('shard')
- grad_mix_gain: float32 [1024], P('shard')
- grad_ffn_gain: float32 [1024], P('shard')
- grad_taps: float32 [3, 1024], P(None, 'shard')
All inputs are finite; a program needn't handle non-finite values.
Results may differ from a plain program's by a relative error of at most 0.0097.
Values may be sent and summed in bfloat16 or wider, within the bound.
No kernel may reach another device: no remote copies, remote signals or barrier semaphores. Data moves between devices by JAX's collectives and lax.ppermute only.
A program may use at most 192 MiB of HBM per device.

v0:
```python
import jax
import jax.numpy as jnp
from jax import lax
from jax.sharding import PartitionSpec as P

epsilon = 1e-05


def passed_along(value, axis, steps):
    count = lax.axis_size(axis)
    initial, last = (max(0, -steps), min(count, count - steps))
    return lax.ppermute(value, axis, [(source, source + steps) for source in range(initial, last)])


def outer_sum(left, right):
    return lax.dot_general(
        left, right, (((0,), (0,)), ((), ())), preferred_element_type=jnp.float32
    )


def times_transposed(grad, weight):
    return lax.dot_general(
        grad, weight, (((1,), (1,)), ((), ())), preferred_element_type=jnp.float32
    )


def local(
    tokens,
    cotangent,
    in_weight,
    out_weight,
    gate_weight,
    up_weight,
    down_weight,
    mix_gain,
    ffn_gain,
    conv_taps,
):
    small = jnp.concatenate([mix_gain[None], ffn_gain[None], conv_taps], 0)
    in_full, out_full, small_full = (
        lax.all_gather(in_weight, "shard", axis=0, tiled=True),
        lax.all_gather(out_weight, "shard", axis=0, tiled=True),
        lax.all_gather(small, "shard", axis=1, tiled=True),
    )
    gate_full, up_full, down_full = (
        lax.all_gather(gate_weight, "shard", axis=0, tiled=True),
        lax.all_gather(up_weight, "shard", axis=0, tiled=True),
        lax.all_gather(down_weight, "shard", axis=0, tiled=True),
    )
    params = small_full.astype(jnp.float32)
    gain_one = params[0]
    gain_two = params[1]
    taps = params[2:5]
    width = tokens.shape[-1]
    length = tokens.shape[1]
    inputs = tokens[0].astype(jnp.float32)
    factor_one = lax.rsqrt(jnp.mean(inputs * inputs, axis=-1, keepdims=True) + epsilon)
    unit_one = inputs * factor_one
    normed = (unit_one * gain_one).astype(jnp.bfloat16)
    mixed = jnp.dot(normed, in_full, preferred_element_type=jnp.float32)
    b_part = mixed[:, :width]
    c_part = mixed[:, width : 2 * width]
    x_part = mixed[:, 2 * width :]
    product = (b_part * x_part).astype(jnp.bfloat16)
    previous = passed_along(product[length - 2 :], "shard", 1)
    padded = jnp.concatenate([previous, product], 0).astype(jnp.float32)
    conv = taps[0] * padded[:length] + taps[1] * padded[1 : length + 1] + taps[2] * padded[2:]
    gated = (c_part * conv).astype(jnp.bfloat16)
    resid = inputs + jnp.dot(gated, out_full, preferred_element_type=jnp.float32)
    factor_two = lax.rsqrt(jnp.mean(resid * resid, axis=-1, keepdims=True) + epsilon)
    unit_two = resid * factor_two
    hnorm = (unit_two * gain_two).astype(jnp.bfloat16)
    gate = jnp.dot(hnorm, gate_full, preferred_element_type=jnp.float32)
    upper = jnp.dot(hnorm, up_full, preferred_element_type=jnp.float32)
    sigma = jax.nn.sigmoid(gate)
    activated = gate * sigma
    hidden = (activated * upper).astype(jnp.bfloat16)
    result = resid + jnp.dot(hidden, down_full, preferred_element_type=jnp.float32)
    output = result.astype(jnp.bfloat16)
    gate_back, up_back, down_back = (
        lax.all_gather(gate_weight, "shard", axis=0, tiled=True),
        lax.all_gather(up_weight, "shard", axis=0, tiled=True),
        lax.all_gather(down_weight, "shard", axis=0, tiled=True),
    )
    grad_out_rows = cotangent[0]
    d_hidden = times_transposed(grad_out_rows, down_back)
    g_down = outer_sum(hidden, grad_out_rows)
    d_gate = (d_hidden * upper * sigma * (1.0 + gate * (1.0 - sigma))).astype(jnp.bfloat16)
    d_up = (d_hidden * activated).astype(jnp.bfloat16)
    g_gate = outer_sum(hnorm, d_gate)
    g_up = outer_sum(hnorm, d_up)
    d_hnorm = times_transposed(d_gate, gate_back) + times_transposed(d_up, up_back)
    g_ffn_gain = jnp.sum(d_hnorm * unit_two, axis=0)
    scaled_two = d_hnorm * gain_two
    d_resid = grad_out_rows.astype(jnp.float32) + factor_two * (
        scaled_two - unit_two * jnp.mean(scaled_two * unit_two, axis=-1, keepdims=True)
    )
    ffn_shares = (
        lax.psum_scatter(g_gate, "shard", scatter_dimension=0, tiled=True),
        lax.psum_scatter(g_up, "shard", scatter_dimension=0, tiled=True),
        lax.psum_scatter(g_down, "shard", scatter_dimension=0, tiled=True),
    )
    ffn_shares = lax.psum((ffn_shares[0], ffn_shares[1], ffn_shares[2]), "rep")
    in_back, out_back = (
        lax.all_gather(in_weight, "shard", axis=0, tiled=True),
        lax.all_gather(out_weight, "shard", axis=0, tiled=True),
    )
    d_branch = d_resid.astype(jnp.bfloat16)
    d_gated = times_transposed(d_branch, out_back)
    g_out = outer_sum(gated, d_branch)
    d_cpart = d_gated * conv
    d_conv = d_gated * c_part
    tap_grads = [jnp.sum(d_conv * padded[k : k + length], axis=0) for k in range(3)]
    spread = (
        jnp.pad(taps[0] * d_conv, ((0, 2), (0, 0)))
        + jnp.pad(taps[1] * d_conv, ((1, 1), (0, 0)))
        + jnp.pad(taps[2] * d_conv, ((2, 0), (0, 0)))
    )
    returned = passed_along(spread[:2], "shard", -1)
    d_product = spread[2:].at[length - 2 :].add(returned)
    d_mixed = jnp.concatenate([d_product * x_part, d_cpart, d_product * b_part], -1).astype(
        jnp.bfloat16
    )
    d_normed = times_transposed(d_mixed, in_back)
    g_in = outer_sum(normed, d_mixed)
    g_mix_gain = jnp.sum(d_normed * unit_one, axis=0)
    scaled_one = d_normed * gain_one
    d_inputs = d_resid + factor_one * (
        scaled_one - unit_one * jnp.mean(scaled_one * unit_one, axis=-1, keepdims=True)
    )
    small_grads = jnp.stack([g_mix_gain, g_ffn_gain] + tap_grads, 0)
    mix_shares = (
        lax.psum_scatter(g_in, "shard", scatter_dimension=0, tiled=True),
        lax.psum_scatter(g_out, "shard", scatter_dimension=0, tiled=True),
        lax.psum_scatter(small_grads, "shard", scatter_dimension=1, tiled=True),
    )
    mix_shares = lax.psum((mix_shares[0], mix_shares[1], mix_shares[2]), "rep")
    small_owned = mix_shares[2]
    return (
        output[None],
        d_inputs.astype(jnp.bfloat16)[None],
        mix_shares[0],
        mix_shares[1],
        ffn_shares[0],
        ffn_shares[1],
        ffn_shares[2],
        small_owned[0],
        small_owned[1],
        small_owned[2:5],
    )


def solution(mesh):
    in_specs = (
        P("rep", "shard", None),
        P("rep", "shard", None),
        P("shard", None),
        P("shard", None),
        P("shard", None),
        P("shard", None),
        P("shard", None),
        P("shard"),
        P("shard"),
        P(None, "shard"),
    )
    out_specs = (
        P("rep", "shard", None),
        P("rep", "shard", None),
        P("shard", None),
        P("shard", None),
        P("shard", None),
        P("shard", None),
        P("shard", None),
        P("shard"),
        P("shard"),
        P(None, "shard"),
    )
    return jax.shard_map(local, mesh=mesh, in_specs=in_specs, out_specs=out_specs, check_vma=False)
```

profile of v0, /device:TPU:0, one launch (start us, length us, event | category | flops | bytes accessed | tf_op | source)
XLA Modules:
  0.0 2109.1 jit_solution(9752614554453717210)
XLA Ops:
  10.7 28.2 %all_gather.23 = bf16[5,1024]{1,0:T(8,128)(2,1)S(1)} all-gather(bf16[5,128]{1,0:T(8,128)(2,1)S(1)} %pad_maximum_fusion.3), channel_id=1, replica_groups=mesh['shard'=8,'rep'=4] {'shard'}, dimensions={1}, use_global_device_ids=true | all-gather | bytes 11520 | tf_op jit(solution)/shard_map/all_gather | solution.py:43
  39.2 73.0 %all-gather.6.cloned.1.call-done = bf16[1024,3072]{1,0:T(8,128)(2,1)} async-done(((bf16[128,3072]{1,0:T(8,128)(2,1)}), bf16[1024,3072]{1,0:T(8,128)(2,1)}) %all-gather.6.cloned.1.call-update) | async-done | bytes 6291472 | tf_op jit(solution)/shard_map/all_gather | solution.py:41
  112.1 5.7 fusion.26
  118.2 2.5 collective-permute-start
  120.6 1.3 collective-permute-done
  122.3 2.4 multiply_convert_fusion.7
  124.7 37.1 %all-gather.8.cloned.1.call-done = bf16[1024,1024]{1,0:T(8,128)(2,1)} async-done(((bf16[128,1024]{1,0:T(8,128)(2,1)}), bf16[1024,1024]{1,0:T(8,128)(2,1)}) %all-gather.8.cloned.1.call-update) | async-done | bytes 2097168 | tf_op jit(solution)/shard_map/all_gather | solution.py:42
  161.8 3.3 multiply_reduce_fusion.5
  165.0 1.3 copy-done.6
  166.6 133.9 %all-gather.12.cloned.1.call-done = bf16[1024,4608]{1,0:T(8,128)(2,1)} async-done(((bf16[128,4608]{1,0:T(8,128)(2,1)}), bf16[1024,4608]{1,0:T(8,128)(2,1)}) %all-gather.12.cloned.1.call-update) | async-done | bytes 9437200 | tf_op jit(solution)/shard_map/all_gather | solution.py:47
  300.5 11.3 fusion.33
  311.8 127.0 %all-gather.10.cloned.1.call-done = bf16[1024,4608]{1,0:T(8,128)(2,1)} async-done(((bf16[128,4608]{1,0:T(8,128)(2,1)}), bf16[1024,4608]{1,0:T(8,128)(2,1)}) %all-gather.10.cloned.1.call-update) | async-done | bytes 9437200 | tf_op jit(solution)/shard_map/all_gather | solution.py:46
  438.8 11.1 fusion.32
  449.9 127.3 %all-gather.14.cloned.1.call-done = bf16[4608,1024]{1,0:T(8,128)(2,1)} async-done(((bf16[576,1024]{1,0:T(8,128)(2,1)}), bf16[4608,1024]{1,0:T(8,128)(2,1)}) %all-gather.14.cloned.1.call-update) | async-done | bytes 9437200 | tf_op jit(solution)/shard_map/all_gather | solution.py:48
  577.2 18.0 multiply_convert_fusion
  595.2 9.2 fusion.34
  604.4 8.3 multiply_reduce_fusion.3
  613.3 1.3 copy-done.1
  614.6 3.4 fusion.21
  618.1 3.7 fusion.23
  621.8 2.7 multiply_reduce_fusion
  624.5 1.0 broadcast_multiply_fusion.2
  625.5 1.3 collective-permute-start.1
  628.2 3.0 collective-permute-done.1
  633.1 6.8 fusion.14
  639.9 1.2 copy-done.21
  641.2 11.7 fusion.17
  652.9 11.8 fusion.36
  664.8 11.5 fusion.35
  676.3 1.2 copy-done.12
  677.8 8.1 fusion.11
  686.6 17.8 reduce-scatter.9.cloned.1.call-done
  704.4 211.1 %reduce-scatter.7.cloned.1.call-done = f32[128,3072]{1,0:T(8,128)} async-done(((f32[1024,3072]{1,0:T(8,128)}), f32[128,3072]{1,0:T(8,128)}) %reduce-scatter.7.cloned.1.call-update) | async-done | bytes 1572880 | tf_op jit(solution)/shard_map/reduce_scatter | solution.py:133
  915.5 316.8 %reduce-scatter.15.cloned.1.call-done = f32[576,1024]{1,0:T(8,128)} async-done(((f32[4608,1024]{1,0:T(8,128)}), f32[576,1024]{1,0:T(8,128)}) %reduce-scatter.15.cloned.1.call-update) | async-done | bytes 2359312 | tf_op jit(solution)/shard_map/reduce_scatter | solution.py:101
  1232.3 316.8 %reduce-scatter.13.cloned.1.call-done = f32[128,4608]{1,0:T(8,128)} async-done(((f32[1024,4608]{1,0:T(8,128)}), f32[128,4608]{1,0:T(8,128)}) %reduce-scatter.13.cloned.1.call-update) | async-done | bytes 2359312 | tf_op jit(solution)/shard_map/reduce_scatter | solution.py:100
  1549.1 316.7 %reduce-scatter.11.cloned.1.call-done = f32[128,4608]{1,0:T(8,128)} async-done(((f32[1024,4608]{1,0:T(8,128)}), f32[128,4608]{1,0:T(8,128)}) %reduce-scatter.11.cloned.1.call-update) | async-done | bytes 2359312 | tf_op jit(solution)/shard_map/reduce_scatter | solution.py:99
  1865.8 1.6 copy-done.8
  1867.4 9.9 fusion.13
  1877.3 1.6 fusion.16
  1878.9 43.6 %reduce-scatter.17.cloned.1.call-done = f32[5,128]{1,0:T(8,128)} async-done(((f32[5,1024]{1,0:T(8,128)}), f32[5,128]{1,0:T(8,128)}) %reduce-scatter.17.cloned.1.call-update) | async-done | bytes 2576 | tf_op jit(solution)/shard_map/reduce_scatter | solution.py:135
  1922.5 5.8 psum.47
  1929.3 162.4 %all-reduce.6.cloned.1.call-done = (f32[128,3072]{1,0:T(8,128)}, f32[128,1024]{1,0:T(8,128)}, f32[128,4608]{1,0:T(8,128)}, f32[128,4608]{1,0:T(8,128)}, f32[576,1024]{1,0:T(8,128)}) async-done(((f32[128,3072]{1,0:T(8,128)}, f32[128,1024]{1,0:T(8,128)}, f32[128,4608]{1,0:T(8,128)}, f32[128,4608]{1,0:T(8,128)}, f32[576,1024]{1,0:T(8,128)}), (f32[128,3072]{1,0:T(8,128)}, f32[128,1024]{1,0:T(8,128)}, ...) | async-done | bytes 9175056 | tf_op jit(solution)/shard_map/psum | solution.py:137
  2091.7 2.9 copy.26
  2095.3 1.4 copy.28
  2096.7 1.1 copy-done.17
  2097.9 1.4 copy.29
  2099.3 1.1 copy-done.16
  2100.4 1.4 copy.30
  (95 shorter events, 11.6 us)
Async XLA Ops:
  7.2 104.9 %all-gather.6.cloned.1.call-start = ((), (), s32[]{:S(2)}) async-start(), calls=%async_computation.6 | async-start | bytes 7077888 | tf_op jit(solution)/shard_map/all_gather | solution.py:41
  7.9 2.7 copy-start.23
  7.9 2.7 copy-start.24
  7.9 2.7 copy-start.25
  7.9 30.9 %copy-start.3 = (bf16[1,512,1024]{2,1,0:T(8,128)(2,1)S(1)}, bf16[1,512,1024]{2,1,0:T(8,128)(2,1)}, u32[]{:S(2)}) copy-start(bf16[1,512,1024]{2,1,0:T(8,128)(2,1)} %param.12) | copy-start | bytes 3145732
  8.0 153.8 %all-gather.8.cloned.1.call-start = ((), (), s32[]{:S(2)}) async-start(), calls=%async_computation.7 | async-start | bytes 2359296 | tf_op jit(solution)/shard_map/all_gather | solution.py:42
  8.7 291.8 %all-gather.12.cloned.1.call-start = ((), (), s32[]{:S(2)}) async-start(), calls=%async_computation.9 | async-start | bytes 10616832 | tf_op jit(solution)/shard_map/all_gather | solution.py:47
  9.4 429.4 %all-gather.10.cloned.1.call-start = ((), (), s32[]{:S(2)}) async-start(), calls=%async_computation.8 | async-start | bytes 10616832 | tf_op jit(solution)/shard_map/all_gather | solution.py:46
  10.0 567.2 %all-gather.14.cloned.1.call-start = ((), (), s32[]{:S(2)}) async-start(), calls=%async_computation.10 | async-start | bytes 10616832 | tf_op jit(solution)/shard_map/all_gather | solution.py:48
  10.6 693.8 %reduce-scatter.9.cloned.1.call-start = ((), (), s32[]{:S(2)}) async-start(), calls=%async_computation.12 | async-start | bytes 4718592 | tf_op jit(solution)/shard_map/reduce_scatter | solution.py:134
  117.8 4.4 copy-start
  118.2 3.8 collective-permute-start
  165.0 1.3 copy-start.6
  595.2 9.2 copy-start.7
  595.2 9.2 copy-start.10
  604.4 8.3 copy-start.20
  612.7 1.9 copy-start.9
  613.3 1.3 copy-start.1
  618.1 297.5 %reduce-scatter.7.cloned.1.call-start = ((), (), s32[]{:S(2)}) async-start(), calls=%async_computation.11 | async-start | bytes 14155776 | tf_op jit(solution)/shard_map/reduce_scatter | solution.py:133
  618.1 3.7 copy-start.5
  624.5 7.6 copy-start.11
  625.5 5.7 collective-permute-start.1
  626.8 4.4 slice-start
  627.8 3.4 slice-start.1
  631.2 1.9 copy-start.4
  632.1 1.0 copy-start.15
  632.1 7.8 copy-start.13
  639.9 1.3 copy-start.21
  639.9 592.4 %reduce-scatter.15.cloned.1.call-start = ((), (), s32[]{:S(2)}) async-start(), calls=%async_computation.15 | async-start | bytes 21233664 | tf_op jit(solution)/shard_map/reduce_scatter | solution.py:101
  652.9 896.2 %reduce-scatter.13.cloned.1.call-start = ((), (), s32[]{:S(2)}) async-start(), calls=%async_computation.14 | async-start | bytes 21233664 | tf_op jit(solution)/shard_map/reduce_scatter | solution.py:100
  664.7 1201.0 %reduce-scatter.11.cloned.1.call-start = ((), (), s32[]{:S(2)}) async-start(), calls=%async_computation.13 | async-start | bytes 21233664 | tf_op jit(solution)/shard_map/reduce_scatter | solution.py:99
  676.2 1.2 copy-start.12
  676.2 1.6 copy-start.14
  676.3 1246.2 %reduce-scatter.17.cloned.1.call-start = ((), (), s32[]{:S(2)}) async-start(), calls=%async_computation.16 | async-start | bytes 36864 | tf_op jit(solution)/shard_map/reduce_scatter | solution.py:135
  686.6 1405.1 %all-reduce.6.cloned.1.call-start = ((), (), s32[]{:S(2)}) async-start(), calls=%async_computation.17 | async-start | bytes 18350080 | tf_op jit(solution)/shard_map/psum | solution.py:137
  1865.8 1.6 copy-start.8
  1867.4 9.9 copy-start.2
  1867.4 9.9 copy-start.19
  2091.7 2.9 copy-start.22
  2091.7 3.7 copy-start.18
  2095.3 2.5 copy-start.17
  2097.9 2.5 copy-start.16
Sparse Core Ops, SparseCore 0:
  10.2 101.8 all-gather.5
  114.2 47.4 all-gather.7
  163.9 136.5 all-gather.11
  302.6 136.2 all-gather.9
  440.9 136.2 all-gather.13
  618.2 86.2 reduce-scatter.8
  708.5 207.0 reduce-scatter.6
  919.9 312.3 reduce-scatter.14
  1236.6 312.4 reduce-scatter.12
  1553.3 312.3 reduce-scatter.10
  1869.8 52.6 reduce-scatter.16
  1925.6 166.0 all-reduce.5
where the time goes:
time: 2110 us
  waiting for transfers between devices  1890 us (90%)
  matrix products  134 us (6%)
  blocking collectives  33.9 us (2%)
    reduce_scatter x1, waiting for transfers between devices, local(): lax.psum_scatter(g_up, 'shard', scatter_dimension=0, tiled=True)  317 us
    reduce_scatter x1, waiting for transfers between devices, local(): lax.psum_scatter(g_down, 'shard', scatter_dimension=0, tiled=True)  317 us
    reduce_scatter x1, waiting for transfers between devices, local(): lax.psum_scatter(g_gate, 'shard', scatter_dimension=0, tiled=True)  317 us
    reduce_scatter x1, waiting for transfers between devices, local(): lax.psum_scatter(g_in, 'shard', scatter_dimension=0, tiled=True)  211 us
    psum x1, waiting for transfers between devices, local(): mix_shares = lax.psum((mix_shares[0], mix_shares[1], mix_shares[2]), 'rep')  162 us
    all_gather x1, waiting for transfers between devices, local(): lax.all_gather(up_weight, 'shard', axis=0, tiled=True)  134 us
    all_gather x1, waiting for transfers between devices, local(): lax.all_gather(down_weight, 'shard', axis=0, tiled=True)  127 us
    all_gather x1, waiting for transfers between devices, local(): lax.all_gather(gate_weight, 'shard', axis=0, tiled=True)  127 us
  transfers between devices with their start and end apart: 14, of which 14 were waited for; matrix products, arithmetic and copies ran while one was open for 5% of the time, Pallas kernels for 0%

commit v1 on v0

v1 whole, which is shorter than its diff:
```python
import jax
import jax.numpy as jnp
from jax import lax
from jax.sharding import Mesh, PartitionSpec as P

epsilon = 1e-05
PAIR = ((0, 1), (1, 0))


def ring_order(count):
    return list(range(0, count, 2)) + list(range(1, count, 2))[::-1]


def ring_pairs(count):
    order = ring_order(count)
    ahead = [(order[i], order[(i + 1) % count]) for i in range(count)]
    return ahead, [(b, a) for a, b in ahead]


def ring_place(count, offset):
    order = ring_order(count)
    position = [order.index(i) for i in range(count)]
    here = jnp.array(position, jnp.int32)[lax.axis_index("shard")]
    return jnp.array(order, jnp.int32)[(here + offset) % count]


def ring_gather(block, flip=False):
    count = lax.axis_size("shard")
    rows = block.shape[0]
    ahead, back = ring_pairs(count)
    sign = 1
    if flip:
        ahead, back, sign = back, ahead, -1
    far, near = count // 2, count - 1 - count // 2
    whole = jnp.zeros((count * rows, block.shape[1]), block.dtype)
    whole = lax.dynamic_update_slice(whole, block, (lax.axis_index("shard") * rows, 0))
    one = two = block
    for step in range(1, far + 1):
        one = lax.ppermute(one, "shard", ahead)
        whole = lax.dynamic_update_slice(whole, one, (ring_place(count, -sign * step) * rows, 0))
        if step <= near:
            two = lax.ppermute(two, "shard", back)
            whole = lax.dynamic_update_slice(whole, two, (ring_place(count, sign * step) * rows, 0))
    return whole


def ring_scatter(value, flip=False):
    count = lax.axis_size("shard")
    rows = value.shape[0] // count
    ahead, back = ring_pairs(count)
    sign = 1
    if flip:
        ahead, back, sign = back, ahead, -1
    far, near = count // 2, count - 1 - count // 2

    def part(offset):
        start = ring_place(count, offset) * rows
        return lax.dynamic_slice(value, (start, 0), (rows, value.shape[1])).astype(jnp.float32)

    one = part(sign * far).astype(jnp.bfloat16)
    two = part(-sign * near).astype(jnp.bfloat16)
    for step in range(far - 1, -1, -1):
        one = lax.ppermute(one, "shard", ahead)
        if step > 0:
            one = (one.astype(jnp.float32) + part(sign * step)).astype(jnp.bfloat16)
    for step in range(near - 1, -1, -1):
        two = lax.ppermute(two, "shard", back)
        if step > 0:
            two = (two.astype(jnp.float32) + part(-sign * step)).astype(jnp.bfloat16)
    return part(0) + one.astype(jnp.float32) + two.astype(jnp.float32)


def over_core(value):
    return lax.ppermute(value, "core", PAIR)


def over_y(value):
    return lax.ppermute(value, "y", PAIR)


def four_gather(value):
    beside = over_core(value)
    across = over_y(value)
    return jnp.concatenate([value, beside, across, over_core(across)], 0)


def four_scatter(value):
    rows = value.shape[0] // 4
    mine, beside, across, diagonal = (value[i * rows : (i + 1) * rows] for i in range(4))
    other = over_core(diagonal.astype(jnp.bfloat16)).astype(jnp.float32) + across
    received = over_y(other.astype(jnp.bfloat16)).astype(jnp.float32)
    near = over_core(beside.astype(jnp.bfloat16)).astype(jnp.float32)
    return mine + near + received


def outer_sum(left, right):
    return lax.dot_general(
        left, right, (((0,), (0,)), ((), ())), preferred_element_type=jnp.float32
    )


def times_transposed(grad, weight):
    return lax.dot_general(
        grad, weight, (((1,), (1,)), ((), ())), preferred_element_type=jnp.float32
    )


def times(value, weight):
    return jnp.dot(value, weight, preferred_element_type=jnp.float32)


def picked(value, groups, parts, part):
    size = value.shape[1] // (groups * parts)
    row = lax.broadcasted_iota(jnp.int32, (value.shape[1], groups * size), 0)
    column = lax.broadcasted_iota(jnp.int32, (value.shape[1], groups * size), 1)
    wanted = (column // size * parts + part) * size + column % size
    return times(value, (row == wanted).astype(value.dtype)).astype(value.dtype)


def local(
    tokens,
    cotangent,
    in_weight,
    out_weight,
    gate_weight,
    up_weight,
    down_weight,
    mix_gain,
    ffn_gain,
    conv_taps,
):
    shards = lax.axis_size("shard")
    core = lax.axis_index("core")
    member = lax.axis_index("y") * 2 + core
    width = tokens.shape[-1]
    length = tokens.shape[1]
    half = width // 2
    hidden_rows = down_weight.shape[0]

    small = jnp.concatenate([mix_gain[None], ffn_gain[None], conv_taps], 0)
    small_full = lax.all_gather(small, "shard", axis=1, tiled=True)
    in_mine = jnp.concatenate(
        [picked(in_weight[:, i * width : (i + 1) * width], shards, 2, core) for i in range(3)], 1
    )
    out_rows = out_weight.shape[0] // 2
    out_mine = lax.dynamic_slice(out_weight, (core * out_rows, 0), (out_rows, width))
    gate_mine = picked(gate_weight, shards, 4, member)
    up_mine = picked(up_weight, shards, 4, member)
    down_rows = hidden_rows // 4
    down_mine = lax.dynamic_slice(down_weight, (member * down_rows, 0), (down_rows, width))
    in_full = ring_gather(in_mine)
    out_full = ring_gather(out_mine, True)
    gate_full = ring_gather(gate_mine, True)
    up_full = ring_gather(up_mine)
    down_full = ring_gather(down_mine, True)

    params = small_full.astype(jnp.float32)
    gain_one = params[0]
    gain_two = params[1]
    taps = lax.dynamic_index_in_dim(
        params[2:5].reshape(3, shards, 2, half // shards), core, 2, keepdims=False
    ).reshape(3, half)

    inputs = tokens[0].astype(jnp.float32)
    factor_one = lax.rsqrt(jnp.mean(inputs * inputs, axis=-1, keepdims=True) + epsilon)
    unit_one = inputs * factor_one
    normed_own = (unit_one * gain_one).astype(jnp.bfloat16)
    normed = jnp.concatenate([normed_own, over_core(normed_own)], 0)
    mixed = times(normed, in_full)
    b_part = mixed[:, :half].reshape(2, length, half)
    c_part = mixed[:, half : 2 * half].reshape(2, length, half)
    x_part = mixed[:, 2 * half :].reshape(2, length, half)
    product = (b_part * x_part).astype(jnp.bfloat16)
    previous = lax.ppermute(
        product[:, length - 2 :], "shard", [(i, i + 1) for i in range(shards - 1)]
    )
    padded = jnp.concatenate([previous, product], 1).astype(jnp.float32)
    conv = (
        taps[0] * padded[:, :length] + taps[1] * padded[:, 1 : length + 1] + taps[2] * padded[:, 2:]
    )
    gated = (c_part * conv).astype(jnp.bfloat16).reshape(2 * length, half)
    branch = times(gated, out_full)
    resid = (
        inputs
        + branch[:length]
        + over_core(branch[length:].astype(jnp.bfloat16)).astype(jnp.float32)
    )

    factor_two = lax.rsqrt(jnp.mean(resid * resid, axis=-1, keepdims=True) + epsilon)
    unit_two = resid * factor_two
    hnorm = four_gather((unit_two * gain_two).astype(jnp.bfloat16))
    grad_rows = four_gather(cotangent[0])
    gate = times(hnorm, gate_full)
    upper = times(hnorm, up_full)
    sigma = jax.nn.sigmoid(gate)
    activated = gate * sigma
    hidden = (activated * upper).astype(jnp.bfloat16)
    d_hidden = times_transposed(grad_rows, down_full)
    d_gate = (d_hidden * upper * sigma * (1.0 + gate * (1.0 - sigma))).astype(jnp.bfloat16)
    d_up = (d_hidden * activated).astype(jnp.bfloat16)
    d_hnorm = four_scatter(times_transposed(d_gate, gate_full) + times_transposed(d_up, up_full))
    g_down = ring_scatter(outer_sum(hidden, grad_rows))
    g_gate = ring_scatter(outer_sum(hnorm, d_gate), True)
    g_up = ring_scatter(outer_sum(hnorm, d_up))
    output = (resid + four_scatter(times(hidden, down_full))).astype(jnp.bfloat16)

    g_ffn_gain = jnp.sum(d_hnorm * unit_two, axis=0)
    scaled_two = d_hnorm * gain_two
    d_resid = cotangent[0].astype(jnp.float32) + factor_two * (
        scaled_two - unit_two * jnp.mean(scaled_two * unit_two, axis=-1, keepdims=True)
    )

    d_own = d_resid.astype(jnp.bfloat16)
    d_branch = jnp.concatenate([d_own, over_core(d_own)], 0)
    d_gated = times_transposed(d_branch, out_full).reshape(2, length, half)
    g_out = ring_scatter(outer_sum(gated, d_branch), True)
    d_cpart = d_gated * conv
    d_conv = d_gated * c_part
    tap_grads = jnp.stack(
        [jnp.sum(d_conv * padded[:, k : k + length], axis=(0, 1)) for k in range(3)], 0
    )
    spread = (
        jnp.pad(taps[0] * d_conv, ((0, 0), (0, 2), (0, 0)))
        + jnp.pad(taps[1] * d_conv, ((0, 0), (1, 1), (0, 0)))
        + jnp.pad(taps[2] * d_conv, ((0, 0), (2, 0), (0, 0)))
    )
    returned = lax.ppermute(spread[:, :2], "shard", [(i + 1, i) for i in range(shards - 1)])
    d_product = spread[:, 2:].at[:, length - 2 :].add(returned)
    d_mixed = (
        jnp.concatenate([d_product * x_part, d_cpart, d_product * b_part], -1)
        .astype(jnp.bfloat16)
        .reshape(2 * length, 3 * half)
    )
    d_normed = times_transposed(d_mixed, in_full)
    g_in = ring_scatter(outer_sum(normed, d_mixed))
    d_normed = d_normed[:length] + over_core(d_normed[length:].astype(jnp.bfloat16)).astype(
        jnp.float32
    )
    g_mix_gain = jnp.sum(d_normed * unit_one, axis=0)
    scaled_one = d_normed * gain_one
    d_inputs = d_resid + factor_one * (
        scaled_one - unit_one * jnp.mean(scaled_one * unit_one, axis=-1, keepdims=True)
    )

    def summed(value):
        return lax.psum(value, "outer") if lax.axis_size("outer") > 1 else value

    def four_parts(value):
        rows = value.shape[0]
        found = four_gather(summed(value).astype(jnp.bfloat16)).reshape(4, rows, value.shape[1])
        y_bit, c_bit = member // 2, core
        found = jnp.where(c_bit == 1, found[jnp.array([1, 0, 3, 2])], found)
        return jnp.where(y_bit == 1, found[jnp.array([2, 3, 0, 1])], found)

    def spread_four(value):
        rows = value.shape[0]
        parts = four_parts(value).reshape(4, rows, shards, down_rows)
        return parts.transpose(1, 2, 0, 3).reshape(rows, -1).astype(jnp.float32)

    def two_parts(value):
        mine = summed(value).astype(jnp.bfloat16)
        mine = (mine.astype(jnp.float32) + over_y(mine).astype(jnp.float32)).astype(jnp.bfloat16)
        other = over_core(mine)
        return jnp.where(core == 0, jnp.stack([mine, other]), jnp.stack([other, mine]))

    owned_in = two_parts(g_in).reshape(2, -1, 3, shards, half // shards)
    owned_in = owned_in.transpose(1, 2, 3, 0, 4).reshape(-1, 3 * width).astype(jnp.float32)
    owned_out = two_parts(g_out).reshape(-1, width).astype(jnp.float32)
    owned_down = four_parts(g_down).reshape(-1, width).astype(jnp.float32)
    spot = lax.broadcasted_iota(jnp.int32, (3, shards, 2, half // shards), 2)
    tap_full = jnp.where(
        spot == core, tap_grads.reshape(3, shards, 1, half // shards), 0.0
    ).reshape(3, width)
    small_grads = jnp.concatenate([g_mix_gain[None], g_ffn_gain[None], tap_full], 0)
    small_grads = lax.psum(small_grads, ("shard", "outer", "y", "core"))
    own = width // shards
    small_owned = lax.dynamic_slice(small_grads, (0, lax.axis_index("shard") * own), (5, own))
    return (
        output[None],
        d_inputs.astype(jnp.bfloat16)[None],
        owned_in,
        owned_out,
        spread_four(g_gate),
        spread_four(g_up),
        owned_down,
        small_owned[0],
        small_owned[1],
        small_owned[2:5],
    )


def solution(mesh):
    shards = mesh.shape["shard"]
    reps = mesh.shape["rep"]
    finer = Mesh(mesh.devices.reshape(shards, reps // 4, 2, 2), ("shard", "outer", "y", "core"))
    rep = ("outer", "y", "core")
    in_specs = (
        P(rep, "shard", None),
        P(rep, "shard", None),
        P("shard", None),
        P("shard", None),
        P("shard", None),
        P("shard", None),
        P("shard", None),
        P("shard"),
        P("shard"),
        P(None, "shard"),
    )
    return jax.shard_map(
        local, mesh=finer, in_specs=in_specs, out_specs=in_specs, check_vma=False
    )
```

time: 2110 us -> 633 us (0.30)
  waiting for transfers between devices: 1890 us -> 169 us
  local copies, waits for them, and re-layouts: 20.2 us -> 101 us
  starting transfers between devices: 4.23 us -> 83.1 us
  other arithmetic: 11.2 us -> 53 us
  blocking collectives: 33.9 us -> 66.6 us
    reduce_scatter x6 -> x0, waiting for transfers between devices: 1220 us -> none  [the longest x1 317 us: local(): lax.psum_scatter(g_up, 'shard', scatter_dimension=0, tiled=True)]
    all_gather x5 -> x0, waiting for transfers between devices: 498 us -> none  [the longest x1 134 us: local(): lax.all_gather(up_weight, 'shard', axis=0, tiled=True)]
    ppermute x2 -> x101, waiting for transfers between devices: 4.29 us -> 169 us  [the longest x20 57 us: ring_gather(): one = lax.ppermute(one, 'shard', ahead)]
    psum x1 -> x0, waiting for transfers between devices: 162 us -> none  [local(): mix_shares = lax.psum((mix_shares[0], mix_shares[1], mix_shares[2]), 'rep')]
    ppermute x2 -> x101, starting transfers between devices: 3.75 us -> 83.1 us  [the longest x20 24.5 us: ring_scatter(): one = lax.ppermute(one, 'shard', ahead)]
    psum x1, blocking collectives: 5.76 us -> 40.3 us  [local(): small_grads = lax.psum(small_grads, ('shard', 'outer', 'y', 'core'))]
    convert_element_type x3 -> x34, other arithmetic: 2.93 us -> 30.9 us  [the longest x15 5.62 us: ring_scatter(): one = (one.astype(jnp.float32) + part(sign * step)).astype(jnp.bfloat16)]
    gather x0 -> x10, local copies, waits for them, and re-layouts: none -> 25.7 us  [the longest x5 13 us: four_parts(): return jnp.where(y_bit == 1, found[jnp.array([2, 3, 0, 1])], found)]
  transfers between devices with their start and end apart: 14 -> 101, of which waited for: 14 -> 39; matrix products, arithmetic and copies ran while one was open for 5% -> 32% of each run, Pallas kernels for 0% -> 0%
where the time goes in v1:
time: 633 us; the launch traced here: 625 us
  waiting for transfers between devices  169 us (27%)
  matrix products  125 us (20%)
  local copies, waits for them, and re-layouts  101 us (16%)
  starting transfers between devices  83.1 us (13%)
  blocking collectives  66.6 us (11%)
  other arithmetic  53 us (8%)
  between operations  27.2 us (4%)
    dot_general x10, matrix products, times(): return jnp.dot(value, weight, preferred_element_type=jnp.float32)  57.1 us
    ppermute x20, waiting for transfers between devices, ring_gather(): one = lax.ppermute(one, 'shard', ahead)  57 us
    ppermute x20, waiting for transfers between devices, ring_scatter(): one = lax.ppermute(one, 'shard', ahead)  45.8 us
    ppermute x9, waiting for transfers between devices, over_y(): return lax.ppermute(value, 'y', PAIR)  43.3 us
    psum x1, blocking collectives, local(): small_grads = lax.psum(small_grads, ('shard', 'outer', 'y', 'core'))  40.3 us
    dot_general x5, matrix products, times_transposed(): lax.dot_general(grad, weight, (((1,), (1,)), ((), ())), preferred_element...  36.7 us
    dot_general x5, matrix products, outer_sum(): lax.dot_general(left, right, (((0,), (0,)), ((), ())), preferred_element_...  31 us
    all_gather x1, blocking collectives, local(): small_full = lax.all_gather(small, 'shard', axis=1, tiled=True)  26.2 us
  transfers between devices with their start and end apart: 101, of which 39 were waited for; matrix products, arithmetic and copies ran while one was open for 32% of the time, Pallas kernels for 0%

profile of v1, /device:TPU:0, one launch (start us, length us, event | category | flops | bytes accessed | tf_op | source)
XLA Modules:
  0.0 624.6 jit_solution(7396061567477872655)
XLA Ops:
  2.5 4.1 constant_dynamic-update-slice_fusion.19
  37.0 26.2 %all_gather.3 = bf16[5,1024]{1,0:T(8,128)(2,1)S(1)} all-gather(bf16[5,128]{1,0:T(8,128)(2,1)S(1)} %pad_maximum_fusion.18), channel_id=1, replica_groups=mesh['shard'=8,'outer'=1,'y'=2,'core'=2] {'shard'}, dimensions={1}, use_global_device_ids=true | all-gather | bytes 11520 | tf_op jit(solution)/shard_map/all_gather | solution.py:141
  74.8 4.3 constant_dynamic-update-slice_fusion.5
  99.3 4.4 collective-permute-done.28
  109.0 3.7 collective-permute-done.13
  118.3 6.9 %collective-permute-done.15 = bf16[64,1024]{1,0:T(8,128)(2,1)S(1)} collective-permute-done((bf16[64,1024]{1,0:T(8,128)(2,1)S(1)}, bf16[64,1024]{1,0:T(8,128)(2,1)S(1)}, u32[]{:S(2)}, u32[]{:S(2)}) %collective-permute-start.15) | collective-permute-done | bytes 131104 | tf_op jit(solution)/shard_map/ppermute | solution.py:39
  128.0 3.3 collective-permute-done.4
  133.4 10.8 %collective-permute-done.5 = bf16[128,1536]{0,1:T(8,128)(2,1)S(1)} collective-permute-done((bf16[128,1536]{0,1:T(8,128)(2,1)S(1)}, bf16[128,1536]{0,1:T(8,128)(2,1)S(1)}, u32[]{:S(2)}, u32[]{:S(2)}) %collective-permute-start.5) | collective-permute-done | bytes 393248 | tf_op jit(solution)/shard_map/ppermute | solution.py:39
  145.8 6.2 collective-permute-done.7
  153.0 5.5 fusion.41
  160.6 3.8 collective-permute-start.8
  165.7 3.3 collective-permute-start.37
  175.8 6.8 %collective-permute-done.24 = bf16[128,1152]{0,1:T(8,128)(2,1)S(1)} collective-permute-done((bf16[128,1152]{0,1:T(8,128)(2,1)S(1)}, bf16[128,1152]{0,1:T(8,128)(2,1)S(1)}, u32[]{:S(2)}, u32[]{:S(2)}) %collective-permute-start.24) | collective-permute-done | bytes 294944 | tf_op jit(solution)/shard_map/ppermute | solution.py:39
  187.5 3.9 collective-permute-done.31
  191.5 3.6 collective-permute-done.32
  195.1 4.7 collective-permute-done.38
  202.7 5.4 collective-permute-done.33
  210.8 4.6 collective-permute-done.18
  216.1 11.5 %fusion.51 = f32[2048,1152]{1,0:T(8,128)} fusion(bf16[1152,1024]{1,0:T(8,128)(2,1)S(1)} %constant_dynamic-update-slice_fusion.28, bf16[512,1024]{1,0:T(8,128)(2,1)S(1)} %collective-permute-done.46, bf16[512,1024]{1,0:T(8,128)(2,1)S(1)} %collective-permute-done.45, bf16[512,1024]{1,0:T(8,128)(2,1)S(1)} %collective-permute-done.44, ...), kind=kOutput, calls=%fused_computation.111 | convolution fusion | flops 4848615424 | bytes 15990784 | tf_op jit(solution)/shard_map/dot_general | solution.py:103
  229.5 11.5 %fusion.92 = f32[2048,1152]{1,0:T(8,128)} fusion(bf16[1024,1152]{0,1:T(8,128)(2,1)S(1)} %constant_dynamic-update-slice_fusion.18, bf16[512,1024]{1,0:T(8,128)(2,1)S(1)} %collective-permute-done.19, bf16[512,1024]{1,0:T(8,128)(2,1)S(1)} %collective-permute-done.18, bf16[512,1024]{1,0:T(8,128)(2,1)S(1)} %collective-permute-done.17, ...), kind=kOutput, calls=%fused_computation.255 | convolution fusion | flops 4848615424 | bytes 15990784 | tf_op jit(solution)/shard_map/dot_general | solution.py:109
  241.0 18.6 %multiply_convert_fusion.1 = (bf16[2048,1152]{1,0:T(8,128)(2,1)}, bf16[2048,1152]{1,0:T(8,128)(2,1)}, bf16[2048,1152]{1,0:T(8,128)(2,1)}) fusion(f32[2048,1152]{1,0:T(8,128)} %fusion.51, f32[2048,1152]{1,0:T(8,128)} %fusion.92, bf16[1024,1152]{0,1:T(8,128)(2,1)} %constant_dynamic-update-slice_fusion.6, bf16[512,1024]{1,0:T(8,128)(2,1)} %copy-done.99, ...), kind=kOutput, calls=%fused_computation.9 | convolution fusion | flops 4884004864 | bytes 39583744 | tf_op jit(solution)/shard_map/dot_general | solution.py:109
  259.6 10.3 %fusion.102 = (bf16[2048,1024]{1,0:T(8,128)(2,1)S(1)}, f32[2048,1024]{1,0:T(8,128)}) fusion(bf16[2048,1152]{1,0:T(8,128)(2,1)} %get-tuple-element.65, bf16[1152,1024]{1,0:T(8,128)(2,1)} %copy-done.33), kind=kOutput, calls=%fused_computation.264 | convolution fusion | flops 4833935360 | bytes 19660800 | tf_op jit(solution)/shard_map/dot_general | solution.py:109
  272.0 7.7 %fusion.104 = f32[2048,1024]{1,0:T(8,128)} fusion(bf16[2048,1152]{1,0:T(8,128)(2,1)S(1)} %copy-done.104, bf16[1024,1152]{0,1:T(8,128)(2,1)S(1)} %copy-done.32), kind=kOutput, calls=%fused_computation.266 | convolution fusion | flops 4831838208 | bytes 15466496 | tf_op jit(solution)/shard_map/dot_general | solution.py:103
  279.8 8.9 %fusion.101 = (bf16[2048,1024]{1,0:T(8,128)(2,1)S(1)}, f32[2048,1024]{1,0:T(8,128)S(1)}) fusion(f32[2048,1024]{1,0:T(8,128)} %fusion.104, bf16[2048,1152]{1,0:T(8,128)(2,1)S(1)} %bitcast.181, bf16[1024,1152]{0,1:T(8,128)(2,1)} %constant_dynamic-update-slice_fusion.6), kind=kOutput, calls=%fused_computation.263 | convolution fusion | flops 4836032512 | bytes 28049408 | tf_op jit(solution)/shard_map/dot_general | solution.py:103
  294.0 7.6 %fusion.50 = f32[1152,1024]{1,0:T(8,128)S(1)} fusion(bf16[2048,1152]{1,0:T(8,128)(2,1)} %get-tuple-element.65, bf16[512,1024]{1,0:T(8,128)(2,1)S(1)} %copy-done.96, bf16[512,1024]{1,0:T(8,128)(2,1)S(1)} %copy-done.89, bf16[512,1024]{1,0:T(8,128)(2,1)S(1)} %copy-done.91, bf16[512,1024]{1,0:T(8,128)(2,1)S(1)} %bitcast.159), kind=kOutput, calls=%fused_computation.110 | convolution fusion | flops 4848615424 | bytes 13631488 | tf_op jit(solution)/shard_map/dot_general | solution.py:97
  303.8 8.2 %fusion.90 = f32[1024,1152]{1,0:T(8,128)S(1)} fusion(bf16[2048,1152]{1,0:T(8,128)(2,1)} %get-tuple-element.64, bf16[512,1024]{1,0:T(8,128)(2,1)S(1)} %copy-done.100, bf16[512,1024]{1,0:T(8,128)(2,1)S(1)} %copy-done.93, bf16[512,1024]{1,0:T(8,128)(2,1)S(1)} %copy-done.98, bf16[512,1024]{1,0:T(8,128)(2,1)S(1)} %copy-done.45), kind=kOutput, calls=%fused_computation.253 | convolution fusion | flops 4848615424 | bytes 13631488 | tf_op jit(solution)/shard_map/dot_general | solution.py:97
  314.5 8.9 %fusion.91 = f32[1024,1152]{1,0:T(8,128)S(1)} fusion(bf16[2048,1152]{1,0:T(8,128)(2,1)} %get-tuple-element.63, bf16[512,1024]{1,0:T(8,128)(2,1)} %copy-done.99, bf16[512,1024]{1,0:T(8,128)(2,1)S(1)} %copy-done.94, bf16[512,1024]{1,0:T(8,128)(2,1)} %copy-done.97, bf16[512,1024]{1,0:T(8,128)(2,1)S(1)} %copy-done.45), kind=kOutput, calls=%fused_computation.254 | convolution fusion | flops 4848615424 | bytes 13631488 | tf_op jit(solution)/shard_map/dot_general | solution.py:97
  325.8 5.5 collective-permute-done.71
  335.8 5.5 collective-permute-done.82
  342.8 4.8 collective-permute-done.75
  349.7 4.2 collective-permute-done.93
  360.0 3.3 collective-permute-done.73
  377.0 3.4 collective-permute-done.84
  380.5 4.1 collective-permute-done.74
  388.6 6.2 collective-permute-done.89
  396.7 3.4 collective-permute-done.79
  400.7 3.9 reshape.527
  418.5 5.1 reshape.526
  432.3 20.6 %collective-permute-done.49 = bf16[512,1024]{1,0:T(8,128)(2,1)} collective-permute-done((bf16[512,1024]{1,0:T(8,128)(2,1)}, bf16[512,1024]{1,0:T(8,128)(2,1)}, u32[]{:S(2)}, u32[]{:S(2)}) %collective-permute-start.49) | collective-permute-done | bytes 1048608 | tf_op jit(solution)/shard_map/ppermute | solution.py:78
  456.0 5.6 fusion.94
  500.9 3.6 fusion.40
  512.8 3.5 fusion.44
  532.6 5.9 collective-permute-done.65
  540.4 5.4 fusion.42
  549.9 8.1 %collective-permute-done.55 = bf16[128,1536]{1,0:T(8,128)(2,1)S(1)} collective-permute-done((bf16[128,1536]{1,0:T(8,128)(2,1)S(1)}, bf16[128,1536]{1,0:T(8,128)(2,1)S(1)}, u32[]{:S(2)}, u32[]{:S(2)}) %collective-permute-start.55) | collective-permute-done | bytes 393248 | tf_op jit(solution)/shard_map/ppermute | solution.py:63
  563.1 40.3 %psum.7 = f32[5,1024]{1,0:T(8,128)S(1)} all-reduce(f32[5,1024]{1,0:T(8,128)S(1)} %pad_maximum_fusion.17), channel_id=1, replica_groups=mesh['shard'=8,'outer'=1,'y'=2,'core'=2] {'shard','outer','y','core'}, use_global_device_ids=true, to_apply=%region_9.10 | all-reduce | flops 5120 | bytes 40960 | tf_op jit(solution)/shard_map/psum | solution.py:275
  608.4 7.3 %collective-permute-done.60 = bf16[128,1536]{1,0:T(8,128)(2,1)S(1)} collective-permute-done((bf16[128,1536]{1,0:T(8,128)(2,1)S(1)}, bf16[128,1536]{1,0:T(8,128)(2,1)S(1)}, u32[]{:S(2)}, u32[]{:S(2)}) %collective-permute-start.60) | collective-permute-done | bytes 393248 | tf_op jit(solution)/shard_map/ppermute | solution.py:78
  616.5 3.2 fusion.49
  (562 shorter events, 240.0 us)
Async XLA Ops:
  6.7 85.8 %collective-permute-start.20 = (bf16[128,1152]{0,1:T(8,128)(2,1)}, bf16[128,1152]{0,1:T(8,128)(2,1)}, u32[]{:S(2)}, u32[]{:S(2)}) collective-permute-start(bf16[128,1152]{0,1:T(8,128)(2,1)} %get-tuple-element.126), channel_id=1, source_target_pairs={{8,0},{16,8},{24,16},{28,24},{20,28},{12,20},{4,12},{0,4},{9,1},{1... | collective-permute-start | bytes 884744 | tf_op jit(solution)/shard_map/ppermute | solution.py:39
  9.7 85.0 %collective-permute-start.21 = (bf16[128,1152]{0,1:T(8,128)(2,1)}, bf16[128,1152]{0,1:T(8,128)(2,1)}, u32[]{:S(2)}, u32[]{:S(2)}) collective-permute-start(bf16[128,1152]{0,1:T(8,128)(2,1)} %get-tuple-element.126), channel_id=1, source_target_pairs={{0,8},{8,16},{16,24},{24,28},{28,20},{20,12},{12,4},{4,0},{1,9},{9... | collective-permute-start | bytes 884744 | tf_op jit(solution)/shard_map/ppermute | solution.py:42
  10.0 73.6 %collective-permute-start.9 = (bf16[64,1024]{1,0:T(8,128)(2,1)S(1)}, bf16[64,1024]{1,0:T(8,128)(2,1)}, u32[]{:S(2)}, u32[]{:S(2)}) collective-permute-start(bf16[64,1024]{1,0:T(8,128)(2,1)S(1)} %get-tuple-element.60), channel_id=1, source_target_pairs={{8,0},{16,8},{24,16},{28,24},{20,28},{12,20},{4,12},{0,4},{9,1},{1... | collective-permute-start | bytes 393224 | tf_op jit(solution)/shard_map/ppermute | solution.py:39
  11.9 72.2 %collective-permute-start.10 = (bf16[64,1024]{1,0:T(8,128)(2,1)S(1)}, bf16[64,1024]{1,0:T(8,128)(2,1)}, u32[]{:S(2)}, u32[]{:S(2)}) collective-permute-start(bf16[64,1024]{1,0:T(8,128)(2,1)S(1)} %get-tuple-element.60), channel_id=1, source_target_pairs={{0,8},{8,16},{16,24},{24,28},{28,20},{20,12},{12,4},{4,0},{1,9},{9... | collective-permute-start | bytes 393224 | tf_op jit(solution)/shard_map/ppermute | solution.py:42
  16.7 96.8 %collective-permute-start.1 = (bf16[128,1536]{0,1:T(8,128)(2,1)}, bf16[128,1536]{0,1:T(8,128)(2,1)}, u32[]{:S(2)}, u32[]{:S(2)}) collective-permute-start(bf16[128,1536]{0,1:T(8,128)(2,1)} %get-tuple-element.110), channel_id=1, source_target_pairs={{0,8},{8,16},{16,24},{24,28},{28,20},{20,12},{12,4},{4,0},{1,9},{9... | collective-permute-start | bytes 1179656 | tf_op jit(solution)/shard_map/ppermute | solution.py:39
  90.4 27.0 %collective-permute-start.2 = (bf16[128,1536]{0,1:T(8,128)(2,1)}, bf16[128,1536]{0,1:T(8,128)(2,1)S(1)}, u32[]{:S(2)}, u32[]{:S(2)}) collective-permute-start(bf16[128,1536]{0,1:T(8,128)(2,1)} %get-tuple-element.110), channel_id=1, source_target_pairs={{8,0},{16,8},{24,16},{28,24},{20,28},{12,20},{4,12},{0,4},{9,1},{1... | collective-permute-start | bytes 1179656 | tf_op jit(solution)/shard_map/ppermute | solution.py:42
  103.7 49.1 %collective-permute-start = (bf16[512,1024]{1,0:T(8,128)(2,1)S(1)}, bf16[512,1024]{1,0:T(8,128)(2,1)S(1)}, u32[]{:S(2)}, u32[]{:S(2)}) collective-permute-start(bf16[512,1024]{1,0:T(8,128)(2,1)S(1)} %copy-done.42), channel_id=1, source_target_pairs={{0,1},{1,0},{2,3},{3,2},{4,5},{5,4},{6,7},{7,6},{8,9},{9,8},{10,11... | collective-permute-start | bytes 3145736 | tf_op jit(solution)/shard_map/ppermute | solution.py:74
  112.7 14.0 %collective-permute-start.22 = (bf16[128,1152]{0,1:T(8,128)(2,1)}, bf16[128,1152]{0,1:T(8,128)(2,1)S(1)}, u32[]{:S(2)}, u32[]{:S(2)}) collective-permute-start(bf16[128,1152]{0,1:T(8,128)(2,1)} %collective-permute-done.20), channel_id=1, source_target_pairs={{8,0},{16,8},{24,16},{28,24},{20,28},{12,20},{4,12},{0,4},{9,1},{1... | collective-permute-start | bytes 884744 | tf_op jit(solution)/shard_map/ppermute | solution.py:39
  113.5 14.1 %collective-permute-start.3 = (bf16[128,1536]{0,1:T(8,128)(2,1)}, bf16[128,1536]{0,1:T(8,128)(2,1)S(1)}, u32[]{:S(2)}, u32[]{:S(2)}) collective-permute-start(bf16[128,1536]{0,1:T(8,128)(2,1)} %collective-permute-done.1), channel_id=1, source_target_pairs={{0,8},{8,16},{16,24},{24,28},{28,20},{20,12},{12,4},{4,0},{1,9},{9... | collective-permute-start | bytes 1179656 | tf_op jit(solution)/shard_map/ppermute | solution.py:39
  117.4 13.9 %collective-permute-start.4 = (bf16[128,1536]{0,1:T(8,128)(2,1)S(1)}, bf16[128,1536]{0,1:T(8,128)(2,1)S(1)}, u32[]{:S(2)}, u32[]{:S(2)}) collective-permute-start(bf16[128,1536]{0,1:T(8,128)(2,1)S(1)} %collective-permute-done.2), channel_id=1, source_target_pairs={{8,0},{16,8},{24,16},{28,24},{20,28},{12,20},{4,12},{0,4},{9,1},{1... | collective-permute-start | bytes 1179656 | tf_op jit(solution)/shard_map/ppermute | solution.py:42
  125.2 74.9 %collective-permute-start.45 = (bf16[512,1024]{1,0:T(8,128)(2,1)S(1)}, bf16[512,1024]{1,0:T(8,128)(2,1)S(1)}, u32[]{:S(2)}, u32[]{:S(2)}) collective-permute-start(bf16[512,1024]{1,0:T(8,128)(2,1)S(1)} %bitcast.156), channel_id=1, source_target_pairs={{0,2},{2,0},{1,3},{3,1},{4,6},{6,4},{5,7},{7,5},{8,10},{10,8},{9,1... | collective-permute-start | bytes 3145736 | tf_op jit(solution)/shard_map/ppermute | solution.py:78
  126.7 33.9 %collective-permute-start.23 = (bf16[128,1152]{0,1:T(8,128)(2,1)}, bf16[128,1152]{0,1:T(8,128)(2,1)S(1)}, u32[]{:S(2)}, u32[]{:S(2)}) collective-permute-start(bf16[128,1152]{0,1:T(8,128)(2,1)} %collective-permute-done.21), channel_id=1, source_target_pairs={{0,8},{8,16},{16,24},{24,28},{28,20},{20,12},{12,4},{4,0},{1,9},{9... | collective-permute-start | bytes 884744 | tf_op jit(solution)/shard_map/ppermute | solution.py:42
  127.6 16.5 %collective-permute-start.5 = (bf16[128,1536]{0,1:T(8,128)(2,1)S(1)}, bf16[128,1536]{0,1:T(8,128)(2,1)S(1)}, u32[]{:S(2)}, u32[]{:S(2)}) collective-permute-start(bf16[128,1536]{0,1:T(8,128)(2,1)S(1)} %collective-permute-done.3), channel_id=1, source_target_pairs={{0,8},{8,16},{16,24},{24,28},{28,20},{20,12},{12,4},{4,0},{1,9},{9... | collective-permute-start | bytes 1179656 | tf_op jit(solution)/shard_map/ppermute | solution.py:39
  131.3 13.6 %collective-permute-start.6 = (bf16[128,1536]{0,1:T(8,128)(2,1)S(1)}, bf16[128,1536]{0,1:T(8,128)(2,1)S(1)}, u32[]{:S(2)}, u32[]{:S(2)}) collective-permute-start(bf16[128,1536]{0,1:T(8,128)(2,1)S(1)} %collective-permute-done.4), channel_id=1, source_target_pairs={{8,0},{16,8},{24,16},{28,24},{20,28},{12,20},{4,12},{0,4},{9,1},{1... | collective-permute-start | bytes 1179656 | tf_op jit(solution)/shard_map/ppermute | solution.py:42
  145.0 27.9 %collective-permute-start.29 = (bf16[128,1152]{0,1:T(8,128)(2,1)S(1)}, bf16[128,1152]{0,1:T(8,128)(2,1)S(1)}, u32[]{:S(2)}, u32[]{:S(2)}) collective-permute-start(bf16[128,1152]{0,1:T(8,128)(2,1)S(1)} %collective-permute-done.27), channel_id=1, source_target_pairs={{0,8},{8,16},{16,24},{24,28},{28,20},{20,12},{12,4},{4,0},{1,9},{9... | collective-permute-start | bytes 884744 | tf_op jit(solution)/shard_map/ppermute | solution.py:39
  151.9 21.1 %collective-permute-start.30 = (bf16[128,1152]{0,1:T(8,128)(2,1)S(1)}, bf16[128,1152]{0,1:T(8,128)(2,1)S(1)}, u32[]{:S(2)}, u32[]{:S(2)}) collective-permute-start(bf16[128,1152]{0,1:T(8,128)(2,1)S(1)} %collective-permute-done.28), channel_id=1, source_target_pairs={{8,0},{16,8},{24,16},{28,24},{20,28},{12,20},{4,12},{0,4},{9,1},{1... | collective-permute-start | bytes 884744 | tf_op jit(solution)/shard_map/ppermute | solution.py:42
  152.8 20.5 %collective-permute-start.36 = (bf16[144,1024]{1,0:T(8,128)(2,1)S(1)}, bf16[144,1024]{1,0:T(8,128)(2,1)S(1)}, u32[]{:S(2)}, u32[]{:S(2)}) collective-permute-start(bf16[144,1024]{1,0:T(8,128)(2,1)S(1)} %collective-permute-done.34), channel_id=1, source_target_pairs={{8,0},{16,8},{24,16},{28,24},{20,28},{12,20},{4,12},{0,4},{9,1},{1... | collective-permute-start | bytes 884744 | tf_op jit(solution)/shard_map/ppermute | solution.py:39
  173.3 42.8 %collective-permute-start.44 = (bf16[512,1024]{1,0:T(8,128)(2,1)S(1)}, bf16[512,1024]{1,0:T(8,128)(2,1)S(1)}, u32[]{:S(2)}, u32[]{:S(2)}) collective-permute-start(bf16[512,1024]{1,0:T(8,128)(2,1)S(1)} %bitcast.157), channel_id=1, source_target_pairs={{0,1},{1,0},{2,3},{3,2},{4,5},{5,4},{6,7},{7,6},{8,9},{9,8},{10,11... | collective-permute-start | bytes 3145736 | tf_op jit(solution)/shard_map/ppermute | solution.py:74
  191.4 24.0 %collective-permute-start.18 = (bf16[512,1024]{1,0:T(8,128)(2,1)S(1)}, bf16[512,1024]{1,0:T(8,128)(2,1)S(1)}, u32[]{:S(2)}, u32[]{:S(2)}) collective-permute-start(bf16[512,1024]{1,0:T(8,128)(2,1)S(1)} %multiply_convert_fusion.6), channel_id=1, source_target_pairs={{0,2},{2,0},{1,3},{3,1},{4,6},{6,4},{5,7},{7,5},{8,10},{10,8},{9,1... | collective-permute-start | bytes 3145736 | tf_op jit(solution)/shard_map/ppermute | solution.py:78
  200.1 16.0 %collective-permute-start.46 = (bf16[512,1024]{1,0:T(8,128)(2,1)S(1)}, bf16[512,1024]{1,0:T(8,128)(2,1)S(1)}, u32[]{:S(2)}, u32[]{:S(2)}) collective-permute-start(bf16[512,1024]{1,0:T(8,128)(2,1)S(1)} %collective-permute-done.45), channel_id=1, source_target_pairs={{0,1},{1,0},{2,3},{3,2},{4,5},{5,4},{6,7},{7,6},{8,9},{9,8},{10,11... | collective-permute-start | bytes 3145736 | tf_op jit(solution)/shard_map/ppermute | solution.py:74
  210.8 16.8 %collective-permute-start.17 = (bf16[512,1024]{1,0:T(8,128)(2,1)S(1)}, bf16[512,1024]{1,0:T(8,128)(2,1)S(1)}, u32[]{:S(2)}, u32[]{:S(2)}) collective-permute-start(bf16[512,1024]{1,0:T(8,128)(2,1)S(1)} %multiply_convert_fusion.6), channel_id=1, source_target_pairs={{0,1},{1,0},{2,3},{3,2},{4,5},{5,4},{6,7},{7,6},{8,9},{9,8},{10,11... | collective-permute-start | bytes 3145736 | tf_op jit(solution)/shard_map/ppermute | solution.py:74
  271.1 97.6 %collective-permute-start.42 = (bf16[512,1024]{1,0:T(8,128)(2,1)S(1)}, bf16[512,1024]{1,0:T(8,128)(2,1)S(1)}, u32[]{:S(2)}, u32[]{:S(2)}) collective-permute-start(bf16[512,1024]{1,0:T(8,128)(2,1)S(1)} %get-tuple-element.96), channel_id=1, source_target_pairs={{0,1},{1,0},{2,3},{3,2},{4,5},{5,4},{6,7},{7,6},{8,9},{9,8},{10,11... | collective-permute-start | bytes 3145736 | tf_op jit(solution)/shard_map/ppermute | solution.py:74
  301.7 21.8 %collective-permute-start.91 = (bf16[144,1024]{1,0:T(8,128)(2,1)S(1)}, bf16[144,1024]{1,0:T(8,128)(2,1)S(1)}, u32[]{:S(2)}, u32[]{:S(2)}) collective-permute-start(bf16[144,1024]{1,0:T(8,128)(2,1)S(1)} %get-tuple-element.79), channel_id=1, source_target_pairs={{0,8},{8,16},{16,24},{24,28},{28,20},{20,12},{12,4},{4,0},{1,9},{9... | collective-permute-start | bytes 884744 | tf_op jit(solution)/shard_map/ppermute | solution.py:63
  303.1 29.7 %collective-permute-start.95 = (bf16[144,1024]{1,0:T(8,128)(2,1)S(1)}, bf16[144,1024]{1,0:T(8,128)(2,1)S(1)}, u32[]{:S(2)}, u32[]{:S(2)}) collective-permute-start(bf16[144,1024]{1,0:T(8,128)(2,1)S(1)} %get-tuple-element.80), channel_id=1, source_target_pairs={{8,0},{16,8},{24,16},{28,24},{20,28},{12,20},{4,12},{0,4},{9,1},{1... | collective-permute-start | bytes 884744 | tf_op jit(solution)/shard_map/ppermute | solution.py:67
  313.4 21.7 %collective-permute-start.85 = (bf16[128,1152]{1,0:T(8,128)(2,1)S(1)}, bf16[128,1152]{1,0:T(8,128)(2,1)S(1)}, u32[]{:S(2)}, u32[]{:S(2)}) collective-permute-start(bf16[128,1152]{1,0:T(8,128)(2,1)S(1)} %get-tuple-element.86), channel_id=1, source_target_pairs={{8,0},{16,8},{24,16},{28,24},{20,28},{12,20},{4,12},{0,4},{9,1},{1... | collective-permute-start | bytes 884744 | tf_op jit(solution)/shard_map/ppermute | solution.py:67
  332.8 14.7 %collective-permute-start.75 = (bf16[128,1152]{1,0:T(8,128)(2,1)S(1)}, bf16[128,1152]{1,0:T(8,128)(2,1)S(1)}, u32[]{:S(2)}, u32[]{:S(2)}) collective-permute-start(bf16[128,1152]{1,0:T(8,128)(2,1)S(1)} %get-tuple-element.92), channel_id=1, source_target_pairs={{0,8},{8,16},{16,24},{24,28},{28,20},{20,12},{12,4},{4,0},{1,9},{9... | collective-permute-start | bytes 884744 | tf_op jit(solution)/shard_map/ppermute | solution.py:67
  333.5 15.5 %collective-permute-start.72 = (bf16[128,1152]{1,0:T(8,128)(2,1)S(1)}, bf16[128,1152]{1,0:T(8,128)(2,1)S(1)}, u32[]{:S(2)}, u32[]{:S(2)}) collective-permute-start(bf16[128,1152]{1,0:T(8,128)(2,1)S(1)} %add_convert_fusion.24), channel_id=1, source_target_pairs={{8,0},{16,8},{24,16},{28,24},{20,28},{12,20},{4,12},{0,4},{9,1},{1... | collective-permute-start | bytes 884744 | tf_op jit(solution)/shard_map/ppermute | solution.py:63
  335.1 18.8 %collective-permute-start.93 = (bf16[144,1024]{1,0:T(8,128)(2,1)S(1)}, bf16[144,1024]{1,0:T(8,128)(2,1)S(1)}, u32[]{:S(2)}, u32[]{:S(2)}) collective-permute-start(bf16[144,1024]{1,0:T(8,128)(2,1)S(1)} %get-tuple-element.77), channel_id=1, source_target_pairs={{0,8},{8,16},{16,24},{24,28},{28,20},{20,12},{12,4},{4,0},{1,9},{9... | collective-permute-start | bytes 884744 | tf_op jit(solution)/shard_map/ppermute | solution.py:63
  353.9 31.8 %collective-permute-start.48 = (bf16[512,1024]{1,0:T(8,128)(2,1)S(1)}, bf16[512,1024]{1,0:T(8,128)(2,1)S(1)}, u32[]{:S(2)}, u32[]{:S(2)}) collective-permute-start(bf16[512,1024]{1,0:T(8,128)(2,1)S(1)} %get-tuple-element.94), channel_id=1, source_target_pairs={{0,1},{1,0},{2,3},{3,2},{4,5},{5,4},{6,7},{7,6},{8,9},{9,8},{10,11... | collective-permute-start | bytes 3145736 | tf_op jit(solution)/shard_map/ppermute | solution.py:74
  358.7 15.5 %collective-permute-start.94 = (bf16[144,1024]{1,0:T(8,128)(2,1)S(1)}, bf16[144,1024]{1,0:T(8,128)(2,1)S(1)}, u32[]{:S(2)}, u32[]{:S(2)}) collective-permute-start(bf16[144,1024]{1,0:T(8,128)(2,1)S(1)} %get-tuple-element.75), channel_id=1, source_target_pairs={{0,8},{8,16},{16,24},{24,28},{28,20},{20,12},{12,4},{4,0},{1,9},{9... | collective-permute-start | bytes 884744 | tf_op jit(solution)/shard_map/ppermute | solution.py:63
  380.4 24.2 %collective-permute-start.98 = (bf16[144,1024]{1,0:T(8,128)(2,1)}, bf16[144,1024]{1,0:T(8,128)(2,1)}, u32[]{:S(2)}, u32[]{:S(2)}) collective-permute-start(bf16[144,1024]{1,0:T(8,128)(2,1)} %add_convert_fusion.7), channel_id=1, source_target_pairs={{0,1},{1,0},{2,3},{3,2},{4,5},{5,4},{6,7},{7,6},{8,9},{9,8},{10,11... | collective-permute-start | bytes 884744 | tf_op jit(solution)/shard_map/ppermute | solution.py:74
  385.7 14.4 %collective-permute-start.79 = (bf16[128,1152]{1,0:T(8,128)(2,1)}, bf16[128,1152]{1,0:T(8,128)(2,1)}, u32[]{:S(2)}, u32[]{:S(2)}) collective-permute-start(bf16[128,1152]{1,0:T(8,128)(2,1)} %add_convert_fusion.19), channel_id=1, source_target_pairs={{0,2},{2,0},{1,3},{3,1},{4,6},{6,4},{5,7},{7,5},{8,10},{10,8},{9,1... | collective-permute-start | bytes 884744 | tf_op jit(solution)/shard_map/ppermute | solution.py:78
  388.6 16.0 %collective-permute-start.100 = (bf16[144,1024]{1,0:T(8,128)(2,1)}, bf16[144,1024]{1,0:T(8,128)(2,1)}, u32[]{:S(2)}, u32[]{:S(2)}) collective-permute-start(bf16[144,1024]{1,0:T(8,128)(2,1)} %collective-permute-done.99), channel_id=1, source_target_pairs={{0,1},{1,0},{2,3},{3,2},{4,5},{5,4},{6,7},{7,6},{8,9},{9,8},{10,11... | collective-permute-start | bytes 884744 | tf_op jit(solution)/shard_map/ppermute | solution.py:74
  396.2 59.8 %collective-permute-start.41 = (bf16[512,1024]{1,0:T(8,128)(2,1)}, bf16[512,1024]{1,0:T(8,128)(2,1)}, u32[]{:S(2)}, u32[]{:S(2)}) collective-permute-start(bf16[512,1024]{1,0:T(8,128)(2,1)} %get-tuple-element.95), channel_id=1, source_target_pairs={{0,1},{1,0},{2,3},{3,2},{4,5},{5,4},{6,7},{7,6},{8,9},{9,8},{10,11... | collective-permute-start | bytes 3145736 | tf_op jit(solution)/shard_map/ppermute | solution.py:74
  400.0 14.2 %collective-permute-start.78 = (bf16[128,1152]{1,0:T(8,128)(2,1)}, bf16[128,1152]{1,0:T(8,128)(2,1)}, u32[]{:S(2)}, u32[]{:S(2)}) collective-permute-start(bf16[128,1152]{1,0:T(8,128)(2,1)} %add_convert_fusion.19), channel_id=1, source_target_pairs={{0,1},{1,0},{2,3},{3,2},{4,5},{5,4},{6,7},{7,6},{8,9},{9,8},{10,11... | collective-permute-start | bytes 884744 | tf_op jit(solution)/shard_map/ppermute | solution.py:74
  400.1 16.2 %collective-permute-start.80 = (bf16[128,1152]{1,0:T(8,128)(2,1)}, bf16[128,1152]{1,0:T(8,128)(2,1)}, u32[]{:S(2)}, u32[]{:S(2)}) collective-permute-start(bf16[128,1152]{1,0:T(8,128)(2,1)} %collective-permute-done.79), channel_id=1, source_target_pairs={{0,1},{1,0},{2,3},{3,2},{4,5},{5,4},{6,7},{7,6},{8,9},{9,8},{10,11... | collective-permute-start | bytes 884744 | tf_op jit(solution)/shard_map/ppermute | solution.py:74
  404.6 27.8 %collective-permute-start.47 = (bf16[512,1024]{1,0:T(8,128)(2,1)}, bf16[512,1024]{1,0:T(8,128)(2,1)}, u32[]{:S(2)}, u32[]{:S(2)}) collective-permute-start(bf16[512,1024]{1,0:T(8,128)(2,1)} %get-tuple-element.93), channel_id=1, source_target_pairs={{0,1},{1,0},{2,3},{3,2},{4,5},{5,4},{6,7},{7,6},{8,9},{9,8},{10,11... | collective-permute-start | bytes 3145736 | tf_op jit(solution)/shard_map/ppermute | solution.py:74
  404.6 51.4 %collective-permute-start.43 = (bf16[512,1024]{1,0:T(8,128)(2,1)}, bf16[512,1024]{1,0:T(8,128)(2,1)}, u32[]{:S(2)}, u32[]{:S(2)}) collective-permute-start(bf16[512,1024]{1,0:T(8,128)(2,1)} %fusion.33), channel_id=1, source_target_pairs={{0,2},{2,0},{1,3},{3,1},{4,6},{6,4},{5,7},{7,5},{8,10},{10,8},{9,1... | collective-permute-start | bytes 3145736 | tf_op jit(solution)/shard_map/ppermute | solution.py:78
  414.2 38.7 %collective-permute-start.49 = (bf16[512,1024]{1,0:T(8,128)(2,1)}, bf16[512,1024]{1,0:T(8,128)(2,1)}, u32[]{:S(2)}, u32[]{:S(2)}) collective-permute-start(bf16[512,1024]{1,0:T(8,128)(2,1)} %fusion.31), channel_id=1, source_target_pairs={{0,2},{2,0},{1,3},{3,1},{4,6},{6,4},{5,7},{7,5},{8,10},{10,8},{9,1... | collective-permute-start | bytes 3145736 | tf_op jit(solution)/shard_map/ppermute | solution.py:78
  461.6 21.2 %collective-permute-start.50 = (bf16[512,1024]{1,0:T(8,128)(2,1)}, bf16[512,1024]{1,0:T(8,128)(2,1)}, u32[]{:S(2)}, u32[]{:S(2)}) collective-permute-start(bf16[512,1024]{1,0:T(8,128)(2,1)} %get-tuple-element.53), channel_id=1, source_target_pairs={{0,1},{1,0},{2,3},{3,2},{4,5},{5,4},{6,7},{7,6},{8,9},{9,8},{10,11... | collective-permute-start | bytes 3145736 | tf_op jit(solution)/shard_map/ppermute | solution.py:74
  506.2 23.6 %collective-permute-start.53 = (bf16[128,1536]{1,0:T(8,128)(2,1)}, bf16[128,1536]{1,0:T(8,128)(2,1)}, u32[]{:S(2)}, u32[]{:S(2)}) collective-permute-start(bf16[128,1536]{1,0:T(8,128)(2,1)} %get-tuple-element.70), channel_id=1, source_target_pairs={{0,8},{8,16},{16,24},{24,28},{28,20},{20,12},{12,4},{4,0},{1,9},{9... | collective-permute-start | bytes 1179656 | tf_op jit(solution)/shard_map/ppermute | solution.py:63
  510.7 15.8 %collective-permute-start.64 = (bf16[64,1024]{1,0:T(8,128)(2,1)}, bf16[64,1024]{1,0:T(8,128)(2,1)}, u32[]{:S(2)}, u32[]{:S(2)}) collective-permute-start(bf16[64,1024]{1,0:T(8,128)(2,1)} %get-tuple-element.99), channel_id=1, source_target_pairs={{8,0},{16,8},{24,16},{28,24},{20,28},{12,20},{4,12},{0,4},{9,1},{1... | collective-permute-start | bytes 393224 | tf_op jit(solution)/shard_map/ppermute | solution.py:63
  511.4 15.2 %collective-permute-start.67 = (bf16[64,1024]{1,0:T(8,128)(2,1)}, bf16[64,1024]{1,0:T(8,128)(2,1)}, u32[]{:S(2)}, u32[]{:S(2)}) collective-permute-start(bf16[64,1024]{1,0:T(8,128)(2,1)} %get-tuple-element.100), channel_id=1, source_target_pairs={{0,8},{8,16},{16,24},{24,28},{28,20},{20,12},{12,4},{4,0},{1,9},{9... | collective-permute-start | bytes 393224 | tf_op jit(solution)/shard_map/ppermute | solution.py:67
  525.9 20.7 %collective-permute-start.57 = (bf16[128,1536]{1,0:T(8,128)(2,1)}, bf16[128,1536]{1,0:T(8,128)(2,1)S(1)}, u32[]{:S(2)}, u32[]{:S(2)}) collective-permute-start(bf16[128,1536]{1,0:T(8,128)(2,1)} %get-tuple-element.71), channel_id=1, source_target_pairs={{8,0},{16,8},{24,16},{28,24},{20,28},{12,20},{4,12},{0,4},{9,1},{1... | collective-permute-start | bytes 1179656 | tf_op jit(solution)/shard_map/ppermute | solution.py:67
  531.1 15.5 %collective-permute-start.54 = (bf16[128,1536]{1,0:T(8,128)(2,1)S(1)}, bf16[128,1536]{1,0:T(8,128)(2,1)S(1)}, u32[]{:S(2)}, u32[]{:S(2)}) collective-permute-start(bf16[128,1536]{1,0:T(8,128)(2,1)S(1)} %add_convert_fusion.6), channel_id=1, source_target_pairs={{0,8},{8,16},{16,24},{24,28},{28,20},{20,12},{12,4},{4,0},{1,9},{9... | collective-permute-start | bytes 1179656 | tf_op jit(solution)/shard_map/ppermute | solution.py:63
  545.9 16.1 %collective-permute-start.52 = (bf16[512,1024]{1,0:T(8,128)(2,1)S(1)}, bf16[512,1024]{1,0:T(8,128)(2,1)S(1)}, u32[]{:S(2)}, u32[]{:S(2)}) collective-permute-start(bf16[512,1024]{1,0:T(8,128)(2,1)S(1)} %slice.256), channel_id=1, source_target_pairs={{0,1},{1,0},{2,3},{3,2},{4,5},{5,4},{6,7},{7,6},{8,9},{9,8},{10,11... | collective-permute-start | bytes 3145736 | tf_op jit(solution)/shard_map/ppermute | solution.py:74
  559.7 44.3 %collective-permute-start.56 = (bf16[128,1536]{1,0:T(8,128)(2,1)}, bf16[128,1536]{1,0:T(8,128)(2,1)}, u32[]{:S(2)}, u32[]{:S(2)}) collective-permute-start(bf16[128,1536]{1,0:T(8,128)(2,1)} %get-tuple-element.66), channel_id=1, source_target_pairs={{0,8},{8,16},{16,24},{24,28},{28,20},{20,12},{12,4},{4,0},{1,9},{9... | collective-permute-start | bytes 1179656 | tf_op jit(solution)/shard_map/ppermute | solution.py:63
  561.1 42.9 %collective-permute-start.59 = (bf16[128,1536]{1,0:T(8,128)(2,1)}, bf16[128,1536]{1,0:T(8,128)(2,1)}, u32[]{:S(2)}, u32[]{:S(2)}) collective-permute-start(bf16[128,1536]{1,0:T(8,128)(2,1)} %get-tuple-element.67), channel_id=1, source_target_pairs={{8,0},{16,8},{24,16},{28,24},{20,28},{12,20},{4,12},{0,4},{9,1},{1... | collective-permute-start | bytes 1179656 | tf_op jit(solution)/shard_map/ppermute | solution.py:67
  (162 other events, 1946.0 us)

commit v2 on v1

--- a/solution.py
+++ b/solution.py
@@ -1,6 +1,10 @@
+import functools
+
 import jax
 import jax.numpy as jnp
 from jax import lax
+from jax.experimental import pallas as pl
+from jax.experimental.pallas import tpu as pltpu
 from jax.sharding import Mesh, PartitionSpec as P
 
 epsilon = 1e-05
@@ -91,6 +95,31 @@
     received = over_y(other.astype(jnp.bfloat16)).astype(jnp.float32)
     near = over_core(beside.astype(jnp.bfloat16)).astype(jnp.float32)
     return mine + near + received
+
+
+def lay_out_kernel(groups, member_ref, parts_ref, out_ref):
+    member = member_ref[0]
+    size = parts_ref.shape[2] // groups
+    for place in range(4):
+        part = parts_ref[jnp.bitwise_xor(place, member)].astype(jnp.float32)
+        for group in range(groups):
+            start = (group * 4 + place) * size
+            out_ref[:, start : start + size] = part[:, group * size : (group + 1) * size]
+
+
+def lay_out(parts, member, groups):
+    rows, columns = parts.shape[1:]
+    return pl.pallas_call(
+        functools.partial(lay_out_kernel, groups),
+        out_shape=jax.ShapeDtypeStruct((rows, 4 * columns), jnp.float32),
+        in_specs=[
+            pl.BlockSpec(memory_space=pltpu.SMEM),
+            pl.BlockSpec(memory_space=pltpu.VMEM),
+        ],
+        out_specs=pl.BlockSpec(memory_space=pltpu.VMEM),
+        compiler_params=pltpu.CompilerParams(vmem_limit_bytes=32 * 2**20),
+        cost_estimate=pl.CostEstimate(flops=0, bytes_accessed=24 * rows * columns, transcendentals=0),
+    )(member[None], parts)
 
 
 def outer_sum(left, right):
@@ -138,21 +167,29 @@
     hidden_rows = down_weight.shape[0]
 
     small = jnp.concatenate([mix_gain[None], ffn_gain[None], conv_taps], 0)
-    small_full = lax.all_gather(small, "shard", axis=1, tiled=True)
+    own = small.shape[1]
     in_mine = jnp.concatenate(
         [picked(in_weight[:, i * width : (i + 1) * width], shards, 2, core) for i in range(3)], 1
     )
     out_rows = out_weight.shape[0] // 2
     out_mine = lax.dynamic_slice(out_weight, (core * out_rows, 0), (out_rows, width))
-    gate_mine = picked(gate_weight, shards, 4, member)
-    up_mine = picked(up_weight, shards, 4, member)
+    out_mine = jnp.concatenate([out_mine[:, :half], out_mine[:, half:]], 0)
+    small_rows = jnp.pad(small, ((0, 11), (0, 4 * half - own)))
+    mix_mine = jnp.concatenate([jnp.concatenate([in_mine, out_mine], 1), small_rows], 0)
+    mix_full = ring_gather(mix_mine).reshape(shards, own + 16, 4 * half)
+    in_full = mix_full[:, :own, : 3 * half].reshape(width, 3 * half)
+    out_full = mix_full[:, :own, 3 * half :].reshape(shards, 2, out_rows, half)
+    out_full = out_full.transpose(0, 2, 1, 3).reshape(half, width)
+    small_full = mix_full[:, own : own + 5, :own].transpose(1, 0, 2).reshape(5, width)
+
+    quarter = hidden_rows * shards // 4
+    both_mine = jnp.concatenate(
+        [picked(gate_weight, shards, 4, member), picked(up_weight, shards, 4, member)], 1
+    )
     down_rows = hidden_rows // 4
     down_mine = lax.dynamic_slice(down_weight, (member * down_rows, 0), (down_rows, width))
-    in_full = ring_gather(in_mine)
-    out_full = ring_gather(out_mine, True)
-    gate_full = ring_gather(gate_mine, True)
-    up_full = ring_gather(up_mine)
-    down_full = ring_gather(down_mine, True)
+    both_full = ring_gather(both_mine, True)
+    down_full = ring_gather(down_mine)
 
     params = small_full.astype(jnp.float32)
     gain_one = params[0]
@@ -161,11 +198,11 @@
         params[2:5].reshape(3, shards, 2, half // shards), core, 2, keepdims=False
     ).reshape(3, half)
 
-    inputs = tokens[0].astype(jnp.float32)
-    factor_one = lax.rsqrt(jnp.mean(inputs * inputs, axis=-1, keepdims=True) + epsilon)
-    unit_one = inputs * factor_one
-    normed_own = (unit_one * gain_one).astype(jnp.bfloat16)
-    normed = jnp.concatenate([normed_own, over_core(normed_own)], 0)
+    pair = jnp.concatenate([tokens[0], over_core(tokens[0])], 0).astype(jnp.float32)
+    factor_pair = lax.rsqrt(jnp.mean(pair * pair, axis=-1, keepdims=True) + epsilon)
+    unit_pair = pair * factor_pair
+    normed = (unit_pair * gain_one).astype(jnp.bfloat16)
+    inputs, factor_one, unit_one = pair[:length], factor_pair[:length], unit_pair[:length]
     mixed = times(normed, in_full)
     b_part = mixed[:, :half].reshape(2, length, half)
     c_part = mixed[:, half : 2 * half].reshape(2, length, half)
@@ -190,18 +227,19 @@
     unit_two = resid * factor_two
     hnorm = four_gather((unit_two * gain_two).astype(jnp.bfloat16))
     grad_rows = four_gather(cotangent[0])
-    gate = times(hnorm, gate_full)
-    upper = times(hnorm, up_full)
+    mid = times(hnorm, both_full)
+    gate = mid[:, :quarter]
+    upper = mid[:, quarter:]
     sigma = jax.nn.sigmoid(gate)
     activated = gate * sigma
     hidden = (activated * upper).astype(jnp.bfloat16)
     d_hidden = times_transposed(grad_rows, down_full)
     d_gate = (d_hidden * upper * sigma * (1.0 + gate * (1.0 - sigma))).astype(jnp.bfloat16)
     d_up = (d_hidden * activated).astype(jnp.bfloat16)
-    d_hnorm = four_scatter(times_transposed(d_gate, gate_full) + times_transposed(d_up, up_full))
+    d_both = jnp.concatenate([d_gate, d_up], 1)
+    d_hnorm = four_scatter(times_transposed(d_both, both_full))
     g_down = ring_scatter(outer_sum(hidden, grad_rows))
-    g_gate = ring_scatter(outer_sum(hnorm, d_gate), True)
-    g_up = ring_scatter(outer_sum(hnorm, d_up))
+    g_both = ring_scatter(outer_sum(hnorm, d_both), True)
     output = (resid + four_scatter(times(hidden, down_full))).astype(jnp.bfloat16)
 
     g_ffn_gain = jnp.sum(d_hnorm * unit_two, axis=0)
@@ -213,7 +251,7 @@
     d_own = d_resid.astype(jnp.bfloat16)
     d_branch = jnp.concatenate([d_own, over_core(d_own)], 0)
     d_gated = times_transposed(d_branch, out_full).reshape(2, length, half)
-    g_out = ring_scatter(outer_sum(gated, d_branch), True)
+    g_out = outer_sum(gated, d_branch)
     d_cpart = d_gated * conv
     d_conv = d_gated * c_part
     tap_grads = jnp.stack(
@@ -232,56 +270,78 @@
         .reshape(2 * length, 3 * half)
     )
     d_normed = times_transposed(d_mixed, in_full)
-    g_in = ring_scatter(outer_sum(normed, d_mixed))
-    d_normed = d_normed[:length] + over_core(d_normed[length:].astype(jnp.bfloat16)).astype(
-        jnp.float32
-    )
-    g_mix_gain = jnp.sum(d_normed * unit_one, axis=0)
-    scaled_one = d_normed * gain_one
-    d_inputs = d_resid + factor_one * (
-        scaled_one - unit_one * jnp.mean(scaled_one * unit_one, axis=-1, keepdims=True)
-    )
-
-    def summed(value):
-        return lax.psum(value, "outer") if lax.axis_size("outer") > 1 else value
-
-    def four_parts(value):
-        rows = value.shape[0]
-        found = four_gather(summed(value).astype(jnp.bfloat16)).reshape(4, rows, value.shape[1])
-        y_bit, c_bit = member // 2, core
-        found = jnp.where(c_bit == 1, found[jnp.array([1, 0, 3, 2])], found)
-        return jnp.where(y_bit == 1, found[jnp.array([2, 3, 0, 1])], found)
-
-    def spread_four(value):
-        rows = value.shape[0]
-        parts = four_parts(value).reshape(4, rows, shards, down_rows)
-        return parts.transpose(1, 2, 0, 3).reshape(rows, -1).astype(jnp.float32)
-
-    def two_parts(value):
-        mine = summed(value).astype(jnp.bfloat16)
-        mine = (mine.astype(jnp.float32) + over_y(mine).astype(jnp.float32)).astype(jnp.bfloat16)
-        other = over_core(mine)
-        return jnp.where(core == 0, jnp.stack([mine, other]), jnp.stack([other, mine]))
-
-    owned_in = two_parts(g_in).reshape(2, -1, 3, shards, half // shards)
-    owned_in = owned_in.transpose(1, 2, 3, 0, 4).reshape(-1, 3 * width).astype(jnp.float32)
-    owned_out = two_parts(g_out).reshape(-1, width).astype(jnp.float32)
-    owned_down = four_parts(g_down).reshape(-1, width).astype(jnp.float32)
+    g_in = outer_sum(normed, d_mixed)
+    g_mix_gain = jnp.sum(d_normed * unit_pair, axis=0)
     spot = lax.broadcasted_iota(jnp.int32, (3, shards, 2, half // shards), 2)
     tap_full = jnp.where(
         spot == core, tap_grads.reshape(3, shards, 1, half // shards), 0.0
     ).reshape(3, width)
     small_grads = jnp.concatenate([g_mix_gain[None], g_ffn_gain[None], tap_full], 0)
-    small_grads = lax.psum(small_grads, ("shard", "outer", "y", "core"))
-    own = width // shards
-    small_owned = lax.dynamic_slice(small_grads, (0, lax.axis_index("shard") * own), (5, own))
+    small_grads = jnp.pad(
+        small_grads.reshape(5, shards, own).transpose(1, 0, 2),
+        ((0, 0), (0, 11), (0, 4 * half - own)),
+    )
+    g_out = g_out.reshape(shards, out_rows, 2, half).transpose(0, 2, 1, 3)
+    g_mix = jnp.concatenate(
+        [g_in.reshape(shards, own, 3 * half), g_out.reshape(shards, own, half)], 2
+    )
+    g_mix = jnp.concatenate([g_mix, small_grads], 1).reshape(shards * (own + 16), 4 * half)
+    g_mix = ring_scatter(g_mix)
+    d_normed = d_normed[:length] + over_core(d_normed[length:].astype(jnp.bfloat16)).astype(
+        jnp.float32
+    )
+    scaled_one = d_normed * gain_one
+    d_inputs = d_resid + factor_one * (
+        scaled_one - unit_one * jnp.mean(scaled_one * unit_one, axis=-1, keepdims=True)
+    )
+
+    def summed(value):
+        return lax.psum(value, "outer") if lax.axis_size("outer") > 1 else value
+
+    def four_parts(value):
+        found = four_gather(summed(value).astype(jnp.bfloat16))
+        return found.reshape(4, value.shape[0], value.shape[1])
+
+    both_parts = four_parts(g_both)
+    owned_gate = lay_out(both_parts[:, :, :quarter], member, shards)
+    owned_up = lay_out(both_parts[:, :, quarter:], member, shards)
+    down_parts = four_parts(g_down)
+    owned_down = jnp.concatenate(
+        [
+            lax.dynamic_index_in_dim(down_parts, jnp.bitwise_xor(i, member), 0, keepdims=False)
+            for i in range(4)
+        ],
+        0,
+    ).astype(jnp.float32)
+
+    mix_mine = summed(g_mix).astype(jnp.bfloat16)
+    mix_mine = mix_mine.astype(jnp.float32) + over_y(mix_mine).astype(jnp.float32)
+    mix_mine = mix_mine.astype(jnp.bfloat16)
+    mix_other = over_core(mix_mine)
+    low = jnp.where(core == 0, mix_mine, mix_other)
+    high = jnp.where(core == 0, mix_other, mix_mine)
+    size = half // shards
+    owned_in = jnp.stack(
+        [value[:own, : 3 * half].reshape(own, 3 * shards, size) for value in (low, high)], 2
+    )
+    owned_in = owned_in.reshape(own, 3 * width).astype(jnp.float32)
+    owned_out = jnp.concatenate(
+        [
+            jnp.concatenate([value[:out_rows, 3 * half :], value[out_rows:own, 3 * half :]], 1)
+            for value in (low, high)
+        ],
+        0,
+    ).astype(jnp.float32)
+    small_owned = low[own : own + 5, :own].astype(jnp.float32) + high[own : own + 5, :own].astype(
+        jnp.float32
+    )
     return (
         output[None],
         d_inputs.astype(jnp.bfloat16)[None],
         owned_in,
         owned_out,
-        spread_four(g_gate),
-        spread_four(g_up),
+        owned_gate,
+        owned_up,
         owned_down,
         small_owned[0],
         small_owned[1],

time: 633 us -> 494 us (0.78)
  blocking collectives: 66.6 us -> 0 us
  waiting for transfers between devices: 169 us -> 126 us
  local copies, waits for them, and re-layouts: 101 us -> 86 us
  starting transfers between devices: 83.1 us -> 69.2 us
  other arithmetic: 53 us -> 60.8 us
    psum x1 -> x0, blocking collectives: 40.3 us -> none  [local(): small_grads = lax.psum(small_grads, ('shard', 'outer', 'y', 'core'))]
    ppermute x20 -> x12, waiting for transfers between devices: 57 us -> 21.2 us  [ring_gather(): one = lax.ppermute(one, 'shard', ahead)]
    all_gather x1 -> x0, blocking collectives: 26.2 us -> none  [local(): small_full = lax.all_gather(small, 'shard', axis=1, tiled=True)]
    gather x10 -> x0, local copies, waits for them, and re-layouts: 25.7 us -> none  [the longest x5 13 us: four_parts(): return jnp.where(y_bit == 1, found[jnp.array([2, 3, 0, 1])], found)]
    ppermute x20 -> x12, waiting for transfers between devices: 45.8 us -> 21.8 us  [ring_scatter(): one = lax.ppermute(one, 'shard', ahead)]
    ppermute x9 -> x7, waiting for transfers between devices: 43.3 us -> 20.9 us  [over_y(): return lax.ppermute(value, 'y', PAIR)]
    ppermute x15 -> x9, waiting for transfers between devices: 14 us -> 33.5 us  [ring_gather(): two = lax.ppermute(two, 'shard', back)]
    ppermute x15 -> x9, waiting for transfers between devices: 8.67 us -> 27.5 us  [ring_scatter(): two = lax.ppermute(two, 'shard', back)]
  transfers between devices with their start and end apart: 101 -> 68, of which waited for: 39 -> 21; matrix products, arithmetic and copies ran while one was open for 32% -> 42% of each run, Pallas kernels for 0% -> 1%
where the time goes in v2:
time: 494 us; the launch traced here: 486 us
  waiting for transfers between devices  126 us (26%)
  matrix products  119 us (24%)
  local copies, waits for them, and re-layouts  86 us (17%)
  starting transfers between devices  69.2 us (14%)
  other arithmetic  60.8 us (12%)
  between operations  21.4 us (4%)
    dot_general x9, matrix products, times(): return jnp.dot(value, weight, preferred_element_type=jnp.float32)  43 us
    dot_general x4, matrix products, times_transposed(): lax.dot_general(grad, weight, (((1,), (1,)), ((), ())), preferred_element...  41.1 us
    dot_general x4, matrix products, outer_sum(): lax.dot_general(left, right, (((0,), (0,)), ((), ())), preferred_element_...  34.6 us
    ppermute x9, waiting for transfers between devices, ring_gather(): two = lax.ppermute(two, 'shard', back)  33.5 us
    ppermute x9, waiting for transfers between devices, ring_scatter(): two = lax.ppermute(two, 'shard', back)  27.5 us
    ppermute x12, waiting for transfers between devices, ring_scatter(): one = lax.ppermute(one, 'shard', ahead)  21.8 us
    ppermute x12, waiting for transfers between devices, ring_gather(): one = lax.ppermute(one, 'shard', ahead)  21.2 us
    ppermute x7, waiting for transfers between devices, over_y(): return lax.ppermute(value, 'y', PAIR)  20.9 us
  transfers between devices with their start and end apart: 68, of which 21 were waited for; matrix products, arithmetic and copies ran while one was open for 42% of the time, Pallas kernels for 1%

profile of v2, /device:TPU:0, one launch (start us, length us, event | category | flops | bytes accessed | tf_op | source)
XLA Modules:
  0.0 486.2 jit_solution(10353436316315856813)
XLA Ops:
  5.5 3.0 collective-permute-start.1
  14.2 4.1 fusion.16
  18.3 3.5 fusion.19
  25.7 2.8 broadcast_in_dim.47
  61.8 14.9 %collective-permute-done.4 = bf16[144,2048]{1,0:T(8,128)(2,1)S(1)} collective-permute-done((bf16[144,2048]{1,0:T(8,128)(2,1)}, bf16[144,2048]{1,0:T(8,128)(2,1)S(1)}, u32[]{:S(2)}, u32[]{:S(2)}) %collective-permute-start.4) | collective-permute-done | bytes 589856 | tf_op jit(solution)/shard_map/ppermute | solution.py:46
  81.8 9.6 %collective-permute-done.6 = bf16[144,2048]{1,0:T(8,128)(2,1)S(1)} collective-permute-done((bf16[144,2048]{1,0:T(8,128)(2,1)S(1)}, bf16[144,2048]{1,0:T(8,128)(2,1)S(1)}, u32[]{:S(2)}, u32[]{:S(2)}) %collective-permute-start.6) | collective-permute-done | bytes 589856 | tf_op jit(solution)/shard_map/ppermute | solution.py:46
  101.2 3.5 fusion.40
  108.7 3.1 collective-permute-start.8
  115.3 2.4 copy.190
  133.9 6.2 %collective-permute-done.25 = bf16[144,1024]{1,0:T(8,128)(2,1)S(1)} collective-permute-done((bf16[144,1024]{1,0:T(8,128)(2,1)}, bf16[144,1024]{1,0:T(8,128)(2,1)S(1)}, u32[]{:S(2)}, u32[]{:S(2)}) %collective-permute-start.25) | collective-permute-done | bytes 294944 | tf_op jit(solution)/shard_map/ppermute | solution.py:46
  143.4 6.6 %collective-permute-done.26 = bf16[144,1024]{1,0:T(8,128)(2,1)S(1)} collective-permute-done((bf16[144,1024]{1,0:T(8,128)(2,1)S(1)}, bf16[144,1024]{1,0:T(8,128)(2,1)S(1)}, u32[]{:S(2)}, u32[]{:S(2)}) %collective-permute-start.26) | collective-permute-done | bytes 294944 | tf_op jit(solution)/shard_map/ppermute | solution.py:43
  150.7 5.0 %collective-permute-done.17 = bf16[128,2304]{0,1:T(8,128)(2,1)S(1)} collective-permute-done((bf16[128,2304]{0,1:T(8,128)(2,1)S(1)}, bf16[128,2304]{0,1:T(8,128)(2,1)S(1)}, u32[]{:S(2)}, u32[]{:S(2)}) %collective-permute-start.17) | collective-permute-done | bytes 589856 | tf_op jit(solution)/shard_map/ppermute | solution.py:43
  158.6 2.8 collective-permute-done.18
  161.6 8.3 %collective-permute-done.19 = bf16[128,2304]{0,1:T(8,128)(2,1)S(1)} collective-permute-done((bf16[128,2304]{0,1:T(8,128)(2,1)S(1)}, bf16[128,2304]{0,1:T(8,128)(2,1)S(1)}, u32[]{:S(2)}, u32[]{:S(2)}) %collective-permute-start.19) | collective-permute-done | bytes 589856 | tf_op jit(solution)/shard_map/ppermute | solution.py:43
  171.2 17.9 %fusion.43 = f32[2048,2304]{1,0:T(8,128)} fusion(bf16[1024,2304]{0,1:T(8,128)(2,1)S(1)} %constant_dynamic-update-slice_fusion.7, bf16[512,1024]{1,0:T(8,128)(2,1)} %collective-permute-done.12, bf16[512,1024]{1,0:T(8,128)(2,1)} %copy-done.57, bf16[512,1024]{1,0:T(8,128)(2,1)} %copy-done.58, bf16[512,1024]{1,0:T(8,128)(2,1)} %copy-done.37), kind=kOutput, calls=%fused_computation.107 | convolution fusion | flops 9680453632 | bytes 27787264 | tf_op jit(solution)/shard_map/dot_general | solution.py:138
  189.1 18.5 %multiply_convert_fusion.1 = (bf16[2048,1152]{1,0:T(8,128)(2,1)}, bf16[2048,1152]{1,0:T(8,128)(2,1)}, bf16[2048,1152]{1,0:T(8,128)(2,1)}) fusion(f32[2048,2304]{1,0:T(8,128)} %fusion.43, bf16[1152,1024]{1,0:T(8,128)(2,1)} %constant_dynamic-update-slice_fusion.5, bf16[512,1024]{1,0:T(8,128)(2,1)} %collective-permute-done.32, ...), kind=kOutput, calls=%fused_computation.6 | convolution fusion | flops 4884004864 | bytes 39583744 | tf_op jit(solution)/shard_map/dot_general | solution.py:132
  207.6 16.2 %fusion.93 = (bf16[2048,1024]{1,0:T(8,128)(2,1)S(1)}, f32[2048,1024]{1,0:T(8,128)}) fusion(bf16[1024,2304]{0,1:T(8,128)(2,1)} %copy-done.23, bf16[2048,1152]{1,0:T(8,128)(2,1)} %get-tuple-element.72, bf16[2048,1152]{1,0:T(8,128)(2,1)} %get-tuple-element.71), kind=kOutput, calls=%fused_computation.221 | convolution fusion | flops 9684647936 | bytes 26738688 | tf_op jit(solution)/shard_map/dot_general | solution.py:132
  225.8 10.3 %fusion.94 = (bf16[2048,1024]{1,0:T(8,128)(2,1)S(1)}, f32[2048,1024]{1,0:T(8,128)}) fusion(bf16[2048,1152]{1,0:T(8,128)(2,1)} %get-tuple-element.73, bf16[1152,1024]{1,0:T(8,128)(2,1)} %constant_dynamic-update-slice_fusion.5), kind=kOutput, calls=%fused_computation.222 | convolution fusion | flops 4833935360 | bytes 19660800 | tf_op jit(solution)/shard_map/dot_general | solution.py:138
  238.1 7.3 %fusion.41 = f32[1152,1024]{1,0:T(8,128)S(1)} fusion(bf16[2048,1152]{1,0:T(8,128)(2,1)S(1)} %bitcast.180, bf16[512,1024]{1,0:T(8,128)(2,1)} %collective-permute-done.32, bf16[512,1024]{1,0:T(8,128)(2,1)} %collective-permute-done.31, bf16[512,1024]{1,0:T(8,128)(2,1)} %collective-permute-done.30, bf16[512,1024]{1,0:T(8,128)(2,1)} %bitcast.42), kind=kOutput, calls=%fused_computation.105 | convolution fusion | flops 4848615424 | bytes 13631488 | tf_op jit(solution)/shard_map/dot_general | solution.py:126
  247.1 17.2 %fusion.6 = f32[1024,2304]{1,0:T(8,128)} fusion(bf16[2048,1152]{1,0:T(8,128)(2,1)} %get-tuple-element.72, bf16[2048,1152]{1,0:T(8,128)(2,1)} %get-tuple-element.71, bf16[512,1024]{1,0:T(8,128)(2,1)} %collective-permute-done.12, bf16[512,1024]{1,0:T(8,128)(2,1)} %copy-done.57, bf16[512,1024]{1,0:T(8,128)(2,1)} %copy-done.58, bf16[512,1024]{1,0:T(8,128)(2,1)S(1)} %copy-done.38), kind=kOutput, calls=%fused_computation.12 | convolution fusion | flops 9699328000 | bytes 23068672 | tf_op jit(solution)/shard_map/dot_general | solution.py:126
  264.2 2.7 dynamic-slice_convert_fusion.1
  277.2 11.4 %collective-permute-done.62 = bf16[144,1024]{1,0:T(8,128)(2,1)S(1)} collective-permute-done((bf16[144,1024]{1,0:T(8,128)(2,1)}, bf16[144,1024]{1,0:T(8,128)(2,1)S(1)}, u32[]{:S(2)}, u32[]{:S(2)}) %collective-permute-start.62) | collective-permute-done | bytes 294944 | tf_op jit(solution)/shard_map/ppermute | solution.py:71
  292.9 3.9 collective-permute-done.59
  302.8 17.4 %collective-permute-done.29 = bf16[512,1024]{1,0:T(8,128)(2,1)S(1)} collective-permute-done((bf16[512,1024]{1,0:T(8,128)(2,1)S(1)}, bf16[512,1024]{1,0:T(8,128)(2,1)S(1)}, u32[]{:S(2)}, u32[]{:S(2)}) %collective-permute-start.29) | collective-permute-done | bytes 1048608 | tf_op jit(solution)/shard_map/ppermute | solution.py:82
  320.1 4.3 fusion.83
  327.3 2.4 add_convert_fusion.17
  331.7 3.4 add_convert_fusion.7
  337.2 3.1 fusion.82
  340.3 2.9 multiply_reduce_fusion.4
  347.8 4.0 copy.212
  351.8 4.3 fusion.96
  362.4 3.4 fusion.32
  365.9 4.6 fusion.39
  370.5 2.5 copy.211
  373.1 5.7 %fusion.8 = f32[8,128,1536]{2,1,0:T(8,128)S(1)} fusion(bf16[8,128,1024]{2,1,0:T(8,128)(2,1)} %bitcast.157, bf16[1024,512]{1,0:T(8,128)(2,1)} %bitcast.165, bf16[1024,512]{1,0:T(8,128)(2,1)} %bitcast.177, bf16[1024,512]{1,0:T(8,128)(2,1)S(1)} %bitcast.163), kind=kOutput, calls=%fused_computation.20 | convolution fusion | flops 3230662656 | bytes 11534336 | tf_op jit(solution)/shard_map/dot_general | solution.py:126
  380.3 2.5 collective-permute-start.39
  382.8 2.6 add_convert_fusion.6
  385.4 2.6 collective-permute-start.54
  392.9 4.4 collective-permute-done.39
  399.3 10.6 %collective-permute-done.54 = bf16[128,2304]{1,0:T(8,128)(2,1)S(1)} collective-permute-done((bf16[128,2304]{1,0:T(8,128)(2,1)S(1)}, bf16[128,2304]{1,0:T(8,128)(2,1)S(1)}, u32[]{:S(2)}, u32[]{:S(2)}) %collective-permute-start.54) | collective-permute-done | bytes 589856 | tf_op jit(solution)/shard_map/ppermute | solution.py:71
  414.8 6.1 %collective-permute-done.40 = bf16[144,2048]{1,0:T(8,128)(2,1)S(1)} collective-permute-done((bf16[144,2048]{1,0:T(8,128)(2,1)S(1)}, bf16[144,2048]{1,0:T(8,128)(2,1)S(1)}, u32[]{:S(2)}, u32[]{:S(2)}) %collective-permute-start.40) | collective-permute-done | bytes 589856 | tf_op jit(solution)/shard_map/ppermute | solution.py:67
  428.6 7.5 %collective-permute-done.41 = bf16[144,2048]{1,0:T(8,128)(2,1)} collective-permute-done((bf16[144,2048]{1,0:T(8,128)(2,1)}, bf16[144,2048]{1,0:T(8,128)(2,1)}, u32[]{:S(2)}, u32[]{:S(2)}) %collective-permute-start.41) | collective-permute-done | bytes 589856 | tf_op jit(solution)/shard_map/ppermute | solution.py:67
  436.9 3.9 add_convert_fusion.11
  444.6 2.7 slice.368
  450.3 2.9 collective-permute-done.45
  457.6 2.5 add_convert_fusion.1
  469.8 3.6 collective-permute-done.46
  475.6 4.7 fusion.37
  (392 shorter events, 169.0 us)
Async XLA Ops:
  5.5 18.1 %collective-permute-start.1 = (bf16[144,2048]{1,0:T(8,128)(2,1)}, bf16[144,2048]{1,0:T(8,128)(2,1)}, u32[]{:S(2)}, u32[]{:S(2)}) collective-permute-start(bf16[144,2048]{1,0:T(8,128)(2,1)} %copy.186), channel_id=1, source_target_pairs={{0,8},{8,16},{16,24},{24,28},{28,20},{20,12},{12,4},{4,0},{1,9},{9... | collective-permute-start | bytes 1769480 | tf_op jit(solution)/shard_map/ppermute | solution.py:43
  8.5 45.3 %collective-permute-start.2 = (bf16[144,2048]{1,0:T(8,128)(2,1)}, bf16[144,2048]{1,0:T(8,128)(2,1)}, u32[]{:S(2)}, u32[]{:S(2)}) collective-permute-start(bf16[144,2048]{1,0:T(8,128)(2,1)} %copy.186), channel_id=1, source_target_pairs={{8,0},{16,8},{24,16},{28,24},{20,28},{12,20},{4,12},{0,4},{9,1},{1... | collective-permute-start | bytes 1769480 | tf_op jit(solution)/shard_map/ppermute | solution.py:46
  12.1 36.2 %collective-permute-start.20 = (bf16[144,1024]{1,0:T(8,128)(2,1)}, bf16[144,1024]{1,0:T(8,128)(2,1)}, u32[]{:S(2)}, u32[]{:S(2)}) collective-permute-start(bf16[144,1024]{1,0:T(8,128)(2,1)} %get-tuple-element.66), channel_id=1, source_target_pairs={{0,8},{8,16},{16,24},{24,28},{28,20},{20,12},{12,4},{4,0},{1,9},{9... | collective-permute-start | bytes 884744 | tf_op jit(solution)/shard_map/ppermute | solution.py:43
  14.1 36.7 %collective-permute-start.21 = (bf16[144,1024]{1,0:T(8,128)(2,1)}, bf16[144,1024]{1,0:T(8,128)(2,1)}, u32[]{:S(2)}, u32[]{:S(2)}) collective-permute-start(bf16[144,1024]{1,0:T(8,128)(2,1)} %get-tuple-element.66), channel_id=1, source_target_pairs={{8,0},{16,8},{24,16},{28,24},{20,28},{12,20},{4,12},{0,4},{9,1},{1... | collective-permute-start | bytes 884744 | tf_op jit(solution)/shard_map/ppermute | solution.py:46
  14.1 45.7 %collective-permute-start = (bf16[512,1024]{1,0:T(8,128)(2,1)S(1)}, bf16[512,1024]{1,0:T(8,128)(2,1)S(1)}, u32[]{:S(2)}, u32[]{:S(2)}) collective-permute-start(bf16[512,1024]{1,0:T(8,128)(2,1)S(1)} %bitcast.136), channel_id=1, source_target_pairs={{0,1},{1,0},{2,3},{3,2},{4,5},{5,4},{6,7},{7,6},{8,9},{9,8},{10,11... | collective-permute-start | bytes 3145736 | tf_op jit(solution)/shard_map/ppermute | solution.py:78
  23.6 32.8 %collective-permute-start.3 = (bf16[144,2048]{1,0:T(8,128)(2,1)}, bf16[144,2048]{1,0:T(8,128)(2,1)S(1)}, u32[]{:S(2)}, u32[]{:S(2)}) collective-permute-start(bf16[144,2048]{1,0:T(8,128)(2,1)} %collective-permute-done.1), channel_id=1, source_target_pairs={{0,8},{8,16},{16,24},{24,28},{28,20},{20,12},{12,4},{4,0},{1,9},{9... | collective-permute-start | bytes 1769480 | tf_op jit(solution)/shard_map/ppermute | solution.py:43
  48.3 69.7 %collective-permute-start.13 = (bf16[128,2304]{0,1:T(8,128)(2,1)}, bf16[128,2304]{0,1:T(8,128)(2,1)}, u32[]{:S(2)}, u32[]{:S(2)}) collective-permute-start(bf16[128,2304]{0,1:T(8,128)(2,1)} %get-tuple-element.124), channel_id=1, source_target_pairs={{8,0},{16,8},{24,16},{28,24},{20,28},{12,20},{4,12},{0,4},{9,1},{1... | collective-permute-start | bytes 1769480 | tf_op jit(solution)/shard_map/ppermute | solution.py:43
  50.8 68.9 %collective-permute-start.14 = (bf16[128,2304]{0,1:T(8,128)(2,1)}, bf16[128,2304]{0,1:T(8,128)(2,1)}, u32[]{:S(2)}, u32[]{:S(2)}) collective-permute-start(bf16[128,2304]{0,1:T(8,128)(2,1)} %get-tuple-element.124), channel_id=1, source_target_pairs={{0,8},{8,16},{16,24},{24,28},{28,20},{20,12},{12,4},{4,0},{1,9},{9... | collective-permute-start | bytes 1769480 | tf_op jit(solution)/shard_map/ppermute | solution.py:46
  53.8 22.9 %collective-permute-start.4 = (bf16[144,2048]{1,0:T(8,128)(2,1)}, bf16[144,2048]{1,0:T(8,128)(2,1)S(1)}, u32[]{:S(2)}, u32[]{:S(2)}) collective-permute-start(bf16[144,2048]{1,0:T(8,128)(2,1)} %collective-permute-done.2), channel_id=1, source_target_pairs={{8,0},{16,8},{24,16},{28,24},{20,28},{12,20},{4,12},{0,4},{9,1},{1... | collective-permute-start | bytes 1769480 | tf_op jit(solution)/shard_map/ppermute | solution.py:46
  56.4 22.6 %collective-permute-start.5 = (bf16[144,2048]{1,0:T(8,128)(2,1)S(1)}, bf16[144,2048]{1,0:T(8,128)(2,1)S(1)}, u32[]{:S(2)}, u32[]{:S(2)}) collective-permute-start(bf16[144,2048]{1,0:T(8,128)(2,1)S(1)} %collective-permute-done.3), channel_id=1, source_target_pairs={{0,8},{8,16},{16,24},{24,28},{28,20},{20,12},{12,4},{4,0},{1,9},{9... | collective-permute-start | bytes 1769480 | tf_op jit(solution)/shard_map/ppermute | solution.py:43
  59.8 98.7 %collective-permute-start.31 = (bf16[512,1024]{1,0:T(8,128)(2,1)}, bf16[512,1024]{1,0:T(8,128)(2,1)}, u32[]{:S(2)}, u32[]{:S(2)}) collective-permute-start(bf16[512,1024]{1,0:T(8,128)(2,1)} %bitcast.42), channel_id=1, source_target_pairs={{0,2},{2,0},{1,3},{3,1},{4,6},{6,4},{5,7},{7,5},{8,10},{10,8},{9,1... | collective-permute-start | bytes 3145736 | tf_op jit(solution)/shard_map/ppermute | solution.py:82
  79.0 15.6 %collective-permute-start.7 = (bf16[144,2048]{1,0:T(8,128)(2,1)S(1)}, bf16[144,2048]{1,0:T(8,128)(2,1)S(1)}, u32[]{:S(2)}, u32[]{:S(2)}) collective-permute-start(bf16[144,2048]{1,0:T(8,128)(2,1)S(1)} %collective-permute-done.5), channel_id=1, source_target_pairs={{0,8},{8,16},{16,24},{24,28},{28,20},{20,12},{12,4},{4,0},{1,9},{9... | collective-permute-start | bytes 1769480 | tf_op jit(solution)/shard_map/ppermute | solution.py:43
  91.4 17.3 %collective-permute-start.22 = (bf16[144,1024]{1,0:T(8,128)(2,1)}, bf16[144,1024]{1,0:T(8,128)(2,1)S(1)}, u32[]{:S(2)}, u32[]{:S(2)}) collective-permute-start(bf16[144,1024]{1,0:T(8,128)(2,1)} %collective-permute-done.20), channel_id=1, source_target_pairs={{0,8},{8,16},{16,24},{24,28},{28,20},{20,12},{12,4},{4,0},{1,9},{9... | collective-permute-start | bytes 884744 | tf_op jit(solution)/shard_map/ppermute | solution.py:43
  94.6 31.0 %collective-permute-start.23 = (bf16[144,1024]{1,0:T(8,128)(2,1)}, bf16[144,1024]{1,0:T(8,128)(2,1)}, u32[]{:S(2)}, u32[]{:S(2)}) collective-permute-start(bf16[144,1024]{1,0:T(8,128)(2,1)} %collective-permute-done.21), channel_id=1, source_target_pairs={{8,0},{16,8},{24,16},{28,24},{20,28},{12,20},{4,12},{0,4},{9,1},{1... | collective-permute-start | bytes 884744 | tf_op jit(solution)/shard_map/ppermute | solution.py:46
  119.7 21.2 %collective-permute-start.15 = (bf16[128,2304]{0,1:T(8,128)(2,1)}, bf16[128,2304]{0,1:T(8,128)(2,1)S(1)}, u32[]{:S(2)}, u32[]{:S(2)}) collective-permute-start(bf16[128,2304]{0,1:T(8,128)(2,1)} %collective-permute-done.13), channel_id=1, source_target_pairs={{8,0},{16,8},{24,16},{28,24},{20,28},{12,20},{4,12},{0,4},{9,1},{1... | collective-permute-start | bytes 1769480 | tf_op jit(solution)/shard_map/ppermute | solution.py:43
  120.1 22.8 %collective-permute-start.16 = (bf16[128,2304]{0,1:T(8,128)(2,1)}, bf16[128,2304]{0,1:T(8,128)(2,1)S(1)}, u32[]{:S(2)}, u32[]{:S(2)}) collective-permute-start(bf16[128,2304]{0,1:T(8,128)(2,1)} %collective-permute-done.14), channel_id=1, source_target_pairs={{0,8},{8,16},{16,24},{24,28},{28,20},{20,12},{12,4},{4,0},{1,9},{9... | collective-permute-start | bytes 1769480 | tf_op jit(solution)/shard_map/ppermute | solution.py:46
  131.5 26.2 %collective-permute-start.11 = (bf16[512,1024]{1,0:T(8,128)(2,1)S(1)}, bf16[512,1024]{1,0:T(8,128)(2,1)S(1)}, u32[]{:S(2)}, u32[]{:S(2)}) collective-permute-start(bf16[512,1024]{1,0:T(8,128)(2,1)S(1)} %multiply_convert_fusion.7), channel_id=1, source_target_pairs={{0,2},{2,0},{1,3},{3,1},{4,6},{6,4},{5,7},{7,5},{8,10},{10,8},{9,1... | collective-permute-start | bytes 3145736 | tf_op jit(solution)/shard_map/ppermute | solution.py:82
  140.9 14.8 %collective-permute-start.17 = (bf16[128,2304]{0,1:T(8,128)(2,1)S(1)}, bf16[128,2304]{0,1:T(8,128)(2,1)S(1)}, u32[]{:S(2)}, u32[]{:S(2)}) collective-permute-start(bf16[128,2304]{0,1:T(8,128)(2,1)S(1)} %collective-permute-done.15), channel_id=1, source_target_pairs={{8,0},{16,8},{24,16},{28,24},{20,28},{12,20},{4,12},{0,4},{9,1},{1... | collective-permute-start | bytes 1769480 | tf_op jit(solution)/shard_map/ppermute | solution.py:43
  142.9 18.5 %collective-permute-start.18 = (bf16[128,2304]{0,1:T(8,128)(2,1)S(1)}, bf16[128,2304]{0,1:T(8,128)(2,1)S(1)}, u32[]{:S(2)}, u32[]{:S(2)}) collective-permute-start(bf16[128,2304]{0,1:T(8,128)(2,1)S(1)} %collective-permute-done.16), channel_id=1, source_target_pairs={{0,8},{8,16},{16,24},{24,28},{28,20},{20,12},{12,4},{4,0},{1,9},{9... | collective-permute-start | bytes 1769480 | tf_op jit(solution)/shard_map/ppermute | solution.py:46
  158.5 30.6 %collective-permute-start.30 = (bf16[512,1024]{1,0:T(8,128)(2,1)}, bf16[512,1024]{1,0:T(8,128)(2,1)}, u32[]{:S(2)}, u32[]{:S(2)}) collective-permute-start(bf16[512,1024]{1,0:T(8,128)(2,1)} %bitcast.42), channel_id=1, source_target_pairs={{0,1},{1,0},{2,3},{3,2},{4,5},{5,4},{6,7},{7,6},{8,9},{9,8},{10,11... | collective-permute-start | bytes 3145736 | tf_op jit(solution)/shard_map/ppermute | solution.py:78
  161.4 27.7 %collective-permute-start.32 = (bf16[512,1024]{1,0:T(8,128)(2,1)}, bf16[512,1024]{1,0:T(8,128)(2,1)}, u32[]{:S(2)}, u32[]{:S(2)}) collective-permute-start(bf16[512,1024]{1,0:T(8,128)(2,1)} %collective-permute-done.31), channel_id=1, source_target_pairs={{0,1},{1,0},{2,3},{3,2},{4,5},{5,4},{6,7},{7,6},{8,9},{9,8},{10,11... | collective-permute-start | bytes 3145736 | tf_op jit(solution)/shard_map/ppermute | solution.py:78
  225.3 44.2 %collective-permute-start.34 = (bf16[512,1024]{1,0:T(8,128)(2,1)}, bf16[512,1024]{1,0:T(8,128)(2,1)}, u32[]{:S(2)}, u32[]{:S(2)}) collective-permute-start(bf16[512,1024]{1,0:T(8,128)(2,1)} %get-tuple-element.97), channel_id=1, source_target_pairs={{0,1},{1,0},{2,3},{3,2},{4,5},{5,4},{6,7},{7,6},{8,9},{9,8},{10,11... | collective-permute-start | bytes 3145736 | tf_op jit(solution)/shard_map/ppermute | solution.py:78
  225.3 73.0 %collective-permute-start.33 = (bf16[512,1024]{1,0:T(8,128)(2,1)}, bf16[512,1024]{1,0:T(8,128)(2,1)S(1)}, u32[]{:S(2)}, u32[]{:S(2)}) collective-permute-start(bf16[512,1024]{1,0:T(8,128)(2,1)} %get-tuple-element.96), channel_id=1, source_target_pairs={{0,1},{1,0},{2,3},{3,2},{4,5},{5,4},{6,7},{7,6},{8,9},{9,8},{10,11... | collective-permute-start | bytes 3145736 | tf_op jit(solution)/shard_map/ppermute | solution.py:78
  237.6 35.7 %collective-permute-start.28 = (bf16[512,1024]{1,0:T(8,128)(2,1)}, bf16[512,1024]{1,0:T(8,128)(2,1)}, u32[]{:S(2)}, u32[]{:S(2)}) collective-permute-start(bf16[512,1024]{1,0:T(8,128)(2,1)} %get-tuple-element.99), channel_id=1, source_target_pairs={{0,1},{1,0},{2,3},{3,2},{4,5},{5,4},{6,7},{7,6},{8,9},{9,8},{10,11... | collective-permute-start | bytes 3145736 | tf_op jit(solution)/shard_map/ppermute | solution.py:78
  237.6 63.7 %collective-permute-start.27 = (bf16[512,1024]{1,0:T(8,128)(2,1)}, bf16[512,1024]{1,0:T(8,128)(2,1)S(1)}, u32[]{:S(2)}, u32[]{:S(2)}) collective-permute-start(bf16[512,1024]{1,0:T(8,128)(2,1)} %get-tuple-element.98), channel_id=1, source_target_pairs={{0,1},{1,0},{2,3},{3,2},{4,5},{5,4},{6,7},{7,6},{8,9},{9,8},{10,11... | collective-permute-start | bytes 3145736 | tf_op jit(solution)/shard_map/ppermute | solution.py:78
  246.5 20.4 %collective-permute-start.58 = (bf16[144,1024]{1,0:T(8,128)(2,1)}, bf16[144,1024]{1,0:T(8,128)(2,1)}, u32[]{:S(2)}, u32[]{:S(2)}) collective-permute-start(bf16[144,1024]{1,0:T(8,128)(2,1)} %get-tuple-element.94), channel_id=1, source_target_pairs={{0,8},{8,16},{16,24},{24,28},{28,20},{20,12},{12,4},{4,0},{1,9},{9... | collective-permute-start | bytes 884744 | tf_op jit(solution)/shard_map/ppermute | solution.py:67
  266.9 22.2 %collective-permute-start.48 = (bf16[128,2304]{1,0:T(8,128)(2,1)S(1)}, bf16[128,2304]{1,0:T(8,128)(2,1)S(1)}, u32[]{:S(2)}, u32[]{:S(2)}) collective-permute-start(bf16[128,2304]{1,0:T(8,128)(2,1)S(1)} %get-tuple-element.78), channel_id=1, source_target_pairs={{8,0},{16,8},{24,16},{28,24},{20,28},{12,20},{4,12},{0,4},{9,1},{1... | collective-permute-start | bytes 1769480 | tf_op jit(solution)/shard_map/ppermute | solution.py:67
  269.5 19.1 %collective-permute-start.62 = (bf16[144,1024]{1,0:T(8,128)(2,1)}, bf16[144,1024]{1,0:T(8,128)(2,1)S(1)}, u32[]{:S(2)}, u32[]{:S(2)}) collective-permute-start(bf16[144,1024]{1,0:T(8,128)(2,1)} %get-tuple-element.95), channel_id=1, source_target_pairs={{8,0},{16,8},{24,16},{28,24},{20,28},{12,20},{4,12},{0,4},{9,1},{1... | collective-permute-start | bytes 884744 | tf_op jit(solution)/shard_map/ppermute | solution.py:71
  273.3 26.5 %collective-permute-start.35 = (bf16[512,1024]{1,0:T(8,128)(2,1)S(1)}, bf16[512,1024]{1,0:T(8,128)(2,1)S(1)}, u32[]{:S(2)}, u32[]{:S(2)}) collective-permute-start(bf16[512,1024]{1,0:T(8,128)(2,1)S(1)} %fusion.23), channel_id=1, source_target_pairs={{0,2},{2,0},{1,3},{3,1},{4,6},{6,4},{5,7},{7,5},{8,10},{10,8},{9,1... | collective-permute-start | bytes 3145736 | tf_op jit(solution)/shard_map/ppermute | solution.py:82
  289.2 31.0 %collective-permute-start.29 = (bf16[512,1024]{1,0:T(8,128)(2,1)S(1)}, bf16[512,1024]{1,0:T(8,128)(2,1)S(1)}, u32[]{:S(2)}, u32[]{:S(2)}) collective-permute-start(bf16[512,1024]{1,0:T(8,128)(2,1)S(1)} %fusion.25), channel_id=1, source_target_pairs={{0,2},{2,0},{1,3},{3,1},{4,6},{6,4},{5,7},{7,5},{8,10},{10,8},{9,1... | collective-permute-start | bytes 3145736 | tf_op jit(solution)/shard_map/ppermute | solution.py:82
  296.8 35.0 %collective-permute-start.52 = (bf16[128,2304]{1,0:T(8,128)(2,1)}, bf16[128,2304]{1,0:T(8,128)(2,1)}, u32[]{:S(2)}, u32[]{:S(2)}) collective-permute-start(bf16[128,2304]{1,0:T(8,128)(2,1)} %get-tuple-element.79), channel_id=1, source_target_pairs={{0,8},{8,16},{16,24},{24,28},{28,20},{20,12},{12,4},{4,0},{1,9},{9... | collective-permute-start | bytes 1769480 | tf_op jit(solution)/shard_map/ppermute | solution.py:71
  298.4 33.4 %collective-permute-start.49 = (bf16[128,2304]{1,0:T(8,128)(2,1)}, bf16[128,2304]{1,0:T(8,128)(2,1)}, u32[]{:S(2)}, u32[]{:S(2)}) collective-permute-start(bf16[128,2304]{1,0:T(8,128)(2,1)} %add_convert_fusion.8), channel_id=1, source_target_pairs={{8,0},{16,8},{24,16},{28,24},{20,28},{12,20},{4,12},{0,4},{9,1},{1... | collective-permute-start | bytes 1769480 | tf_op jit(solution)/shard_map/ppermute | solution.py:67
  299.8 27.4 %collective-permute-start.60 = (bf16[144,1024]{1,0:T(8,128)(2,1)}, bf16[144,1024]{1,0:T(8,128)(2,1)}, u32[]{:S(2)}, u32[]{:S(2)}) collective-permute-start(bf16[144,1024]{1,0:T(8,128)(2,1)} %get-tuple-element.92), channel_id=1, source_target_pairs={{0,8},{8,16},{16,24},{24,28},{28,20},{20,12},{12,4},{4,0},{1,9},{9... | collective-permute-start | bytes 884744 | tf_op jit(solution)/shard_map/ppermute | solution.py:67
  301.3 26.0 %collective-permute-start.63 = (bf16[144,1024]{1,0:T(8,128)(2,1)}, bf16[144,1024]{1,0:T(8,128)(2,1)}, u32[]{:S(2)}, u32[]{:S(2)}) collective-permute-start(bf16[144,1024]{1,0:T(8,128)(2,1)} %get-tuple-element.93), channel_id=1, source_target_pairs={{8,0},{16,8},{24,16},{28,24},{20,28},{12,20},{4,12},{0,4},{9,1},{1... | collective-permute-start | bytes 884744 | tf_op jit(solution)/shard_map/ppermute | solution.py:71
  329.7 58.4 %collective-permute-start.64 = (bf16[144,1024]{1,0:T(8,128)(2,1)}, bf16[144,1024]{1,0:T(8,128)(2,1)}, u32[]{:S(2)}, u32[]{:S(2)}) collective-permute-start(bf16[144,1024]{1,0:T(8,128)(2,1)} %get-tuple-element.91), channel_id=1, source_target_pairs={{8,0},{16,8},{24,16},{28,24},{20,28},{12,20},{4,12},{0,4},{9,1},{1... | collective-permute-start | bytes 884744 | tf_op jit(solution)/shard_map/ppermute | solution.py:71
  330.1 58.0 %collective-permute-start.61 = (bf16[144,1024]{1,0:T(8,128)(2,1)}, bf16[144,1024]{1,0:T(8,128)(2,1)}, u32[]{:S(2)}, u32[]{:S(2)}) collective-permute-start(bf16[144,1024]{1,0:T(8,128)(2,1)} %get-tuple-element.90), channel_id=1, source_target_pairs={{0,8},{8,16},{16,24},{24,28},{28,20},{20,12},{12,4},{4,0},{1,9},{9... | collective-permute-start | bytes 884744 | tf_op jit(solution)/shard_map/ppermute | solution.py:67
  335.1 47.7 %collective-permute-start.50 = (bf16[128,2304]{1,0:T(8,128)(2,1)}, bf16[128,2304]{1,0:T(8,128)(2,1)}, u32[]{:S(2)}, u32[]{:S(2)}) collective-permute-start(bf16[128,2304]{1,0:T(8,128)(2,1)} %get-tuple-element.76), channel_id=1, source_target_pairs={{8,0},{16,8},{24,16},{28,24},{20,28},{12,20},{4,12},{0,4},{9,1},{1... | collective-permute-start | bytes 1769480 | tf_op jit(solution)/shard_map/ppermute | solution.py:67
  335.5 47.3 %collective-permute-start.53 = (bf16[128,2304]{1,0:T(8,128)(2,1)}, bf16[128,2304]{1,0:T(8,128)(2,1)}, u32[]{:S(2)}, u32[]{:S(2)}) collective-permute-start(bf16[128,2304]{1,0:T(8,128)(2,1)} %get-tuple-element.77), channel_id=1, source_target_pairs={{0,8},{8,16},{16,24},{24,28},{28,20},{20,12},{12,4},{4,0},{1,9},{9... | collective-permute-start | bytes 1769480 | tf_op jit(solution)/shard_map/ppermute | solution.py:71
  380.3 16.9 %collective-permute-start.39 = (bf16[144,2048]{1,0:T(8,128)(2,1)S(1)}, bf16[144,2048]{1,0:T(8,128)(2,1)S(1)}, u32[]{:S(2)}, u32[]{:S(2)}) collective-permute-start(bf16[144,2048]{1,0:T(8,128)(2,1)S(1)} %get-tuple-element.85), channel_id=1, source_target_pairs={{0,8},{8,16},{16,24},{24,28},{28,20},{20,12},{12,4},{4,0},{1,9},{9... | collective-permute-start | bytes 1769480 | tf_op jit(solution)/shard_map/ppermute | solution.py:67
  385.4 24.4 %collective-permute-start.54 = (bf16[128,2304]{1,0:T(8,128)(2,1)S(1)}, bf16[128,2304]{1,0:T(8,128)(2,1)S(1)}, u32[]{:S(2)}, u32[]{:S(2)}) collective-permute-start(bf16[128,2304]{1,0:T(8,128)(2,1)S(1)} %get-tuple-element.75), channel_id=1, source_target_pairs={{0,8},{8,16},{16,24},{24,28},{28,20},{20,12},{12,4},{4,0},{1,9},{9... | collective-permute-start | bytes 1769480 | tf_op jit(solution)/shard_map/ppermute | solution.py:71
  388.1 21.8 %collective-permute-start.51 = (bf16[128,2304]{1,0:T(8,128)(2,1)S(1)}, bf16[128,2304]{1,0:T(8,128)(2,1)S(1)}, u32[]{:S(2)}, u32[]{:S(2)}) collective-permute-start(bf16[128,2304]{1,0:T(8,128)(2,1)S(1)} %get-tuple-element.74), channel_id=1, source_target_pairs={{8,0},{16,8},{24,16},{28,24},{20,28},{12,20},{4,12},{0,4},{9,1},{1... | collective-permute-start | bytes 1769480 | tf_op jit(solution)/shard_map/ppermute | solution.py:67
  389.5 34.8 %collective-permute-start.66 = (bf16[144,1024]{1,0:T(8,128)(2,1)S(1)}, bf16[144,1024]{1,0:T(8,128)(2,1)S(1)}, u32[]{:S(2)}, u32[]{:S(2)}) collective-permute-start(bf16[144,1024]{1,0:T(8,128)(2,1)S(1)} %add_convert_fusion.14), channel_id=1, source_target_pairs={{0,2},{2,0},{1,3},{3,1},{4,6},{6,4},{5,7},{7,5},{8,10},{10,8},{9,1... | collective-permute-start | bytes 884744 | tf_op jit(solution)/shard_map/ppermute | solution.py:82
  391.1 23.6 %collective-permute-start.43 = (bf16[144,2048]{1,0:T(8,128)(2,1)S(1)}, bf16[144,2048]{1,0:T(8,128)(2,1)S(1)}, u32[]{:S(2)}, u32[]{:S(2)}) collective-permute-start(bf16[144,2048]{1,0:T(8,128)(2,1)S(1)} %get-tuple-element.86), channel_id=1, source_target_pairs={{8,0},{16,8},{24,16},{28,24},{20,28},{12,20},{4,12},{0,4},{9,1},{1... | collective-permute-start | bytes 1769480 | tf_op jit(solution)/shard_map/ppermute | solution.py:71
  397.4 23.4 %collective-permute-start.40 = (bf16[144,2048]{1,0:T(8,128)(2,1)S(1)}, bf16[144,2048]{1,0:T(8,128)(2,1)S(1)}, u32[]{:S(2)}, u32[]{:S(2)}) collective-permute-start(bf16[144,2048]{1,0:T(8,128)(2,1)S(1)} %add_convert_fusion.13), channel_id=1, source_target_pairs={{0,8},{8,16},{16,24},{24,28},{28,20},{20,12},{12,4},{4,0},{1,9},{9... | collective-permute-start | bytes 1769480 | tf_op jit(solution)/shard_map/ppermute | solution.py:67
  411.4 16.8 %collective-permute-start.56 = (bf16[128,2304]{1,0:T(8,128)(2,1)S(1)}, bf16[128,2304]{1,0:T(8,128)(2,1)S(1)}, u32[]{:S(2)}, u32[]{:S(2)}) collective-permute-start(bf16[128,2304]{1,0:T(8,128)(2,1)S(1)} %add_convert_fusion.3), channel_id=1, source_target_pairs={{0,2},{2,0},{1,3},{3,1},{4,6},{6,4},{5,7},{7,5},{8,10},{10,8},{9,1... | collective-permute-start | bytes 1769480 | tf_op jit(solution)/shard_map/ppermute | solution.py:82
  428.0 19.3 %collective-permute-start.55 = (bf16[128,2304]{1,0:T(8,128)(2,1)S(1)}, bf16[128,2304]{1,0:T(8,128)(2,1)S(1)}, u32[]{:S(2)}, u32[]{:S(2)}) collective-permute-start(bf16[128,2304]{1,0:T(8,128)(2,1)S(1)} %add_convert_fusion.3), channel_id=1, source_target_pairs={{0,1},{1,0},{2,3},{3,2},{4,5},{5,4},{6,7},{7,6},{8,9},{9,8},{10,11... | collective-permute-start | bytes 1769480 | tf_op jit(solution)/shard_map/ppermute | solution.py:78
  428.2 19.1 %collective-permute-start.57 = (bf16[128,2304]{1,0:T(8,128)(2,1)S(1)}, bf16[128,2304]{1,0:T(8,128)(2,1)S(1)}, u32[]{:S(2)}, u32[]{:S(2)}) collective-permute-start(bf16[128,2304]{1,0:T(8,128)(2,1)S(1)} %collective-permute-done.56), channel_id=1, source_target_pairs={{0,1},{1,0},{2,3},{3,2},{4,5},{5,4},{6,7},{7,6},{8,9},{9,8},{10,11... | collective-permute-start | bytes 1769480 | tf_op jit(solution)/shard_map/ppermute | solution.py:78
  447.3 19.8 %collective-permute-start.38 = (bf16[512,1024]{1,0:T(8,128)(2,1)}, bf16[512,1024]{1,0:T(8,128)(2,1)}, u32[]{:S(2)}, u32[]{:S(2)}) collective-permute-start(bf16[512,1024]{1,0:T(8,128)(2,1)} %slice.368), channel_id=1, source_target_pairs={{0,1},{1,0},{2,3},{3,2},{4,5},{5,4},{6,7},{7,6},{8,9},{9,8},{10,11... | collective-permute-start | bytes 3145736 | tf_op jit(solution)/shard_map/ppermute | solution.py:78
  (89 other events, 806.6 us)

commit v3 on v0

v3 whole, which is shorter than its diff:
```python
import functools

import jax
import jax.numpy as jnp
from jax import lax
from jax.experimental import pallas as pl
from jax.experimental.pallas import tpu as pltpu
from jax.sharding import Mesh, PartitionSpec as P

epsilon = 1e-05
PAIR = ((0, 1), (1, 0))


def over_core(value):
    return lax.ppermute(value, "core", PAIR)


def over_y(value):
    return lax.ppermute(value, "y", PAIR)


def outer_sum(left, right):
    return lax.dot_general(
        left, right, (((0,), (0,)), ((), ())), preferred_element_type=jnp.float32
    )


def times_transposed(grad, weight):
    return lax.dot_general(
        grad, weight, (((1,), (1,)), ((), ())), preferred_element_type=jnp.float32
    )


def times(value, weight):
    return jnp.dot(value, weight, preferred_element_type=jnp.float32)


def wide(value):
    return value.astype(jnp.float32)


def narrow(value):
    return value.astype(jnp.bfloat16)


def tie_kernel(*refs):
    del refs


def tie(value, *others):
    return pl.pallas_call(
        tie_kernel,
        out_shape=jax.ShapeDtypeStruct(value.shape, value.dtype),
        in_specs=[pl.BlockSpec(memory_space=pl.ANY)] * (1 + len(others)),
        out_specs=pl.BlockSpec(memory_space=pl.ANY),
        input_output_aliases={0: 0},
    )(value, *others)


def ring_order(count):
    return list(range(0, count, 2)) + list(range(1, count, 2))[::-1]


def ring_pairs(count):
    order = ring_order(count)
    ahead = [(order[i], order[(i + 1) % count]) for i in range(count)]
    return ahead, [(b, a) for a, b in ahead]


def ring_place(count, offset):
    me = lax.axis_index("shard")
    here = jnp.where(me % 2 == 0, me // 2, count - 1 - me // 2)
    there = (here + offset) % count
    return jnp.where(there < count // 2, 2 * there, 2 * (count - 1 - there) + 1)


class Gather:
    def __init__(self, block, flip):
        self.count = lax.axis_size("shard")
        self.far, self.near = self.count // 2, self.count - 1 - self.count // 2
        self.sign = -1 if flip else 1
        self.pairs = ring_pairs(self.count)[:: self.sign]
        self.step = 0
        self.one = self.two = block
        self.whole = jnp.zeros((self.count,) + block.shape, block.dtype)
        self.put(block, 0)

    def put(self, block, offset):
        place = ring_place(self.count, offset)
        self.whole = lax.dynamic_update_slice(self.whole, block[None], (place, 0, 0))

    def hop(self):
        self.step += 1
        if self.step <= self.far:
            self.one = lax.ppermute(self.one, "shard", self.pairs[0])
            self.put(self.one, -self.sign * self.step)
        if self.step <= self.near:
            self.two = lax.ppermute(self.two, "shard", self.pairs[1])
            self.put(self.two, self.sign * self.step)
        return self

    def end(self):
        while self.step < self.far:
            self.hop()
        return self.whole


class Scatter:
    def __init__(self, part, flip):
        self.count = lax.axis_size("shard")
        self.far, self.near = self.count // 2, self.count - 1 - self.count // 2
        self.sign = -1 if flip else 1
        self.pairs = ring_pairs(self.count)[:: self.sign]
        self.step = 0
        self.part = lambda offset: wide(part(ring_place(self.count, offset)))
        self.one = narrow(self.part(self.sign * self.far))
        self.two = narrow(self.part(-self.sign * self.near))

    def hop(self):
        self.step += 1
        if self.step <= self.far:
            self.one = lax.ppermute(self.one, "shard", self.pairs[0])
            if self.step < self.far:
                self.one = narrow(wide(self.one) + self.part(self.sign * (self.far - self.step)))
        if self.step <= self.near:
            self.two = lax.ppermute(self.two, "shard", self.pairs[1])
            if self.step < self.near:
                self.two = narrow(wide(self.two) + self.part(-self.sign * (self.near - self.step)))
        return self

    def end(self):
        while self.step < self.far:
            self.hop()
        return self.part(0) + wide(self.one) + wide(self.two)


def rows_block(tile, columns, first=0):
    return pl.BlockSpec((tile, columns), lambda i: (first + i, 0))


def whole_block(shape):
    zeros = (0,) * len(shape)
    return pl.BlockSpec(shape, lambda i: zeros, pipeline_mode=pl.Buffered(1))


def params(size=48):
    return pltpu.CompilerParams(vmem_limit_bytes=size * 2**20)


def flat(value):
    return value.reshape(-1, value.shape[-1])


def mix_in_kernel(half, own, tokens_ref, gain_ref, mix_ref, normed_ref, b_ref, c_ref, x_ref, p_ref):
    inputs = wide(tokens_ref[...])
    unit = inputs * lax.rsqrt(jnp.mean(inputs * inputs, axis=-1, keepdims=True) + epsilon)
    normed = narrow(unit * gain_ref[...])
    normed_ref[...] = normed
    for i, ref in enumerate((b_ref, c_ref, x_ref)):
        ref[...] = times(normed, flat(mix_ref[:, :own, i * half : (i + 1) * half]))
    p_ref[...] = narrow(b_ref[...] * x_ref[...])


def mix_in(tokens, gain, mix, own):
    count, width = tokens.shape
    half = width // 2
    tile = count // 4
    f32, bf16 = jnp.float32, jnp.bfloat16
    shapes = [(width, bf16), (half, f32), (half, f32), (half, f32), (half, bf16)]
    return pl.pallas_call(
        functools.partial(mix_in_kernel, half, own),
        grid=(4,),
        in_specs=[rows_block(tile, width), whole_block((1, width)), whole_block(mix.shape)],
        out_specs=[rows_block(tile, columns) for columns, _ in shapes],
        out_shape=[jax.ShapeDtypeStruct((count, columns), kind) for columns, kind in shapes],
        compiler_params=params(),
        cost_estimate=pl.CostEstimate(
            flops=6 * count * width * half, bytes_accessed=14 * count * width, transcendentals=0
        ),
    )(tokens, gain, mix)


def delayed(product, halo):
    row = lax.broadcasted_iota(jnp.int32, product.shape, 0)
    one = jnp.where(row == 0, halo[1:2], pltpu.roll(product, 1, 0))
    two = jnp.where(row == 0, halo[0:1], jnp.where(row == 1, halo[1:2], pltpu.roll(product, 2, 0)))
    return one, two


def mix_out_kernel(half, own, c_ref, p_ref, halo_ref, taps_ref, mix_ref, conv_ref, gated_ref, out_ref):
    product = wide(p_ref[...])
    one, two = delayed(product, wide(halo_ref[0]))
    conv = taps_ref[0:1] * two + taps_ref[1:2] * one + taps_ref[2:3] * product
    conv_ref[...] = conv
    gated = narrow(c_ref[...] * conv)
    gated_ref[...] = gated
    for i in range(2):
        weight = flat(mix_ref[:, i * own // 2 : (i + 1) * own // 2, 3 * half :])
        out_ref[:, i * half : (i + 1) * half] = narrow(times(gated, weight))


def mix_out(c_part, product, halo, taps, mix, own):
    count, half = product.shape
    length = count // 2
    shapes = [(half, jnp.float32), (half, jnp.bfloat16), (2 * half, jnp.bfloat16)]
    return pl.pallas_call(
        functools.partial(mix_out_kernel, half, own),
        grid=(2,),
        in_specs=[
            rows_block(length, half),
            rows_block(length, half),
            pl.BlockSpec((1,) + halo.shape[1:], lambda i: (i, 0, 0)),
            whole_block(taps.shape),
            whole_block(mix.shape),
        ],
        out_specs=[rows_block(length, columns) for columns, _ in shapes],
        out_shape=[jax.ShapeDtypeStruct((count, columns), kind) for columns, kind in shapes],
        compiler_params=params(),
        cost_estimate=pl.CostEstimate(
            flops=4 * count * half * half, bytes_accessed=16 * count * half, transcendentals=0
        ),
    )(c_part, product, halo, taps, mix)


def mix_back_kernel(
    half, own, d_ref, c_ref, conv_ref, p_ref, halo_ref, taps_ref, mix_ref, d_c_ref, d_p_ref, edge_ref, sums_ref
):
    grad = d_ref[...]
    d_gated = times_transposed(grad[:, :half], flat(mix_ref[:, : own // 2, 3 * half :]))
    d_gated += times_transposed(grad[:, half:], flat(mix_ref[:, own // 2 : own, 3 * half :]))
    d_c_ref[...] = narrow(d_gated * conv_ref[...])
    d_conv = d_gated * c_ref[...]
    product = wide(p_ref[...])
    one, two = delayed(product, wide(halo_ref[0]))

    @pl.when(pl.program_id(0) == 0)
    def _():
        sums_ref[...] = jnp.zeros_like(sums_ref)

    for k, value in enumerate((two, one, product)):
        sums_ref[k : k + 1] += jnp.sum(d_conv * value, axis=0, keepdims=True)
    taps = taps_ref[...]
    length = d_conv.shape[0]
    row = lax.broadcasted_iota(jnp.int32, d_conv.shape, 0)
    later = jnp.where(row < length - 1, pltpu.roll(d_conv, length - 1, 0), 0.0)
    latest = jnp.where(row < length - 2, pltpu.roll(d_conv, length - 2, 0), 0.0)
    d_p_ref[...] = taps[2:3] * d_conv + taps[1:2] * later + taps[0:1] * latest
    edge_ref[0, 0:1] = taps[0:1] * d_conv[0:1]
    edge_ref[0, 1:2] = taps[0:1] * d_conv[1:2] + taps[1:2] * d_conv[0:1]


def mix_back(d_branch, c_part, conv, product, halo, taps, mix, own):
    count, half = product.shape
    length = count // 2
    f32 = jnp.float32
    return pl.pallas_call(
        functools.partial(mix_back_kernel, half, own),
        grid=(2,),
        in_specs=[
            rows_block(length, 2 * half),
            rows_block(length, half),
            rows_block(length, half),
            rows_block(length, half),
            pl.BlockSpec((1,) + halo.shape[1:], lambda i: (i, 0, 0)),
            whole_block(taps.shape),
            whole_block(mix.shape),
        ],
        out_specs=[
            rows_block(length, half),
            rows_block(length, half),
            pl.BlockSpec((1, 2, half), lambda i: (i, 0, 0)),
            pl.BlockSpec((3, half), lambda i: (0, 0)),
        ],
        out_shape=[
            jax.ShapeDtypeStruct((count, half), jnp.bfloat16),
            jax.ShapeDtypeStruct((count, half), f32),
            jax.ShapeDtypeStruct((2, 2, half), f32),
            jax.ShapeDtypeStruct((3, half), f32),
        ],
        compiler_params=params(),
        cost_estimate=pl.CostEstimate(
            flops=4 * count * half * half, bytes_accessed=20 * count * half, transcendentals=0
        ),
    )(d_branch, c_part, conv, product, halo, taps, mix)


def mix_last_kernel(
    half, own, d_p_ref, edge_ref, b_ref, x_ref, d_c_ref, tokens_ref, mix_ref, d_mixed_ref, d_n_ref, sums_ref
):
    d_product = d_p_ref[...]
    length = d_product.shape[0]
    row = lax.broadcasted_iota(jnp.int32, d_product.shape, 0)
    edge = edge_ref[0]
    d_product += jnp.where(
        row == length - 2, edge[0:1], jnp.where(row == length - 1, edge[1:2], 0.0)
    )
    d_mixed_ref[:, :half] = narrow(d_product * x_ref[...])
    d_mixed_ref[:, half : 2 * half] = d_c_ref[...]
    d_mixed_ref[:, 2 * half :] = narrow(d_product * b_ref[...])
    d_normed = times_transposed(d_mixed_ref[...], flat(mix_ref[:, :own, : 3 * half]))
    d_n_ref[...] = narrow(d_normed)
    inputs = wide(tokens_ref[...])
    unit = inputs * lax.rsqrt(jnp.mean(inputs * inputs, axis=-1, keepdims=True) + epsilon)

    @pl.when(pl.program_id(0) == 0)
    def _():
        sums_ref[...] = jnp.zeros_like(sums_ref)

    sums_ref[...] += jnp.sum(d_normed * unit, axis=0, keepdims=True)


def mix_last(d_product, edge, b_part, x_part, d_c, tokens, mix, own):
    count, half = d_product.shape
    length = count // 2
    return pl.pallas_call(
        functools.partial(mix_last_kernel, half, own),
        grid=(2,),
        in_specs=[
            rows_block(length, half),
            pl.BlockSpec((1, 2, half), lambda i: (i, 0, 0)),
            rows_block(length, half),
            rows_block(length, half),
            rows_block(length, half),
            rows_block(length, 2 * half),
            whole_block(mix.shape),
        ],
        out_specs=[
            rows_block(length, 3 * half),
            rows_block(length, 2 * half),
            pl.BlockSpec((1, 2 * half), lambda i: (0, 0)),
        ],
        out_shape=[
            jax.ShapeDtypeStruct((count, 3 * half), jnp.bfloat16),
            jax.ShapeDtypeStruct((count, 2 * half), jnp.bfloat16),
            jax.ShapeDtypeStruct((1, 2 * half), jnp.float32),
        ],
        compiler_params=params(),
        cost_estimate=pl.CostEstimate(
            flops=12 * count * half * half, bytes_accessed=28 * count * half, transcendentals=0
        ),
    )(d_product, edge, b_part, x_part, d_c, tokens, mix)


def feed_forward_kernel(size, rows_ref, cot_ref, both_ref, down_ref, *refs):
    hidden_ref, d_both_ref, d_rows_ref, out_ref = refs[-4:]
    rows = rows_ref[...]
    cot = cot_ref[...]
    for start in range(0, size, 256):
        stop = min(start + 256, size)
        gate = times(rows, both_ref[:, start:stop])
        upper = times(rows, both_ref[:, size + start : size + stop])
        d_hidden = times_transposed(cot, down_ref[start:stop])
        sigma = jax.nn.sigmoid(gate)
        activated = gate * sigma
        hidden_ref[:, start:stop] = narrow(activated * upper)
        d_both_ref[:, start:stop] = narrow(d_hidden * upper * sigma * (1.0 + gate * (1.0 - sigma)))
        d_both_ref[:, size + start : size + stop] = narrow(d_hidden * activated)
    d_rows_ref[...] = narrow(times_transposed(d_both_ref[...], both_ref[...]))
    out_ref[...] = narrow(times(hidden_ref[...], down_ref[...]))


def feed_forward(rows, cot, both, down, at, kept=(), first=()):
    width = rows.shape[1]
    tokens = cot.shape[0] // 2
    tile = tokens // 2
    size = down.shape[0]
    here = 2 * at
    aliases = {4 + i: i for i in range(len(kept))}
    return pl.pallas_call(
        functools.partial(feed_forward_kernel, size),
        grid=(2,),
        in_specs=[
            rows_block(tile, width, here),
            rows_block(tile, width, here),
            whole_block(both.shape),
            whole_block(down.shape),
        ]
        + [pl.BlockSpec(memory_space=pl.ANY)] * (len(kept) + len(first)),
        out_specs=[
            rows_block(tile, size, here),
            rows_block(tile, 2 * size, here),
            rows_block(tile, width),
            rows_block(tile, width),
        ],
        out_shape=[
            jax.ShapeDtypeStruct((2 * tokens, size), jnp.bfloat16),
            jax.ShapeDtypeStruct((2 * tokens, 2 * size), jnp.bfloat16),
            jax.ShapeDtypeStruct((tokens, width), jnp.bfloat16),
            jax.ShapeDtypeStruct((tokens, width), jnp.bfloat16),
        ],
        input_output_aliases=aliases,
        compiler_params=params(),
        cost_estimate=pl.CostEstimate(
            flops=12 * tokens * width * size,
            bytes_accessed=16 * tokens * width,
            transcendentals=tokens * size,
        ),
    )(rows, cot, both, down, *kept, *first)


def lay_out_kernel(groups, member_ref, parts_ref, gate_ref, up_ref):
    member = member_ref[0]
    size = parts_ref.shape[2] // (2 * groups)
    for place in range(4):
        part = wide(parts_ref[jnp.bitwise_xor(place, member)])
        for half, out_ref in enumerate((gate_ref, up_ref)):
            for group in range(groups):
                start = (group * 4 + place) * size
                taken = (half * groups + group) * size
                out_ref[:, start : start + size] = part[:, taken : taken + size]


def lay_out(parts, member, groups):
    _, rows, columns = parts.shape
    return pl.pallas_call(
        functools.partial(lay_out_kernel, groups),
        out_shape=[jax.ShapeDtypeStruct((rows, 2 * columns), jnp.float32)] * 2,
        in_specs=[
            pl.BlockSpec(memory_space=pltpu.SMEM),
            pl.BlockSpec(memory_space=pltpu.VMEM),
        ],
        out_specs=[pl.BlockSpec(memory_space=pltpu.VMEM)] * 2,
        compiler_params=params(),
        cost_estimate=pl.CostEstimate(
            flops=0, bytes_accessed=24 * rows * columns, transcendentals=0
        ),
    )(member[None], parts)


def picked(value, groups, parts, part, first=0, size=None):
    whole = value.shape[1] // (groups * parts)
    size = whole if size is None else size
    row = lax.broadcasted_iota(jnp.int32, (value.shape[1], groups * size), 0)
    column = lax.broadcasted_iota(jnp.int32, (value.shape[1], groups * size), 1)
    wanted = (column // size * parts + part) * whole + first + column % size
    return narrow(times(value, (row == wanted).astype(value.dtype)))


def local(
    tokens,
    cotangent,
    in_weight,
    out_weight,
    gate_weight,
    up_weight,
    down_weight,
    mix_gain,
    ffn_gain,
    conv_taps,
):
    shards = lax.axis_size("shard")
    core = lax.axis_index("core")
    member = lax.axis_index("y") * 2 + core
    width = tokens.shape[-1]
    length = tokens.shape[1]
    half = width // 2
    own = mix_gain.shape[0]
    lane = half // shards

    small = jnp.concatenate([mix_gain[None], ffn_gain[None], conv_taps], 0)
    in_mine = jnp.concatenate(
        [picked(in_weight[:, i * width : (i + 1) * width], shards, 2, core) for i in range(3)], 1
    )
    out_rows = own // 2
    out_mine = lax.dynamic_slice(out_weight, (core * out_rows, 0), (out_rows, width))
    out_mine = jnp.concatenate([out_mine[:, :half], out_mine[:, half:]], 0)
    small_rows = jnp.pad(small, ((0, 11), (0, 4 * half - own)))
    mix_ring = Gather(
        jnp.concatenate([jnp.concatenate([in_mine, out_mine], 1), small_rows], 0), False
    )
    pair = jnp.concatenate([tokens[0], over_core(tokens[0])], 0)
    mix = mix_ring.end()

    quarter = down_weight.shape[0] // 4
    both = picked(jnp.concatenate([gate_weight, up_weight], 0), shards, 4, member)
    both_ring = Gather(jnp.concatenate([both[:own], both[own:]], 1), True)
    down_ring = Gather(
        lax.dynamic_slice(down_weight, (member * quarter, 0), (quarter, width)), False
    )
    both_full = flat(both_ring.end())
    down_full = flat(down_ring.end())

    small = wide(mix[:, own : own + 5, :own].transpose(1, 0, 2).reshape(5, width))
    gain_one, gain_two = small[0:1], small[1]
    taps = lax.dynamic_index_in_dim(
        small[2:5].reshape(3, shards, 2, lane), core, 2, keepdims=False
    ).reshape(3, half)

    normed, b_part, c_part, x_part, product = mix_in(pair, gain_one, mix, own)
    halo = lax.ppermute(
        product.reshape(2, length, half)[:, length - 2 :],
        "shard",
        [(i, i + 1) for i in range(shards - 1)],
    )
    conv, gated, branch = mix_out(c_part, product, halo, taps, mix, own)
    inputs = wide(tokens[0])
    resid = inputs + wide(branch[:length]) + wide(over_core(branch[length:]))

    factor_two = lax.rsqrt(jnp.mean(resid * resid, axis=-1, keepdims=True) + epsilon)
    unit_two = resid * factor_two
    hnorm = narrow(unit_two * gain_two)
    across = over_y(hnorm)
    hnorm_all = jnp.concatenate([hnorm, over_core(hnorm), across, over_core(across)], 0)
    cot = cotangent[0]
    cot_across = over_y(cot)
    cot_all = jnp.concatenate([cot, over_core(cot), cot_across, over_core(cot_across)], 0)

    hidden, d_both, d_far, out_far = feed_forward(hnorm_all, cot_all, both_full, down_full, 1)
    d_far = narrow(wide(over_core(d_far[length:])) + wide(d_far[:length]))
    hidden, d_both, d_near, out_near = feed_forward(
        hnorm_all, cot_all, both_full, down_full, 0, (hidden, d_both), (d_far,)
    )
    d_far = over_y(d_far)
    g_both = outer_sum(hnorm_all, d_both)
    g_down = outer_sum(hidden, cot_all)

    def rows_of(value):
        rows = value.shape[0] // shards
        return lambda place: lax.dynamic_slice(value, (place * rows, 0), (rows, value.shape[1]))

    back_both = Scatter(rows_of(g_both), True)
    back_down = Scatter(rows_of(g_down), False)
    d_near = wide(d_near[:length]) + wide(over_core(d_near[length:]))
    d_hnorm = d_near + wide(d_far)

    g_ffn_gain = jnp.sum(d_hnorm * unit_two, axis=0, keepdims=True)
    scaled_two = d_hnorm * gain_two
    d_resid = wide(cotangent[0]) + factor_two * (
        scaled_two - unit_two * jnp.mean(scaled_two * unit_two, axis=-1, keepdims=True)
    )
    out_far = tie(out_far, d_far)
    out_far = over_y(narrow(wide(over_core(out_far[length:])) + wide(out_far[:length])))
    out_near = wide(out_near[:length]) + wide(over_core(out_near[length:]))
    output = narrow(resid + out_near + wide(out_far))

    d_own = narrow(d_resid)
    d_branch = jnp.concatenate([d_own, over_core(d_own)], 0)
    d_c, d_product, edge, tap_grads = mix_back(
        d_branch, c_part, conv, product, halo, taps, mix, own
    )
    returned = lax.ppermute(edge, "shard", [(i + 1, i) for i in range(shards - 1)])
    g_out = outer_sum(gated, d_branch)
    d_mixed, d_normed, g_mix_gain = mix_last(
        d_product, returned, b_part, x_part, d_c, pair, mix, own
    )
    g_in = outer_sum(normed, d_mixed)
    spot = lax.broadcasted_iota(jnp.int32, (3, shards, 2, lane), 2)
    tap_full = jnp.where(spot == core, tap_grads.reshape(3, shards, 1, lane), 0.0)
    small_grads = jnp.concatenate([g_mix_gain, g_ffn_gain, tap_full.reshape(3, width)], 0)

    def mix_part(place):
        out = lax.dynamic_slice(g_out, (place * out_rows, 0), (out_rows, width))
        out = jnp.concatenate([out[:, :half], out[:, half:]], 0)
        main = lax.dynamic_slice(g_in, (place * own, 0), (own, 3 * half))
        few = lax.dynamic_slice(small_grads, (0, place * own), (5, own))
        few = jnp.pad(few, ((0, 11), (0, 4 * half - own)))
        return jnp.concatenate([jnp.concatenate([main, out], 1), few], 0)

    back_mix = Scatter(mix_part, False)
    d_normed = wide(d_normed[:length]) + wide(over_core(d_normed[length:]))
    factor_one = lax.rsqrt(jnp.mean(inputs * inputs, axis=-1, keepdims=True) + epsilon)
    unit_one = inputs * factor_one
    scaled_one = d_normed * gain_one
    d_inputs = d_resid + factor_one * (
        scaled_one - unit_one * jnp.mean(scaled_one * unit_one, axis=-1, keepdims=True)
    )

    def summed(value):
        return narrow(lax.psum(value, "outer") if lax.axis_size("outer") > 1 else value)

    def four_parts(value):
        mine = summed(value)
        across = over_y(mine)
        return jnp.stack([mine, over_core(mine), across, over_core(across)], 0)

    owned_gate, owned_up = lay_out(four_parts(back_both.end()), member, shards)
    down_parts = four_parts(back_down.end())
    owned_down = wide(
        jnp.concatenate(
            [
                lax.dynamic_index_in_dim(down_parts, jnp.bitwise_xor(i, member), 0, keepdims=False)
                for i in range(4)
            ],
            0,
        )
    )

    mix_mine = summed(back_mix.end())
    mix_mine = narrow(wide(mix_mine) + wide(over_y(mix_mine)))
    mix_other = over_core(mix_mine)
    low = jnp.where(core == 0, mix_mine, mix_other)
    high = jnp.where(core == 0, mix_other, mix_mine)
    owned_in = jnp.stack(
        [value[:own, : 3 * half].reshape(own, 3 * shards, lane) for value in (low, high)], 2
    )
    owned_in = wide(owned_in.reshape(own, 3 * width))
    owned_out = wide(
        jnp.concatenate(
            [
                jnp.concatenate([value[:out_rows, 3 * half :], value[out_rows:own, 3 * half :]], 1)
                for value in (low, high)
            ],
            0,
        )
    )
    small_owned = wide(low[own : own + 5, :own]) + wide(high[own : own + 5, :own])
    return (
        output[None],
        narrow(d_inputs)[None],
        owned_in,
        owned_out,
        owned_gate,
        owned_up,
        owned_down,
        small_owned[0],
        small_owned[1],
        small_owned[2:5],
    )


def solution(mesh):
    shards = mesh.shape["shard"]
    reps = mesh.shape["rep"]
    finer = Mesh(mesh.devices.reshape(shards, reps // 4, 2, 2), ("shard", "outer", "y", "core"))
    rep = ("outer", "y", "core")
    specs = (
        P(rep, "shard", None),
        P(rep, "shard", None),
        P("shard", None),
        P("shard", None),
        P("shard", None),
        P("shard", None),
        P("shard", None),
        P("shard"),
        P("shard"),
        P(None, "shard"),
    )
    return jax.shard_map(local, mesh=finer, in_specs=specs, out_specs=specs, check_vma=False)
```

time: 2110 us -> 457 us (0.22)
  waiting for transfers between devices: 1890 us -> 158 us
  matrix products: 134 us -> 39.3 us
  Pallas kernels: 0 us -> 76.1 us
  starting transfers between devices: 4.23 us -> 63.3 us
  local copies, waits for them, and re-layouts: 20.2 us -> 61.4 us
  other arithmetic: 11.2 us -> 47.2 us
  blocking collectives: 33.9 us -> 0 us
    reduce_scatter x6 -> x0, waiting for transfers between devices: 1220 us -> none  [the longest x1 317 us: local(): lax.psum_scatter(g_up, 'shard', scatter_dimension=0, tiled=True)]
    all_gather x5 -> x0, waiting for transfers between devices: 498 us -> none  [the longest x1 134 us: local(): lax.all_gather(up_weight, 'shard', axis=0, tiled=True)]
    psum x1 -> x0, waiting for transfers between devices: 162 us -> none  [local(): mix_shares = lax.psum((mix_shares[0], mix_shares[1], mix_shares[2]), 'rep')]
    ppermute x2 -> x68, waiting for transfers between devices: 4.29 us -> 158 us  [the longest x24 65.6 us: hop(): self.one = lax.ppermute(self.one, 'shard', self.pairs[0])]
    dot_general x10 -> x4, matrix products: 88.4 us -> 5.95 us  [times(): return jnp.dot(value, weight, preferred_element_type=jnp.float32)]
    pallas_call x0 -> x8, Pallas kernels: none -> 76.1 us  [the longest x2 42.8 us: feed_forward(): pl.pallas_call(functools.partial(feed_forward_kernel, size), grid=(2,), i...]
    ppermute x2 -> x68, starting transfers between devices: 3.75 us -> 63.3 us  [the longest x24 30.9 us: hop(): self.one = lax.ppermute(self.one, 'shard', self.pairs[0])]
    all_gather x1 -> x0, blocking collectives: 28.2 us -> none  [local(): lax.all_gather(small, 'shard', axis=1, tiled=True)]
  transfers between devices with their start and end apart: 14 -> 68, of which waited for: 14 -> 25; matrix products, arithmetic and copies ran while one was open for 5% -> 28% of each run, Pallas kernels for 0% -> 12%
where the time goes in v3:
time: 457 us; the launch traced here: 448 us
  waiting for transfers between devices  158 us (35%)
  Pallas kernels  76.1 us (17%)
  starting transfers between devices  63.3 us (14%)
  local copies, waits for them, and re-layouts  61.4 us (13%)
  other arithmetic  47.2 us (10%)
  matrix products  39.3 us (9%)
    ppermute x24, waiting for transfers between devices, hop(): self.one = lax.ppermute(self.one, 'shard', self.pairs[0])  65.6 us
    ppermute x18, waiting for transfers between devices, hop(): self.two = lax.ppermute(self.two, 'shard', self.pairs[1])  45.2 us
    ppermute x7, waiting for transfers between devices, over_y(): return lax.ppermute(value, 'y', PAIR)  44.1 us
    pallas_call x2, Pallas kernels, feed_forward(): pl.pallas_call(functools.partial(feed_forward_kernel, size), grid=(2,), i...  42.8 us
    dot_general x4, matrix products, outer_sum(): lax.dot_general(left, right, (((0,), (0,)), ((), ())), preferred_element_...  33.4 us
    ppermute x24, starting transfers between devices, hop(): self.one = lax.ppermute(self.one, 'shard', self.pairs[0])  30.9 us
    dynamic_update_slice x22, local copies, waits for them, and re-layouts, put(): lax.dynamic_update_slice(self.whole, block[None], (place, 0, 0))  25.4 us
    convert_element_type x19, other arithmetic, narrow(): return value.astype(jnp.bfloat16)  23.6 us
  transfers between devices with their start and end apart: 68, of which 25 were waited for; matrix products, arithmetic and copies ran while one was open for 28% of the time, Pallas kernels for 12%

profile of v3, /device:TPU:0, one launch (start us, length us, event | category | flops | bytes accessed | tf_op | source)
XLA Modules:
  0.0 447.5 jit_solution(3531271708382374385)
XLA Ops:
  4.3 3.0 collective-permute-start.23
  7.3 4.4 fusion.10
  19.3 2.2 copy-done.19
  21.6 2.8 broadcast_in_dim.119
  35.1 5.7 %collective-permute-done.1 = bf16[144,2048]{1,0:T(8,128)(2,1)S(1)} collective-permute-done((bf16[144,2048]{1,0:T(8,128)(2,1)}, bf16[144,2048]{1,0:T(8,128)(2,1)S(1)}, u32[]{:S(2)}, u32[]{:S(2)}) %collective-permute-start.1) | collective-permute-done | bytes 589856 | tf_op jit(solution)/shard_map/ppermute | solution.py:95
  42.4 5.7 %collective-permute-done.25 = bf16[144,1024]{1,0:T(8,128)(2,1)S(1)} collective-permute-done((bf16[144,1024]{1,0:T(8,128)(2,1)}, bf16[144,1024]{1,0:T(8,128)(2,1)S(1)}, u32[]{:S(2)}, u32[]{:S(2)}) %collective-permute-start.25) | collective-permute-done | bytes 294944 | tf_op jit(solution)/shard_map/ppermute | solution.py:95
  51.7 3.3 collective-permute-done.26
  64.5 4.5 %collective-permute-done.3 = bf16[144,2048]{1,0:T(8,128)(2,1)S(1)} collective-permute-done((bf16[144,2048]{1,0:T(8,128)(2,1)S(1)}, bf16[144,2048]{1,0:T(8,128)(2,1)S(1)}, u32[]{:S(2)}, u32[]{:S(2)}) %collective-permute-start.3) | collective-permute-done | bytes 589856 | tf_op jit(solution)/shard_map/ppermute | solution.py:95
  70.3 8.2 %collective-permute-done.4 = bf16[144,2048]{1,0:T(8,128)(2,1)S(1)} collective-permute-done((bf16[144,2048]{1,0:T(8,128)(2,1)S(1)}, bf16[144,2048]{1,0:T(8,128)(2,1)S(1)}, u32[]{:S(2)}, u32[]{:S(2)}) %collective-permute-start.4) | collective-permute-done | bytes 589856 | tf_op jit(solution)/shard_map/ppermute | solution.py:98
  79.7 2.8 collective-permute-done.5
  83.7 8.2 %collective-permute-done.6 = bf16[144,2048]{1,0:T(8,128)(2,1)S(1)} collective-permute-done((bf16[144,2048]{1,0:T(8,128)(2,1)S(1)}, bf16[144,2048]{1,0:T(8,128)(2,1)S(1)}, u32[]{:S(2)}, u32[]{:S(2)}) %collective-permute-start.6) | collective-permute-done | bytes 589856 | tf_op jit(solution)/shard_map/ppermute | solution.py:98
  97.7 7.9 %shard_map.177 = (bf16[1024,1024]{1,0:T(8,128)(2,1)S(1)}, f32[1024,512]{1,0:T(8,128)S(1)}, f32[1024,512]{1,0:T(8,128)}, f32[1024,512]{1,0:T(8,128)}, bf16[1024,512]{1,0:T(8,128)(2,1)S(1)}) custom-call(bf16[1024,1024]{1,0:T(8,128)(2,1)} %pad_maximum_fusion.3.tokens_ref, f32[1,1024]{1,0:T(1,128)S(1)} %get-tuple-element.141.gain_ref, ...), custom_call_target="tpu_custom_call" | custom-call | flops 3221225472 | bytes 14680064 | tf_op jit(solution)/shard_map/pallas_call | solution.py:170
  108.3 3.7 collective-permute-start.8
  114.7 5.5 %shard_map.178 = (f32[1024,512]{1,0:T(8,128)S(1)}, bf16[1024,512]{1,0:T(8,128)(2,1)S(1)}, bf16[1024,1024]{1,0:T(8,128)(2,1)}) custom-call(f32[1024,512]{1,0:T(8,128)} %get-tuple-element.35.c_ref, bf16[1024,512]{1,0:T(8,128)(2,1)S(1)} %get-tuple-element.36.p_ref, bf16[2,2,512]{2,1,0:T(2,128)(2,1)S(1)} %collective-permute-done.8.halo_ref, ...), custom_call_target="tpu_custom_call" | custom-call | flops 1073741824 | bytes 8388608 | tf_op jit(solution)/shard_map/pallas_call | solution.py:206
  120.2 2.2 slice.173
  129.7 10.8 %collective-permute-done.20 = bf16[128,2304]{1,0:T(8,128)(2,1)S(1)} collective-permute-done((bf16[128,2304]{1,0:T(8,128)(2,1)}, bf16[128,2304]{1,0:T(8,128)(2,1)S(1)}, u32[]{:S(2)}, u32[]{:S(2)}) %collective-permute-start.20) | collective-permute-done | bytes 589856 | tf_op jit(solution)/shard_map/ppermute | solution.py:95
  146.2 20.7 %collective-permute-done.11 = bf16[512,1024]{1,0:T(8,128)(2,1)S(1)} collective-permute-done((bf16[512,1024]{1,0:T(8,128)(2,1)S(1)}, bf16[512,1024]{1,0:T(8,128)(2,1)S(1)}, u32[]{:S(2)}, u32[]{:S(2)}) %collective-permute-start.11) | collective-permute-done | bytes 1048608 | tf_op jit(solution)/shard_map/ppermute | solution.py:19
  166.9 4.2 pad_maximum_fusion.1.cot_ref
  172.0 2.5 pad_maximum_fusion.rows_ref
  174.6 20.9 %shard_map.179 = (bf16[2048,1152]{1,0:T(8,128)(2,1)}, bf16[2048,2304]{1,0:T(8,128)(2,1)}, bf16[1024,1024]{1,0:T(8,128)(2,1)S(1)}, bf16[1024,1024]{1,0:T(8,128)(2,1)S(1)}) custom-call(bf16[2048,1024]{1,0:T(8,128)(2,1)} %pad_maximum_fusion.rows_ref, bf16[2048,1024]{1,0:T(8,128)(2,1)} %pad_maximum_fusion.1.cot_ref, bf16[1024,2304]{1,0:T(8,128)(2,1)} %bitcast.112, ...), custom_call_target="tpu_custom_call" | custom-call | flops 14495514624 | bytes 16777216 | tf_op jit(solution)/shard_map/pallas_call | solution.py:369
  198.1 2.9 collective-permute-done.30
  204.1 21.9 %shard_map.180 = (bf16[2048,1152]{1,0:T(8,128)(2,1)}, bf16[2048,2304]{1,0:T(8,128)(2,1)}, bf16[1024,1024]{1,0:T(8,128)(2,1)S(1)}, bf16[1024,1024]{1,0:T(8,128)(2,1)S(1)}) custom-call(bf16[2048,1024]{1,0:T(8,128)(2,1)} %pad_maximum_fusion.rows_ref, bf16[2048,1024]{1,0:T(8,128)(2,1)} %pad_maximum_fusion.1.cot_ref, ...), custom_call_target="tpu_custom_call", output_to_operand_aliasing={{0}: (4, {}), {1}: (5, {})} | custom-call | flops 14495514624 | bytes 16777216 | tf_op jit(solution)/shard_map/pallas_call | solution.py:369
  226.0 10.2 %fusion.76 = f32[1152,1024]{1,0:T(8,128)} fusion(bf16[2048,1152]{1,0:T(8,128)(2,1)} %get-tuple-element.59, bf16[512,1024]{1,0:T(8,128)(2,1)S(1)} %copy-done.30, bf16[512,1024]{1,0:T(8,128)(2,1)} %collective-permute-done.14, bf16[512,1024]{1,0:T(8,128)(2,1)} %collective-permute-done.13, bf16[512,1024]{1,0:T(8,128)(2,1)S(1)} %bitcast.117), kind=kOutput, calls=%fused_computation.208 | convolution fusion | flops 4848615424 | bytes 13631488 | tf_op jit(solution)/shard_map/dot_general | solution.py:23
  236.3 2.1 dynamic-slice_convert_fusion.5
  241.4 2.4 slice.221
  243.8 15.2 %fusion.77 = f32[1024,2304]{1,0:T(8,128)} fusion(bf16[2048,2304]{1,0:T(8,128)(2,1)} %get-tuple-element.56, bf16[512,1024]{1,0:T(8,128)(2,1)} %copy-done.34, bf16[512,1024]{1,0:T(8,128)(2,1)S(1)} %copy-done.32, bf16[512,1024]{1,0:T(8,128)(2,1)} %copy-done.33, bf16[512,1024]{1,0:T(8,128)(2,1)S(1)} %copy-done.24), kind=kOutput, calls=%fused_computation.209 | convolution fusion | flops 9680453632 | bytes 23068672 | tf_op jit(solution)/shard_map/dot_general | solution.py:23
  262.1 2.8 dynamic-slice_convert_fusion.1
  267.5 3.1 collective-permute-done.59
  275.9 5.4 %collective-permute-done.48 = bf16[128,2304]{1,0:T(8,128)(2,1)} collective-permute-done((bf16[128,2304]{1,0:T(8,128)(2,1)}, bf16[128,2304]{1,0:T(8,128)(2,1)}, u32[]{:S(2)}, u32[]{:S(2)}) %collective-permute-start.48) | collective-permute-done | bytes 589856 | tf_op jit(solution)/shard_map/ppermute | solution.py:122
  281.9 2.3 add_convert_fusion.8
  293.4 11.9 %collective-permute-done.34 = bf16[512,1024]{1,0:T(8,128)(2,1)S(1)} collective-permute-done((bf16[512,1024]{1,0:T(8,128)(2,1)S(1)}, bf16[512,1024]{1,0:T(8,128)(2,1)S(1)}, u32[]{:S(2)}, u32[]{:S(2)}) %collective-permute-start.34) | collective-permute-done | bytes 1048608 | tf_op jit(solution)/shard_map/ppermute | solution.py:19
  305.2 3.0 fusion.78
  311.1 3.2 add_convert_fusion.7
  316.4 3.6 collective-permute-done.66
  319.9 3.1 pad_maximum_fusion.4.d_ref
  323.0 7.3 %shard_map.182 = (bf16[1024,512]{1,0:T(8,128)(2,1)S(1)}, f32[1024,512]{1,0:T(8,128)S(1)}, f32[2,2,512]{2,1,0:T(2,128)S(1)}, f32[3,512]{1,0:T(4,128)S(1)}) custom-call(bf16[1024,1024]{1,0:T(8,128)(2,1)} %pad_maximum_fusion.4.d_ref, f32[1024,512]{1,0:T(8,128)} %get-tuple-element.35.c_ref, f32[1024,512]{1,0:T(8,128)} %copy-done.2, ...), custom_call_target="tpu_custom_call" | custom-call | flops 1073741824 | bytes 10485760 | tf_op jit(solution)/shard_map/pallas_call | solution.py:256
  331.7 2.5 fusion.75
  340.3 9.5 %shard_map.183 = (bf16[1024,1536]{1,0:T(8,128)(2,1)}, bf16[1024,1024]{1,0:T(8,128)(2,1)S(1)}, f32[1,1024]{1,0:T(1,128)S(1)}) custom-call(f32[1024,512]{1,0:T(8,128)S(1)} %get-tuple-element.45.d_p_ref, f32[2,2,512]{2,1,0:T(2,128)S(1)} %collective-permute-done.37.edge_ref, f32[1024,512]{1,0:T(8,128)} %copy-done.5, f32[1024,512]{1,0:T(8,128)} %get-tuple-element.48.x_ref, ...), custom_call_target="tpu_custom_call" | custom-call | flops 3221225472 | bytes 14680064 | tf_op jit(solution)/shard_map/pallas_call | solution.py:315
  349.7 5.4 %fusion.86 = f32[1024,1536]{1,0:T(8,128)S(1)} fusion(bf16[1024,1024]{1,0:T(8,128)(2,1)S(1)} %copy-done.11, bf16[1024,1536]{1,0:T(8,128)(2,1)} %get-tuple-element.52), kind=kOutput, calls=%fused_computation.217 | convolution fusion | flops 3221225472 | bytes 11534336 | tf_op jit(solution)/shard_map/dot_general | solution.py:23
  355.4 2.9 collective-permute-start.39
  358.9 12.9 %collective-permute-done.39 = bf16[144,2048]{1,0:T(8,128)(2,1)S(1)} collective-permute-done((bf16[144,2048]{1,0:T(8,128)(2,1)S(1)}, bf16[144,2048]{1,0:T(8,128)(2,1)S(1)}, u32[]{:S(2)}, u32[]{:S(2)}) %collective-permute-start.39) | collective-permute-done | bytes 589856 | tf_op jit(solution)/shard_map/ppermute | solution.py:122
  374.1 2.2 add_convert_fusion.6
  378.0 10.0 %collective-permute-done.43 = bf16[144,2048]{1,0:T(8,128)(2,1)S(1)} collective-permute-done((bf16[144,2048]{1,0:T(8,128)(2,1)S(1)}, bf16[144,2048]{1,0:T(8,128)(2,1)S(1)}, u32[]{:S(2)}, u32[]{:S(2)}) %collective-permute-start.43) | collective-permute-done | bytes 589856 | tf_op jit(solution)/shard_map/ppermute | solution.py:126
  390.4 10.3 %collective-permute-done.51 = bf16[128,2304]{1,0:T(8,128)(2,1)S(1)} collective-permute-done((bf16[128,2304]{1,0:T(8,128)(2,1)S(1)}, bf16[128,2304]{1,0:T(8,128)(2,1)S(1)}, u32[]{:S(2)}, u32[]{:S(2)}) %collective-permute-start.51) | collective-permute-done | bytes 589856 | tf_op jit(solution)/shard_map/ppermute | solution.py:122
  404.7 7.3 %collective-permute-done.44 = bf16[144,2048]{1,0:T(8,128)(2,1)S(1)} collective-permute-done((bf16[144,2048]{1,0:T(8,128)(2,1)S(1)}, bf16[144,2048]{1,0:T(8,128)(2,1)S(1)}, u32[]{:S(2)}, u32[]{:S(2)}) %collective-permute-start.44) | collective-permute-done | bytes 589856 | tf_op jit(solution)/shard_map/ppermute | solution.py:126
  419.1 7.2 %collective-permute-done.45 = bf16[144,2048]{1,0:T(8,128)(2,1)S(1)} collective-permute-done((bf16[144,2048]{1,0:T(8,128)(2,1)S(1)}, bf16[144,2048]{1,0:T(8,128)(2,1)S(1)}, u32[]{:S(2)}, u32[]{:S(2)}) %collective-permute-start.45) | collective-permute-done | bytes 589856 | tf_op jit(solution)/shard_map/ppermute | solution.py:126
  428.7 3.1 shard_map.184
  432.5 7.9 %collective-permute-done.46 = bf16[144,2048]{1,0:T(8,128)(2,1)S(1)} collective-permute-done((bf16[144,2048]{1,0:T(8,128)(2,1)S(1)}, bf16[144,2048]{1,0:T(8,128)(2,1)S(1)}, u32[]{:S(2)}, u32[]{:S(2)}) %collective-permute-start.46) | collective-permute-done | bytes 589856 | tf_op jit(solution)/shard_map/ppermute | solution.py:19
  (321 shorter events, 134.3 us)
Async XLA Ops:
  4.3 21.1 %collective-permute-start.23 = (bf16[144,1024]{1,0:T(8,128)(2,1)}, bf16[144,1024]{1,0:T(8,128)(2,1)}, u32[]{:S(2)}, u32[]{:S(2)}) collective-permute-start(bf16[144,1024]{1,0:T(8,128)(2,1)} %get-tuple-element.75), channel_id=1, source_target_pairs={{0,8},{8,16},{16,24},{24,28},{28,20},{20,12},{12,4},{4,0},{1,9},{9... | collective-permute-start | bytes 884744 | tf_op jit(solution)/shard_map/ppermute | solution.py:95
  7.3 19.8 %collective-permute-start.24 = (bf16[144,1024]{1,0:T(8,128)(2,1)}, bf16[144,1024]{1,0:T(8,128)(2,1)}, u32[]{:S(2)}, u32[]{:S(2)}) collective-permute-start(bf16[144,1024]{1,0:T(8,128)(2,1)} %get-tuple-element.75), channel_id=1, source_target_pairs={{8,0},{16,8},{24,16},{28,24},{20,28},{12,20},{4,12},{0,4},{9,1},{1... | collective-permute-start | bytes 884744 | tf_op jit(solution)/shard_map/ppermute | solution.py:98
  11.9 18.8 %collective-permute-start.16 = (bf16[128,2304]{1,0:T(8,128)(2,1)S(1)}, bf16[128,2304]{1,0:T(8,128)(2,1)}, u32[]{:S(2)}, u32[]{:S(2)}) collective-permute-start(bf16[128,2304]{1,0:T(8,128)(2,1)S(1)} %pad_maximum_fusion.7), channel_id=1, source_target_pairs={{8,0},{16,8},{24,16},{28,24},{20,28},{12,20},{4,12},{0,4},{9,1},{1... | collective-permute-start | bytes 1769480 | tf_op jit(solution)/shard_map/ppermute | solution.py:95
  13.9 18.8 %collective-permute-start.17 = (bf16[128,2304]{1,0:T(8,128)(2,1)S(1)}, bf16[128,2304]{1,0:T(8,128)(2,1)}, u32[]{:S(2)}, u32[]{:S(2)}) collective-permute-start(bf16[128,2304]{1,0:T(8,128)(2,1)S(1)} %pad_maximum_fusion.7), channel_id=1, source_target_pairs={{0,8},{8,16},{16,24},{24,28},{28,20},{20,12},{12,4},{4,0},{1,9},{9... | collective-permute-start | bytes 1769480 | tf_op jit(solution)/shard_map/ppermute | solution.py:98
  17.0 23.8 %collective-permute-start.1 = (bf16[144,2048]{1,0:T(8,128)(2,1)}, bf16[144,2048]{1,0:T(8,128)(2,1)S(1)}, u32[]{:S(2)}, u32[]{:S(2)}) collective-permute-start(bf16[144,2048]{1,0:T(8,128)(2,1)} %pad_maximum_fusion.6), channel_id=1, source_target_pairs={{0,8},{8,16},{16,24},{24,28},{28,20},{20,12},{12,4},{4,0},{1,9},{9... | collective-permute-start | bytes 1769480 | tf_op jit(solution)/shard_map/ppermute | solution.py:95
  25.3 24.3 %collective-permute-start.2 = (bf16[144,2048]{1,0:T(8,128)(2,1)}, bf16[144,2048]{1,0:T(8,128)(2,1)S(1)}, u32[]{:S(2)}, u32[]{:S(2)}) collective-permute-start(bf16[144,2048]{1,0:T(8,128)(2,1)} %pad_maximum_fusion.6), channel_id=1, source_target_pairs={{8,0},{16,8},{24,16},{28,24},{20,28},{12,20},{4,12},{0,4},{9,1},{1... | collective-permute-start | bytes 1769480 | tf_op jit(solution)/shard_map/ppermute | solution.py:98
  27.1 85.9 %collective-permute-start.14 = (bf16[512,1024]{1,0:T(8,128)(2,1)S(1)}, bf16[512,1024]{1,0:T(8,128)(2,1)}, u32[]{:S(2)}, u32[]{:S(2)}) collective-permute-start(bf16[512,1024]{1,0:T(8,128)(2,1)S(1)} %bitcast.114), channel_id=1, source_target_pairs={{0,2},{2,0},{1,3},{3,1},{4,6},{6,4},{5,7},{7,5},{8,10},{10,8},{9,1... | collective-permute-start | bytes 3145736 | tf_op jit(solution)/shard_map/ppermute | solution.py:19
  30.7 136.2 %collective-permute-start.13 = (bf16[512,1024]{1,0:T(8,128)(2,1)S(1)}, bf16[512,1024]{1,0:T(8,128)(2,1)}, u32[]{:S(2)}, u32[]{:S(2)}) collective-permute-start(bf16[512,1024]{1,0:T(8,128)(2,1)S(1)} %bitcast.115), channel_id=1, source_target_pairs={{0,1},{1,0},{2,3},{3,2},{4,5},{5,4},{6,7},{7,6},{8,9},{9,8},{10,11... | collective-permute-start | bytes 3145736 | tf_op jit(solution)/shard_map/ppermute | solution.py:15
  32.7 28.7 %collective-permute-start = (bf16[512,1024]{1,0:T(8,128)(2,1)S(1)}, bf16[512,1024]{1,0:T(8,128)(2,1)S(1)}, u32[]{:S(2)}, u32[]{:S(2)}) collective-permute-start(bf16[512,1024]{1,0:T(8,128)(2,1)S(1)} %bitcast.109), channel_id=1, source_target_pairs={{0,1},{1,0},{2,3},{3,2},{4,5},{5,4},{6,7},{7,6},{8,9},{9,8},{10,11... | collective-permute-start | bytes 3145736 | tf_op jit(solution)/shard_map/ppermute | solution.py:15
  55.0 14.0 %collective-permute-start.3 = (bf16[144,2048]{1,0:T(8,128)(2,1)S(1)}, bf16[144,2048]{1,0:T(8,128)(2,1)S(1)}, u32[]{:S(2)}, u32[]{:S(2)}) collective-permute-start(bf16[144,2048]{1,0:T(8,128)(2,1)S(1)} %collective-permute-done.1), channel_id=1, source_target_pairs={{0,8},{8,16},{16,24},{24,28},{28,20},{20,12},{12,4},{4,0},{1,9},{9... | collective-permute-start | bytes 1769480 | tf_op jit(solution)/shard_map/ppermute | solution.py:95
  58.7 49.6 %collective-permute-start.28 = (bf16[144,1024]{1,0:T(8,128)(2,1)S(1)}, bf16[144,1024]{1,0:T(8,128)(2,1)S(1)}, u32[]{:S(2)}, u32[]{:S(2)}) collective-permute-start(bf16[144,1024]{1,0:T(8,128)(2,1)S(1)} %collective-permute-done.26), channel_id=1, source_target_pairs={{8,0},{16,8},{24,16},{28,24},{20,28},{12,20},{4,12},{0,4},{9,1},{1... | collective-permute-start | bytes 884744 | tf_op jit(solution)/shard_map/ppermute | solution.py:98
  61.3 17.2 %collective-permute-start.4 = (bf16[144,2048]{1,0:T(8,128)(2,1)S(1)}, bf16[144,2048]{1,0:T(8,128)(2,1)S(1)}, u32[]{:S(2)}, u32[]{:S(2)}) collective-permute-start(bf16[144,2048]{1,0:T(8,128)(2,1)S(1)} %collective-permute-done.2), channel_id=1, source_target_pairs={{8,0},{16,8},{24,16},{28,24},{20,28},{12,20},{4,12},{0,4},{9,1},{1... | collective-permute-start | bytes 1769480 | tf_op jit(solution)/shard_map/ppermute | solution.py:98
  69.0 13.5 %collective-permute-start.5 = (bf16[144,2048]{1,0:T(8,128)(2,1)S(1)}, bf16[144,2048]{1,0:T(8,128)(2,1)S(1)}, u32[]{:S(2)}, u32[]{:S(2)}) collective-permute-start(bf16[144,2048]{1,0:T(8,128)(2,1)S(1)} %collective-permute-done.3), channel_id=1, source_target_pairs={{0,8},{8,16},{16,24},{24,28},{28,20},{20,12},{12,4},{4,0},{1,9},{9... | collective-permute-start | bytes 1769480 | tf_op jit(solution)/shard_map/ppermute | solution.py:95
  91.9 30.5 %collective-permute-start.18 = (bf16[128,2304]{1,0:T(8,128)(2,1)}, bf16[128,2304]{1,0:T(8,128)(2,1)}, u32[]{:S(2)}, u32[]{:S(2)}) collective-permute-start(bf16[128,2304]{1,0:T(8,128)(2,1)} %collective-permute-done.16), channel_id=1, source_target_pairs={{8,0},{16,8},{24,16},{28,24},{20,28},{12,20},{4,12},{0,4},{9,1},{1... | collective-permute-start | bytes 1769480 | tf_op jit(solution)/shard_map/ppermute | solution.py:95
  95.8 30.1 %collective-permute-start.19 = (bf16[128,2304]{1,0:T(8,128)(2,1)}, bf16[128,2304]{1,0:T(8,128)(2,1)}, u32[]{:S(2)}, u32[]{:S(2)}) collective-permute-start(bf16[128,2304]{1,0:T(8,128)(2,1)} %collective-permute-done.17), channel_id=1, source_target_pairs={{0,8},{8,16},{16,24},{24,28},{28,20},{20,12},{12,4},{4,0},{1,9},{9... | collective-permute-start | bytes 1769480 | tf_op jit(solution)/shard_map/ppermute | solution.py:98
  114.7 52.2 %collective-permute-start.15 = (bf16[512,1024]{1,0:T(8,128)(2,1)}, bf16[512,1024]{1,0:T(8,128)(2,1)S(1)}, u32[]{:S(2)}, u32[]{:S(2)}) collective-permute-start(bf16[512,1024]{1,0:T(8,128)(2,1)} %collective-permute-done.14), channel_id=1, source_target_pairs={{0,1},{1,0},{2,3},{3,2},{4,5},{5,4},{6,7},{7,6},{8,9},{9,8},{10,11... | collective-permute-start | bytes 3145736 | tf_op jit(solution)/shard_map/ppermute | solution.py:15
  122.5 18.9 %collective-permute-start.9 = (bf16[512,1024]{1,0:T(8,128)(2,1)S(1)}, bf16[512,1024]{1,0:T(8,128)(2,1)S(1)}, u32[]{:S(2)}, u32[]{:S(2)}) collective-permute-start(bf16[512,1024]{1,0:T(8,128)(2,1)S(1)} %slice.173), channel_id=1, source_target_pairs={{0,1},{1,0},{2,3},{3,2},{4,5},{5,4},{6,7},{7,6},{8,9},{9,8},{10,11... | collective-permute-start | bytes 3145736 | tf_op jit(solution)/shard_map/ppermute | solution.py:15
  124.9 15.5 %collective-permute-start.20 = (bf16[128,2304]{1,0:T(8,128)(2,1)}, bf16[128,2304]{1,0:T(8,128)(2,1)S(1)}, u32[]{:S(2)}, u32[]{:S(2)}) collective-permute-start(bf16[128,2304]{1,0:T(8,128)(2,1)} %collective-permute-done.18), channel_id=1, source_target_pairs={{8,0},{16,8},{24,16},{28,24},{20,28},{12,20},{4,12},{0,4},{9,1},{1... | collective-permute-start | bytes 1769480 | tf_op jit(solution)/shard_map/ppermute | solution.py:95
  125.9 19.5 %collective-permute-start.21 = (bf16[128,2304]{1,0:T(8,128)(2,1)}, bf16[128,2304]{1,0:T(8,128)(2,1)S(1)}, u32[]{:S(2)}, u32[]{:S(2)}) collective-permute-start(bf16[128,2304]{1,0:T(8,128)(2,1)} %collective-permute-done.19), channel_id=1, source_target_pairs={{0,8},{8,16},{16,24},{24,28},{28,20},{20,12},{12,4},{4,0},{1,9},{9... | collective-permute-start | bytes 1769480 | tf_op jit(solution)/shard_map/ppermute | solution.py:98
  140.4 30.7 %collective-permute-start.22 = (bf16[128,2304]{1,0:T(8,128)(2,1)S(1)}, bf16[128,2304]{1,0:T(8,128)(2,1)S(1)}, u32[]{:S(2)}, u32[]{:S(2)}) collective-permute-start(bf16[128,2304]{1,0:T(8,128)(2,1)S(1)} %collective-permute-done.20), channel_id=1, source_target_pairs={{8,0},{16,8},{24,16},{28,24},{20,28},{12,20},{4,12},{0,4},{9,1},{1... | collective-permute-start | bytes 1769480 | tf_op jit(solution)/shard_map/ppermute | solution.py:95
  142.9 24.0 %collective-permute-start.11 = (bf16[512,1024]{1,0:T(8,128)(2,1)S(1)}, bf16[512,1024]{1,0:T(8,128)(2,1)S(1)}, u32[]{:S(2)}, u32[]{:S(2)}) collective-permute-start(bf16[512,1024]{1,0:T(8,128)(2,1)S(1)} %multiply_convert_fusion), channel_id=1, source_target_pairs={{0,2},{2,0},{1,3},{3,1},{4,6},{6,4},{5,7},{7,5},{8,10},{10,8},{9,1... | collective-permute-start | bytes 3145736 | tf_op jit(solution)/shard_map/ppermute | solution.py:19
  146.2 25.8 %collective-permute-start.10 = (bf16[512,1024]{1,0:T(8,128)(2,1)S(1)}, bf16[512,1024]{1,0:T(8,128)(2,1)S(1)}, u32[]{:S(2)}, u32[]{:S(2)}) collective-permute-start(bf16[512,1024]{1,0:T(8,128)(2,1)S(1)} %multiply_convert_fusion), channel_id=1, source_target_pairs={{0,1},{1,0},{2,3},{3,2},{4,5},{5,4},{6,7},{7,6},{8,9},{9,8},{10,11... | collective-permute-start | bytes 3145736 | tf_op jit(solution)/shard_map/ppermute | solution.py:15
  202.6 37.9 %collective-permute-start.32 = (bf16[512,1024]{1,0:T(8,128)(2,1)S(1)}, bf16[512,1024]{1,0:T(8,128)(2,1)S(1)}, u32[]{:S(2)}, u32[]{:S(2)}) collective-permute-start(bf16[512,1024]{1,0:T(8,128)(2,1)S(1)} %add_convert_fusion.2.refs_2_), channel_id=1, source_target_pairs={{0,2},{2,0},{1,3},{3,1},{4,6},{6,4},{5,7},{7,5},{8,10},{10,8},{9,1... | collective-permute-start | bytes 3145736 | tf_op jit(solution)/shard_map/ppermute | solution.py:19
  238.4 20.6 %collective-permute-start.58 = (bf16[144,1024]{1,0:T(8,128)(2,1)}, bf16[144,1024]{1,0:T(8,128)(2,1)}, u32[]{:S(2)}, u32[]{:S(2)}) collective-permute-start(bf16[144,1024]{1,0:T(8,128)(2,1)} %get-tuple-element.96), channel_id=1, source_target_pairs={{0,8},{8,16},{16,24},{24,28},{28,20},{20,12},{12,4},{4,0},{1,9},{9... | collective-permute-start | bytes 884744 | tf_op jit(solution)/shard_map/ppermute | solution.py:122
  239.5 27.9 %collective-permute-start.62 = (bf16[144,1024]{1,0:T(8,128)(2,1)}, bf16[144,1024]{1,0:T(8,128)(2,1)S(1)}, u32[]{:S(2)}, u32[]{:S(2)}) collective-permute-start(bf16[144,1024]{1,0:T(8,128)(2,1)} %get-tuple-element.97), channel_id=1, source_target_pairs={{8,0},{16,8},{24,16},{28,24},{20,28},{12,20},{4,12},{0,4},{9,1},{1... | collective-permute-start | bytes 884744 | tf_op jit(solution)/shard_map/ppermute | solution.py:126
  243.8 29.6 %collective-permute-start.33 = (bf16[512,1024]{1,0:T(8,128)(2,1)}, bf16[512,1024]{1,0:T(8,128)(2,1)}, u32[]{:S(2)}, u32[]{:S(2)}) collective-permute-start(bf16[512,1024]{1,0:T(8,128)(2,1)} %slice.221), channel_id=1, source_target_pairs={{0,1},{1,0},{2,3},{3,2},{4,5},{5,4},{6,7},{7,6},{8,9},{9,8},{10,11... | collective-permute-start | bytes 3145736 | tf_op jit(solution)/shard_map/ppermute | solution.py:15
  264.9 16.5 %collective-permute-start.48 = (bf16[128,2304]{1,0:T(8,128)(2,1)}, bf16[128,2304]{1,0:T(8,128)(2,1)}, u32[]{:S(2)}, u32[]{:S(2)}) collective-permute-start(bf16[128,2304]{1,0:T(8,128)(2,1)} %get-tuple-element.82), channel_id=1, source_target_pairs={{8,0},{16,8},{24,16},{28,24},{20,28},{12,20},{4,12},{0,4},{9,1},{1... | collective-permute-start | bytes 1769480 | tf_op jit(solution)/shard_map/ppermute | solution.py:122
  265.8 24.0 %collective-permute-start.35 = (bf16[512,1024]{1,0:T(8,128)(2,1)S(1)}, bf16[512,1024]{1,0:T(8,128)(2,1)S(1)}, u32[]{:S(2)}, u32[]{:S(2)}) collective-permute-start(bf16[512,1024]{1,0:T(8,128)(2,1)S(1)} %slice.184), channel_id=1, source_target_pairs={{0,1},{1,0},{2,3},{3,2},{4,5},{5,4},{6,7},{7,6},{8,9},{9,8},{10,11... | collective-permute-start | bytes 3145736 | tf_op jit(solution)/shard_map/ppermute | solution.py:15
  267.4 25.1 %collective-permute-start.31 = (bf16[512,1024]{1,0:T(8,128)(2,1)S(1)}, bf16[512,1024]{1,0:T(8,128)(2,1)S(1)}, u32[]{:S(2)}, u32[]{:S(2)}) collective-permute-start(bf16[512,1024]{1,0:T(8,128)(2,1)S(1)} %slice.180), channel_id=1, source_target_pairs={{0,1},{1,0},{2,3},{3,2},{4,5},{5,4},{6,7},{7,6},{8,9},{9,8},{10,11... | collective-permute-start | bytes 3145736 | tf_op jit(solution)/shard_map/ppermute | solution.py:15
  273.4 13.6 %collective-permute-start.63 = (bf16[144,1024]{1,0:T(8,128)(2,1)S(1)}, bf16[144,1024]{1,0:T(8,128)(2,1)S(1)}, u32[]{:S(2)}, u32[]{:S(2)}) collective-permute-start(bf16[144,1024]{1,0:T(8,128)(2,1)S(1)} %get-tuple-element.95), channel_id=1, source_target_pairs={{8,0},{16,8},{24,16},{28,24},{20,28},{12,20},{4,12},{0,4},{9,1},{1... | collective-permute-start | bytes 884744 | tf_op jit(solution)/shard_map/ppermute | solution.py:126
  281.4 23.9 %collective-permute-start.34 = (bf16[512,1024]{1,0:T(8,128)(2,1)S(1)}, bf16[512,1024]{1,0:T(8,128)(2,1)S(1)}, u32[]{:S(2)}, u32[]{:S(2)}) collective-permute-start(bf16[512,1024]{1,0:T(8,128)(2,1)S(1)} %add_convert_fusion.1), channel_id=1, source_target_pairs={{0,2},{2,0},{1,3},{3,1},{4,6},{6,4},{5,7},{7,5},{8,10},{10,8},{9,1... | collective-permute-start | bytes 3145736 | tf_op jit(solution)/shard_map/ppermute | solution.py:19
  284.3 26.8 %collective-permute-start.52 = (bf16[128,2304]{1,0:T(8,128)(2,1)}, bf16[128,2304]{1,0:T(8,128)(2,1)}, u32[]{:S(2)}, u32[]{:S(2)}) collective-permute-start(bf16[128,2304]{1,0:T(8,128)(2,1)} %get-tuple-element.83), channel_id=1, source_target_pairs={{0,8},{8,16},{16,24},{24,28},{28,20},{20,12},{12,4},{4,0},{1,9},{9... | collective-permute-start | bytes 1769480 | tf_op jit(solution)/shard_map/ppermute | solution.py:126
  286.9 24.2 %collective-permute-start.49 = (bf16[128,2304]{1,0:T(8,128)(2,1)}, bf16[128,2304]{1,0:T(8,128)(2,1)}, u32[]{:S(2)}, u32[]{:S(2)}) collective-permute-start(bf16[128,2304]{1,0:T(8,128)(2,1)} %add_convert_fusion.8), channel_id=1, source_target_pairs={{8,0},{16,8},{24,16},{28,24},{20,28},{12,20},{4,12},{0,4},{9,1},{1... | collective-permute-start | bytes 1769480 | tf_op jit(solution)/shard_map/ppermute | solution.py:122
  289.9 19.1 %collective-permute-start.61 = (bf16[144,1024]{1,0:T(8,128)(2,1)}, bf16[144,1024]{1,0:T(8,128)(2,1)}, u32[]{:S(2)}, u32[]{:S(2)}) collective-permute-start(bf16[144,1024]{1,0:T(8,128)(2,1)} %get-tuple-element.92), channel_id=1, source_target_pairs={{0,8},{8,16},{16,24},{24,28},{28,20},{20,12},{12,4},{4,0},{1,9},{9... | collective-permute-start | bytes 884744 | tf_op jit(solution)/shard_map/ppermute | solution.py:122
  292.5 16.5 %collective-permute-start.64 = (bf16[144,1024]{1,0:T(8,128)(2,1)S(1)}, bf16[144,1024]{1,0:T(8,128)(2,1)}, u32[]{:S(2)}, u32[]{:S(2)}) collective-permute-start(bf16[144,1024]{1,0:T(8,128)(2,1)S(1)} %get-tuple-element.93), channel_id=1, source_target_pairs={{8,0},{16,8},{24,16},{28,24},{20,28},{12,20},{4,12},{0,4},{9,1},{1... | collective-permute-start | bytes 884744 | tf_op jit(solution)/shard_map/ppermute | solution.py:126
  310.9 104.3 %collective-permute-start.65 = (bf16[144,1024]{1,0:T(8,128)(2,1)S(1)}, bf16[144,1024]{1,0:T(8,128)(2,1)}, u32[]{:S(2)}, u32[]{:S(2)}) collective-permute-start(bf16[144,1024]{1,0:T(8,128)(2,1)S(1)} %add_convert_fusion.10), channel_id=1, source_target_pairs={{0,1},{1,0},{2,3},{3,2},{4,5},{5,4},{6,7},{7,6},{8,9},{9,8},{10,11... | collective-permute-start | bytes 884744 | tf_op jit(solution)/shard_map/ppermute | solution.py:15
  314.3 59.4 %collective-permute-start.50 = (bf16[128,2304]{1,0:T(8,128)(2,1)}, bf16[128,2304]{1,0:T(8,128)(2,1)}, u32[]{:S(2)}, u32[]{:S(2)}) collective-permute-start(bf16[128,2304]{1,0:T(8,128)(2,1)} %get-tuple-element.80), channel_id=1, source_target_pairs={{8,0},{16,8},{24,16},{28,24},{20,28},{12,20},{4,12},{0,4},{9,1},{1... | collective-permute-start | bytes 1769480 | tf_op jit(solution)/shard_map/ppermute | solution.py:122
  315.1 58.9 %collective-permute-start.53 = (bf16[128,2304]{1,0:T(8,128)(2,1)}, bf16[128,2304]{1,0:T(8,128)(2,1)}, u32[]{:S(2)}, u32[]{:S(2)}) collective-permute-start(bf16[128,2304]{1,0:T(8,128)(2,1)} %get-tuple-element.81), channel_id=1, source_target_pairs={{0,8},{8,16},{16,24},{24,28},{28,20},{20,12},{12,4},{4,0},{1,9},{9... | collective-permute-start | bytes 1769480 | tf_op jit(solution)/shard_map/ppermute | solution.py:126
  319.9 95.3 %collective-permute-start.67 = (bf16[144,1024]{1,0:T(8,128)(2,1)}, bf16[144,1024]{1,0:T(8,128)(2,1)}, u32[]{:S(2)}, u32[]{:S(2)}) collective-permute-start(bf16[144,1024]{1,0:T(8,128)(2,1)} %collective-permute-done.66), channel_id=1, source_target_pairs={{0,1},{1,0},{2,3},{3,2},{4,5},{5,4},{6,7},{7,6},{8,9},{9,8},{10,11... | collective-permute-start | bytes 884744 | tf_op jit(solution)/shard_map/ppermute | solution.py:15
  355.4 16.4 %collective-permute-start.39 = (bf16[144,2048]{1,0:T(8,128)(2,1)S(1)}, bf16[144,2048]{1,0:T(8,128)(2,1)S(1)}, u32[]{:S(2)}, u32[]{:S(2)}) collective-permute-start(bf16[144,2048]{1,0:T(8,128)(2,1)S(1)} %fusion.43), channel_id=1, source_target_pairs={{0,8},{8,16},{16,24},{24,28},{28,20},{20,12},{12,4},{4,0},{1,9},{9... | collective-permute-start | bytes 1769480 | tf_op jit(solution)/shard_map/ppermute | solution.py:122
  371.8 16.2 %collective-permute-start.43 = (bf16[144,2048]{1,0:T(8,128)(2,1)S(1)}, bf16[144,2048]{1,0:T(8,128)(2,1)S(1)}, u32[]{:S(2)}, u32[]{:S(2)}) collective-permute-start(bf16[144,2048]{1,0:T(8,128)(2,1)S(1)} %fusion.44), channel_id=1, source_target_pairs={{8,0},{16,8},{24,16},{28,24},{20,28},{12,20},{4,12},{0,4},{9,1},{1... | collective-permute-start | bytes 1769480 | tf_op jit(solution)/shard_map/ppermute | solution.py:126
  373.7 16.5 %collective-permute-start.40 = (bf16[144,2048]{1,0:T(8,128)(2,1)S(1)}, bf16[144,2048]{1,0:T(8,128)(2,1)S(1)}, u32[]{:S(2)}, u32[]{:S(2)}) collective-permute-start(bf16[144,2048]{1,0:T(8,128)(2,1)S(1)} %fusion.32), channel_id=1, source_target_pairs={{0,8},{8,16},{16,24},{24,28},{28,20},{20,12},{12,4},{4,0},{1,9},{9... | collective-permute-start | bytes 1769480 | tf_op jit(solution)/shard_map/ppermute | solution.py:122
  376.2 24.5 %collective-permute-start.51 = (bf16[128,2304]{1,0:T(8,128)(2,1)S(1)}, bf16[128,2304]{1,0:T(8,128)(2,1)S(1)}, u32[]{:S(2)}, u32[]{:S(2)}) collective-permute-start(bf16[128,2304]{1,0:T(8,128)(2,1)S(1)} %get-tuple-element.78), channel_id=1, source_target_pairs={{8,0},{16,8},{24,16},{28,24},{20,28},{12,20},{4,12},{0,4},{9,1},{1... | collective-permute-start | bytes 1769480 | tf_op jit(solution)/shard_map/ppermute | solution.py:122
  388.1 14.6 %collective-permute-start.54 = (bf16[128,2304]{1,0:T(8,128)(2,1)S(1)}, bf16[128,2304]{1,0:T(8,128)(2,1)S(1)}, u32[]{:S(2)}, u32[]{:S(2)}) collective-permute-start(bf16[128,2304]{1,0:T(8,128)(2,1)S(1)} %get-tuple-element.79), channel_id=1, source_target_pairs={{0,8},{8,16},{16,24},{24,28},{28,20},{20,12},{12,4},{4,0},{1,9},{9... | collective-permute-start | bytes 1769480 | tf_op jit(solution)/shard_map/ppermute | solution.py:126
  390.2 21.9 %collective-permute-start.44 = (bf16[144,2048]{1,0:T(8,128)(2,1)S(1)}, bf16[144,2048]{1,0:T(8,128)(2,1)S(1)}, u32[]{:S(2)}, u32[]{:S(2)}) collective-permute-start(bf16[144,2048]{1,0:T(8,128)(2,1)S(1)} %fusion.26), channel_id=1, source_target_pairs={{8,0},{16,8},{24,16},{28,24},{20,28},{12,20},{4,12},{0,4},{9,1},{1... | collective-permute-start | bytes 1769480 | tf_op jit(solution)/shard_map/ppermute | solution.py:126
  412.2 14.1 %collective-permute-start.45 = (bf16[144,2048]{1,0:T(8,128)(2,1)S(1)}, bf16[144,2048]{1,0:T(8,128)(2,1)S(1)}, u32[]{:S(2)}, u32[]{:S(2)}) collective-permute-start(bf16[144,2048]{1,0:T(8,128)(2,1)S(1)} %fusion.24), channel_id=1, source_target_pairs={{8,0},{16,8},{24,16},{28,24},{20,28},{12,20},{4,12},{0,4},{9,1},{1... | collective-permute-start | bytes 1769480 | tf_op jit(solution)/shard_map/ppermute | solution.py:126
  413.8 13.7 %collective-permute-start.42 = (bf16[144,2048]{1,0:T(8,128)(2,1)S(1)}, bf16[144,2048]{1,0:T(8,128)(2,1)S(1)}, u32[]{:S(2)}, u32[]{:S(2)}) collective-permute-start(bf16[144,2048]{1,0:T(8,128)(2,1)S(1)} %fusion.28), channel_id=1, source_target_pairs={{0,8},{8,16},{16,24},{24,28},{28,20},{20,12},{12,4},{4,0},{1,9},{9... | collective-permute-start | bytes 1769480 | tf_op jit(solution)/shard_map/ppermute | solution.py:122
  417.3 14.5 %collective-permute-start.38 = (bf16[512,1024]{1,0:T(8,128)(2,1)S(1)}, bf16[512,1024]{1,0:T(8,128)(2,1)S(1)}, u32[]{:S(2)}, u32[]{:S(2)}) collective-permute-start(bf16[512,1024]{1,0:T(8,128)(2,1)S(1)} %slice.186), channel_id=1, source_target_pairs={{0,1},{1,0},{2,3},{3,2},{4,5},{5,4},{6,7},{7,6},{8,9},{9,8},{10,11... | collective-permute-start | bytes 3145736 | tf_op jit(solution)/shard_map/ppermute | solution.py:15
  (68 other events, 509.5 us)
